TPU v7x, 256 devices: a whole 4x4x8 slice. The times are simulated.
256 devices in a mesh: prefix: 16 (over y, z_lo), resp: 16 (over z_hi, x, core).
Axes of the slice: x: 4, y: 4, z: 8 (z_hi: 2, z_lo: 4; z = z_hi * 4 + z_lo), core: 2. Of those that a mesh axis runs over, the one named last changes fastest.
Arguments:
- response_queries: bfloat16 [16, 2048, 2560], P('resp', 'prefix'), may hold values from -120 to 120
- response_keys: bfloat16 [16, 2048, 512], P('resp', 'prefix'), may hold values from -6 to 6
- response_values: bfloat16 [16, 2048, 512], P('resp', 'prefix'), may hold values from -6 to 6
- prompt_keys: bfloat16 [768, 512], P('prefix'), may hold values from -6.1 to 6.1
- prompt_values: bfloat16 [768, 512], P('prefix'), may hold values from -6 to 6
- output_grad: bfloat16 [16, 2048, 2560], P('resp', 'prefix'), may hold values from -6 to 6
- lengths: int32 [16], replicated, may hold values from 1 to 2048, 17408 in all
Outputs:
- attention_out: bfloat16 [16, 2048, 2560], P('resp', 'prefix')
- query_grad: bfloat16 [16, 2048, 2560], P('resp', 'prefix')
- response_key_grad: float32 [16, 2048, 512], P('resp', 'prefix')
- response_value_grad: float32 [16, 2048, 512], P('resp', 'prefix')
- prompt_key_grad: float32 [768, 512], P('prefix')
- prompt_value_grad: float32 [768, 512], P('prefix')
Inputs may be any that keep to these rules, and one draw needn't show every extreme that they name: `lengths`: the longest response has exactly 2048 positions.
All inputs are finite; a program needn't handle non-finite values.
Results may differ from a plain program's by a relative error of at most 0.035.
Values may be sent and summed in bfloat16 or wider, within the bound.
No kernel may reach another device: no remote copies, remote signals or barrier semaphores. Data moves between devices by JAX's collectives and lax.ppermute only.
A program may use at most 128 MiB of HBM per device.

v0:
```python
import math

import jax
import jax.numpy as jnp
from jax import lax
from jax.experimental import pallas as pl
from jax.experimental.pallas import tpu as pltpu
from jax.sharding import PartitionSpec as P

HD = 128
BLOCK = 128
PROMPT_ROWS = 48
PIECE = PROMPT_ROWS + BLOCK
HEADS = 5
NY = 4
NZ = 4
PROMPT = PROMPT_ROWS * NY * NZ
KEYS = PROMPT + BLOCK * NY * NZ
ROWS = NY * HEADS * BLOCK
CHUNK = 256
TILE = 256
MASKED = -1e30
SCALE = 1.0 / math.sqrt(HD)
SCALE2 = SCALE * math.log2(math.e)
F32 = jnp.float32
BF16 = jnp.bfloat16
CLASSES = ((0, 2, 2, 0), (2, 5, 4, 0), (5, 7, 6, 4), (7, 10, 8, 4))
PROMPT_CHUNKS = PROMPT // CHUNK
TILES = ROWS // TILE
RESP = KEYS - PROMPT
VMEM = pl.BlockSpec(memory_space=pltpu.VMEM)
SMEM = pl.BlockSpec(memory_space=pltpu.SMEM)


def shaped(shape, dtype):
    return jax.ShapeDtypeStruct(shape, dtype)


def aligned(start, size):
    return pl.ds(pl.multiple_of(start, size), size)


def tile_positions(tile, z):
    u = tile * 2
    lane = lax.broadcasted_iota(jnp.int32, (1, TILE), 1)
    low = (u // HEADS * NZ + z) * BLOCK
    high = ((u + 1) // HEADS * NZ + z) * BLOCK - BLOCK
    return low, lane + jnp.where(lane < BLOCK, low, high)


def causal(s, chunk, query_pos):
    key_pos = lax.broadcasted_iota(jnp.int32, (CHUNK, TILE), 0) + chunk * CHUNK
    return jnp.where(key_pos <= query_pos, s, MASKED)


def fold(a):
    return a.reshape(CHUNK // 8, 8, TILE)


def chunk_rows(c):
    return slice(c * CHUNK, (c + 1) * CHUNK)


def over_tiles(body):
    for first, last, chunks, first_masked in CLASSES:

        def step(tile, carry, chunks=chunks, first_masked=first_masked):
            body(tile, chunks, first_masked)
            return carry

        lax.fori_loop(first, last, step, 0)


def forward_kernel(
    info,
    x0, x1, x2, x3,
    kv0, kv1, kv2, kv3,
    r0, r1, r2, r3,
    os, qs, gs, ks, vs, kt, tops, deltas, dq_part,
    kp, vp, kpt, vpt, vt, sc, pm, dk, dv,
):
    y = info[0]
    z = info[1]
    length = info[2]
    for s, x in enumerate((x0, x1, x2, x3)):
        block = lax.rem(y - s + NY, NY)
        start = (block * NZ + z) * BLOCK
        valid = (lax.broadcasted_iota(jnp.int32, (BLOCK, HD), 0) + start) < length
        for j in range(HEADS):
            at = aligned((block * HEADS + j) * BLOCK, BLOCK)
            cols = slice(j * HD, (j + 1) * HD)
            qs[at, :] = x[0, :, cols]
            gs[at, :] = jnp.where(valid, x[1, :, cols].astype(F32), 0.0).astype(BF16)
    for s, kv in enumerate((kv0, kv1, kv2, kv3)):
        zp = lax.rem(z - s + NZ, NZ)
        for b in range(NY):
            at = aligned((zp * NY + b) * PROMPT_ROWS, PROMPT_ROWS)
            kp[at, :] = kv[b, 0, :PROMPT_ROWS, :]
            vp[at, :] = kv[b, 1, :PROMPT_ROWS, :]
            at = aligned((b * NZ + zp) * BLOCK, BLOCK)
            k = kv[b, 0, PROMPT_ROWS:, :]
            v = kv[b, 1, PROMPT_ROWS:, :]
            ks[at, :] = k
            vs[at, :] = v
            kt[:, at] = k.T
            vt[:, at] = v.T
    for c in range(PROMPT_CHUNKS):
        rows = chunk_rows(c)
        kpt[:, rows] = kp[rows, :].T
        vpt[:, rows] = vp[rows, :].T
    dk[...] = jnp.zeros_like(dk)
    dv[...] = jnp.zeros_like(dv)

    def tile_step(tile, chunks, first_masked):
        at = aligned(tile * TILE, TILE)
        low_pos, query_pos = tile_positions(tile, z)

        @pl.when(low_pos < length)
        def _():
            q = qs[at, :]
            qt = q.T
            top = jnp.full((8, TILE), MASKED, F32)
            for c in range(-PROMPT_CHUNKS, chunks):
                k = kp[chunk_rows(c + PROMPT_CHUNKS), :] if c < 0 else ks[chunk_rows(c), :]
                s = jnp.dot(k, qt, preferred_element_type=F32)
                if c >= first_masked:
                    s = causal(s, c, query_pos)
                sc[chunk_rows(c + PROMPT_CHUNKS), :] = s
                top = jnp.maximum(top, jnp.max(fold(s), axis=0))
            top = jnp.max(top, axis=0, keepdims=True)
            total = jnp.zeros((8, TILE), F32)
            out_t = jnp.zeros((HD, TILE), F32)
            for c in range(-PROMPT_CHUNKS, chunks):
                p = jnp.exp2((sc[chunk_rows(c + PROMPT_CHUNKS), :] - top) * SCALE2)
                total = total + jnp.sum(fold(p), axis=0)
                low = p.astype(BF16)
                if c < 0:
                    pm[chunk_rows(c + PROMPT_CHUNKS), :] = low
                    v = vpt[:, chunk_rows(c + PROMPT_CHUNKS)]
                else:
                    v = vt[:, chunk_rows(c)]
                out_t = out_t + jnp.dot(v, low, preferred_element_type=F32)
            inv = 1.0 / jnp.sum(total, axis=0, keepdims=True)
            out_t = out_t * inv
            os[at, :] = jnp.where(query_pos < length, out_t, 0.0).T.astype(BF16)
            grad_t = gs[at, :].astype(F32).T
            delta = jnp.sum(grad_t * out_t, axis=0, keepdims=True) * inv
            grad_t = grad_t * inv
            grad = grad_t.T.astype(BF16)
            grad_t = grad_t.astype(BF16)
            gs[at, :] = grad
            stat = aligned(tile * 8, 8)
            tops[stat, :] = jnp.broadcast_to(top, (8, TILE))
            deltas[stat, :] = jnp.broadcast_to(delta, (8, TILE))
            dq_t = jnp.zeros((HD, TILE), F32)
            for c in range(PROMPT_CHUNKS):
                rows = chunk_rows(c)
                dp = jnp.dot(vp[rows, :], grad_t, preferred_element_type=F32)
                low = pm[rows, :]
                ds = (low.astype(F32) * (dp - delta)).astype(BF16)
                dv[rows, :] += jnp.dot(low, grad, preferred_element_type=F32)
                dk[rows, :] += jnp.dot(ds, q, preferred_element_type=F32)
                dq_t = dq_t + jnp.dot(kpt[:, rows], ds, preferred_element_type=F32)
            dq_part[aligned(tile * HD, HD), :] = dq_t

        @pl.when(low_pos >= length)
        def _():
            os[at, :] = jnp.zeros((TILE, HD), BF16)

    over_tiles(tile_step)
    for s, r in enumerate((r0, r1, r2, r3)):
        zp = lax.rem(z + s, NZ)
        for b in range(NY):
            at = aligned((zp * NY + b) * PROMPT_ROWS, PROMPT_ROWS)
            r[b, 0] = (dk[at, :] * SCALE).astype(BF16)
            r[b, 1] = dv[at, :].astype(BF16)


def forward(info, rows, keyvals):
    return pl.pallas_call(
        forward_kernel,
        out_shape=[shaped((NY, 2, PROMPT_ROWS, HD), BF16)] * 4
        + [
            shaped((ROWS, HD), BF16),
            shaped((ROWS, HD), BF16),
            shaped((ROWS, HD), BF16),
            shaped((RESP, HD), BF16),
            shaped((RESP, HD), BF16),
            shaped((HD, RESP), BF16),
            shaped((TILES * 8, TILE), F32),
            shaped((TILES * 8, TILE), F32),
            shaped((TILES * HD, TILE), F32),
        ],
        in_specs=[SMEM] + [VMEM] * 8,
        out_specs=[VMEM] * 13,
        scratch_shapes=[
            pltpu.VMEM((PROMPT, HD), BF16),
            pltpu.VMEM((PROMPT, HD), BF16),
            pltpu.VMEM((HD, PROMPT), BF16),
            pltpu.VMEM((HD, PROMPT), BF16),
            pltpu.VMEM((HD, RESP), BF16),
            pltpu.VMEM((KEYS, TILE), F32),
            pltpu.VMEM((PROMPT, TILE), BF16),
            pltpu.VMEM((PROMPT, HD), F32),
            pltpu.VMEM((PROMPT, HD), F32),
        ],
        cost_estimate=pl.CostEstimate(
            flops=16 * 10**9, bytes_accessed=8 * 2**20, transcendentals=5 * 10**6
        ),
        compiler_params=pltpu.CompilerParams(vmem_limit_bytes=40 * 2**20),
        name="forward",
    )(info, *rows, *keyvals)


def backward_kernel(
    info, os, qs, gs, ks, vs, kt, tops, deltas, dq_part,
    d0, d1, d2, d3,
    r0, r1, r2, r3,
    dk, dv, dq,
):
    y = info[0]
    z = info[1]
    length = info[2]
    dk[...] = jnp.zeros_like(dk)
    dv[...] = jnp.zeros_like(dv)

    def tile_step(tile, chunks, first_masked):
        at = aligned(tile * TILE, TILE)
        low_pos, query_pos = tile_positions(tile, z)

        @pl.when(low_pos < length)
        def _():
            q = qs[at, :]
            qt = q.T
            grad = gs[at, :]
            grad_t = grad.T
            stat = aligned(tile * 8, 8)
            top = tops[stat, :][:1]
            delta = deltas[stat, :][:1]
            dq_t = dq_part[aligned(tile * HD, HD), :]
            for c in range(chunks):
                rows = chunk_rows(c)
                s = jnp.dot(ks[rows, :], qt, preferred_element_type=F32)
                if c >= first_masked:
                    s = causal(s, c, query_pos)
                p = jnp.exp2((s - top) * SCALE2)
                dp = jnp.dot(vs[rows, :], grad_t, preferred_element_type=F32)
                ds = (p * (dp - delta)).astype(BF16)
                dv[rows, :] += jnp.dot(p.astype(BF16), grad, preferred_element_type=F32)
                dk[rows, :] += jnp.dot(ds, q, preferred_element_type=F32)
                dq_t = dq_t + jnp.dot(kt[:, rows], ds, preferred_element_type=F32)
            dq[at, :] = (dq_t * SCALE).T.astype(BF16)

        @pl.when(low_pos >= length)
        def _():
            dq[at, :] = jnp.zeros((TILE, HD), BF16)

    over_tiles(tile_step)
    for s, d in enumerate((d0, d1, d2, d3)):
        block = lax.rem(y + s, NY)
        for j in range(HEADS):
            at = aligned((block * HEADS + j) * BLOCK, BLOCK)
            cols = slice(j * HD, (j + 1) * HD)
            d[0, :, cols] = os[at, :]
            d[1, :, cols] = dq[at, :]
    for s, r in enumerate((r0, r1, r2, r3)):
        zp = lax.rem(z + s, NZ)
        for b in range(NY):
            at = aligned((b * NZ + zp) * BLOCK, BLOCK)
            r[b, 0] = (dk[at, :] * SCALE).astype(BF16)
            r[b, 1] = dv[at, :].astype(BF16)


def backward(info, state):
    return pl.pallas_call(
        backward_kernel,
        out_shape=[shaped((2, BLOCK, HEADS * HD), BF16)] * 4
        + [shaped((NY, 2, BLOCK, HD), BF16)] * 4,
        in_specs=[SMEM] + [VMEM] * 9,
        out_specs=[VMEM] * 8,
        scratch_shapes=[
            pltpu.VMEM((RESP, HD), F32),
            pltpu.VMEM((RESP, HD), F32),
            pltpu.VMEM((ROWS, HD), BF16),
        ],
        cost_estimate=pl.CostEstimate(
            flops=16 * 10**9, bytes_accessed=8 * 2**20, transcendentals=5 * 10**6
        ),
        compiler_params=pltpu.CompilerParams(vmem_limit_bytes=40 * 2**20),
        name="backward",
    )(info, *state)


def settle_kernel(
    info,
    d0, d1, d2, d3,
    r0, r1, r2, r3,
    a, d, p0, p1, p2, p3,
):
    y = info[0]
    width = HEADS * HD
    for s, rows in enumerate((d0, d1, d2, d3)):
        at = aligned(lax.rem(y - s + NY, NY) * width, width)
        a[:, at] = rows[0]
        d[:, at] = rows[1]
    for s, p in enumerate((p0, p1, p2, p3)):
        b = lax.rem(y + s, NY)
        p[...] = (
            (r0[b].astype(F32) + r1[b].astype(F32)) + (r2[b].astype(F32) + r3[b].astype(F32))
        ).astype(BF16)


def settle(info, rows, terms):
    out = shaped((BLOCK, NY * HEADS * HD), BF16)
    return pl.pallas_call(
        settle_kernel,
        out_shape=[out, out] + [shaped((2, BLOCK, HD), BF16)] * 4,
        in_specs=[SMEM] + [VMEM] * 8,
        out_specs=[VMEM] * 6,
        name="settle",
    )(info, *rows, *terms)


def place_kernel(info, p0, p1, p2, p3, dk, dv):
    y = info[0]
    for s, p in enumerate((p0, p1, p2, p3)):
        at = aligned(lax.rem(y - s + NY, NY) * HD, HD)
        dk[:, at] = p[0].astype(F32)
        dv[:, at] = p[1].astype(F32)


def place(info, pieces):
    rows = pieces[0].shape[1]
    out = shaped((rows, NY * HD), F32)
    return pl.pallas_call(
        place_kernel,
        out_shape=[out, out],
        in_specs=[SMEM] + [VMEM] * 4,
        out_specs=[VMEM] * 2,
        name="place",
    )(info, *pieces)


def y_shift(a, s):
    pairs = [(i * NZ + k, (i + s) % NY * NZ + k) for i in range(NY) for k in range(NZ)]
    return lax.ppermute(a, "prefix", pairs)


def z_shift(a, s):
    pairs = [(i * NZ + k, i * NZ + (k + s) % NZ) for i in range(NY) for k in range(NZ)]
    return lax.ppermute(a, "prefix", pairs)


def core_swap(a):
    return lax.ppermute(a, "resp", [(i, i ^ 1) for i in range(16)])


def x_shift(a, s):
    pairs = [(h * 8 + x * 2 + c, h * 8 + (x + s) % 4 * 2 + c) for h in range(2) for x in range(4) for c in range(2)]
    return lax.ppermute(a, "resp", pairs)


def far_swap(a):
    return lax.ppermute(a, "resp", [(i, i ^ 8) for i in range(16)])


def over_responses(dk, dv):
    core = lax.axis_index("resp") % 2
    half = (jnp.where(core == 0, dk, dv) + core_swap(jnp.where(core == 0, dv, dk))).astype(BF16)
    near, across, back = (x_shift(half, s).astype(F32) for s in (1, 2, 3))
    low = ((half.astype(F32) + across) + (near + back)).astype(BF16)
    half = low.astype(F32) + far_swap(low).astype(F32)
    other = core_swap(half)
    return jnp.where(core == 0, half, other), jnp.where(core == 0, other, half)


def by_y(pieces):
    return [pieces[0]] + [y_shift(pieces[s], s) for s in range(1, NY)]


def by_z(pieces):
    return [pieces[0]] + [z_shift(pieces[s], s) for s in range(1, NZ)]


def per_device(
    response_queries,
    response_keys,
    response_values,
    prompt_keys,
    prompt_values,
    output_grad,
    lengths,
):
    prefix = lax.axis_index("prefix")
    y, z = prefix // NZ, prefix % NZ
    info = jnp.stack([y, z, lengths[lax.axis_index("resp")]]).astype(jnp.int32)
    pick = lax.dynamic_index_in_dim

    def split(a, width):
        return [
            lax.dynamic_slice_in_dim(a, (y + s) % NY * width, width, a.ndim - 1)
            for s in range(NY)
        ]

    keyvals = jnp.stack(
        [
            jnp.concatenate([prompt_keys, response_keys[0]], axis=0),
            jnp.concatenate([prompt_values, response_values[0]], axis=0),
        ]
    )
    keyvals = by_y(split(keyvals, HD))
    *keyvals, queries, grads = lax.optimization_barrier(
        (*keyvals, response_queries[0], output_grad[0])
    )
    stacked = jnp.stack(keyvals)
    keyvals = jnp.stack([pick(stacked, (y - b) % NY, 0, keepdims=False) for b in range(NY)])
    keyvals = by_z([keyvals] * NZ)
    rows = by_y(split(jnp.stack([queries, grads]), HEADS * HD))

    *prompt_terms, os, qs, gs, ks, vs, kt, tops, deltas, dq_part = forward(info, rows, keyvals)
    prompt_terms = by_z(prompt_terms)
    back = backward(info, (os, qs, gs, ks, vs, kt, tops, deltas, dq_part))
    *prompt_terms, rows_first, back_first = lax.optimization_barrier(
        (*prompt_terms, back[0], back[4])
    )
    rows = by_y([rows_first, *back[1:4]])
    terms = by_z([back_first, *back[5:]])
    prompt = sum(t.astype(F32) for t in prompt_terms).astype(BF16)
    prompt = by_y([pick(prompt, (y + s) % NY, 0, keepdims=False) for s in range(NY)])
    prompt_key_grad, prompt_value_grad = over_responses(*place(info, prompt))
    attention_out, query_grad, *pieces = settle(info, rows, terms)
    key_own, value_own = place(info, by_y(pieces))
    return (
        attention_out[None],
        query_grad[None],
        key_own[None],
        value_own[None],
        prompt_key_grad,
        prompt_value_grad,
    )


def solution(mesh):
    return jax.shard_map(
        per_device,
        mesh=mesh,
        in_specs=(
            P("resp", "prefix", None),
            P("resp", "prefix", None),
            P("resp", "prefix", None),
            P("prefix", None),
            P("prefix", None),
            P("resp", "prefix", None),
            P(),
        ),
        out_specs=(
            P("resp", "prefix", None),
            P("resp", "prefix", None),
            P("resp", "prefix", None),
            P("resp", "prefix", None),
            P("prefix", None),
            P("prefix", None),
        ),
        check_vma=False,
    )
```

profile of v0, /device:TPU:1, one launch (start us, length us, event | category | flops | bytes accessed | tf_op | source)
XLA Modules:
  0.0 148.1 jit_solution(7112345409328490813)
XLA Ops:
  0.8 1.1 maximum_bitcast_fusion
  1.9 3.6 %collective-permute-start.2 = (bf16[2,176,128]{2,1,0:T(8,128)(2,1)S(1)}, bf16[2,176,128]{2,1,0:T(8,128)(2,1)S(1)}, u32[]{:S(2)}, u32[]{:S(2)}) collective-permute-start(bf16[2,176,128]{2,1,0:T(8,128)(2,1)S(1)} %get-tuple-element.100), channel_id=1, source_target_pairs={{0,192},{16,208},{32,224},{48,240},{64,0},{80,16},{96,32},{112,48}... | collective-permute-start | bytes 270344 | tf_op jit(solution)/shard_map/ppermute | solution.py:346
  5.6 1.6 %collective-permute-start.1 = (bf16[2,176,128]{2,1,0:T(8,128)(2,1)S(1)}, bf16[2,176,128]{2,1,0:T(8,128)(2,1)S(1)}, u32[]{:S(2)}, u32[]{:S(2)}) collective-permute-start(bf16[2,176,128]{2,1,0:T(8,128)(2,1)S(1)} %get-tuple-element.103), channel_id=1, source_target_pairs={{0,128},{16,144},{32,160},{48,176},{64,192},{80,208},{96,224},{112... | collective-permute-start | bytes 270344 | tf_op jit(solution)/shard_map/ppermute | solution.py:346
  7.2 4.2 %collective-permute-done = bf16[2,176,128]{2,1,0:T(8,128)(2,1)S(1)} collective-permute-done((bf16[2,176,128]{2,1,0:T(8,128)(2,1)S(1)}, bf16[2,176,128]{2,1,0:T(8,128)(2,1)S(1)}, u32[]{:S(2)}, u32[]{:S(2)}) %collective-permute-start) | collective-permute-done | bytes 90144 | tf_op jit(solution)/shard_map/ppermute | solution.py:346
  11.6 1.8 %collective-permute-start.5 = (bf16[2,128,640]{2,1,0:T(8,128)(2,1)S(1)}, bf16[2,128,640]{2,1,0:T(8,128)(2,1)S(1)}, u32[]{:S(2)}, u32[]{:S(2)}) collective-permute-start(bf16[2,128,640]{2,1,0:T(8,128)(2,1)S(1)} %get-tuple-element.92), channel_id=1, source_target_pairs={{0,192},{16,208},{32,224},{48,240},{64,0},{80,16},{96,32},{112,48}... | collective-permute-start | bytes 983048 | tf_op jit(solution)/shard_map/ppermute | solution.py:346
  13.5 4.4 %collective-permute-start.8 = (bf16[4,2,176,128]{3,2,1,0:T(8,128)(2,1)S(1)}, bf16[4,2,176,128]{3,2,1,0:T(8,128)(2,1)S(1)}, u32[]{:S(2)}, u32[]{:S(2)}) collective-permute-start(bf16[4,2,176,128]{3,2,1,0:T(8,128)(2,1)S(1)} %pad_maximum_fusion.1.kv0), channel_id=1, source_target_pairs={{0,48},{16,0},{32,16},{48,32},{64,112},{80,64},{96,80},{112,96},{1... | collective-permute-start | bytes 1081352 | tf_op jit(solution)/shard_map/ppermute | solution.py:351
  18.5 1.7 %collective-permute-start.4 = (bf16[2,128,640]{2,1,0:T(8,128)(2,1)S(1)}, bf16[2,128,640]{2,1,0:T(8,128)(2,1)S(1)}, u32[]{:S(2)}, u32[]{:S(2)}) collective-permute-start(bf16[2,128,640]{2,1,0:T(8,128)(2,1)S(1)} %get-tuple-element.95), channel_id=1, source_target_pairs={{0,128},{16,144},{32,160},{48,176},{64,192},{80,208},{96,224},{112... | collective-permute-start | bytes 983048 | tf_op jit(solution)/shard_map/ppermute | solution.py:346
  20.8 0.7 pad_add_fusion.info
  21.5 6.8 %collective-permute-done.3.x1 = bf16[2,128,640]{2,1,0:T(8,128)(2,1)S(1)} collective-permute-done((bf16[2,128,640]{2,1,0:T(8,128)(2,1)S(1)}, bf16[2,128,640]{2,1,0:T(8,128)(2,1)S(1)}, u32[]{:S(2)}, u32[]{:S(2)}) %collective-permute-start.3) | collective-permute-done | bytes 327712 | tf_op jit(solution)/shard_map/ppermute | solution.py:346
  28.3 3.0 %collective-permute-done.4.x2 = bf16[2,128,640]{2,1,0:T(8,128)(2,1)S(1)} collective-permute-done((bf16[2,128,640]{2,1,0:T(8,128)(2,1)S(1)}, bf16[2,128,640]{2,1,0:T(8,128)(2,1)S(1)}, u32[]{:S(2)}, u32[]{:S(2)}) %collective-permute-start.4) | collective-permute-done | bytes 327712 | tf_op jit(solution)/shard_map/ppermute | solution.py:346
  31.3 14.4 %collective-permute-done.7.kv2 = bf16[4,2,176,128]{3,2,1,0:T(8,128)(2,1)S(1)} collective-permute-done((bf16[4,2,176,128]{3,2,1,0:T(8,128)(2,1)S(1)}, bf16[4,2,176,128]{3,2,1,0:T(8,128)(2,1)S(1)}, u32[]{:S(2)}, u32[]{:S(2)}) %collective-permute-start.7) | collective-permute-done | bytes 360480 | tf_op jit(solution)/shard_map/ppermute | solution.py:351
  45.7 19.4 %forward.1 = (bf16[4,2,48,128]{3,2,1,0:T(8,128)(2,1)S(1)}, bf16[4,2,48,128]{3,2,1,0:T(8,128)(2,1)S(1)}, bf16[4,2,48,128]{3,2,1,0:T(8,128)(2,1)S(1)}, bf16[4,2,48...) custom-call(s32[3]{0:T(128)S(1)} %pad_add_fusion.info, ...), custom_call_target="tpu_custom_call" | custom-call | flops 16000000000 | bytes 8388608 | tf_op jit(solution)/shard_map/forward/pallas_call | solution.py:180
  65.1 3.2 %collective-permute-start.9 = (bf16[4,2,48,128]{3,2,1,0:T(8,128)(2,1)S(1)}, bf16[4,2,48,128]{3,2,1,0:T(8,128)(2,1)S(1)}, u32[]{:S(2)}, u32[]{:S(2)}) collective-permute-start(bf16[4,2,48,128]{3,2,1,0:T(8,128)(2,1)S(1)} %get-tuple-element.56), channel_id=1, source_target_pairs={{0,16},{16,32},{32,48},{48,0},{64,80},{80,96},{96,112},{112,64},{1... | collective-permute-start | bytes 294920 | tf_op jit(solution)/shard_map/ppermute | solution.py:351
  68.2 2.0 %collective-permute-start.10 = (bf16[4,2,48,128]{3,2,1,0:T(8,128)(2,1)S(1)}, bf16[4,2,48,128]{3,2,1,0:T(8,128)(2,1)S(1)}, u32[]{:S(2)}, u32[]{:S(2)}) collective-permute-start(bf16[4,2,48,128]{3,2,1,0:T(8,128)(2,1)S(1)} %get-tuple-element.57), channel_id=1, source_target_pairs={{0,32},{16,48},{32,0},{48,16},{64,96},{80,112},{96,64},{112,80},{1... | collective-permute-start | bytes 294920 | tf_op jit(solution)/shard_map/ppermute | solution.py:351
  70.3 2.3 %collective-permute-start.11 = (bf16[4,2,48,128]{3,2,1,0:T(8,128)(2,1)S(1)}, bf16[4,2,48,128]{3,2,1,0:T(8,128)(2,1)S(1)}, u32[]{:S(2)}, u32[]{:S(2)}) collective-permute-start(bf16[4,2,48,128]{3,2,1,0:T(8,128)(2,1)S(1)} %get-tuple-element.58), channel_id=1, source_target_pairs={{0,48},{16,0},{32,16},{48,32},{64,112},{80,64},{96,80},{112,96},{1... | collective-permute-start | bytes 294920 | tf_op jit(solution)/shard_map/ppermute | solution.py:351
  72.5 15.6 %backward.1 = (bf16[2,128,640]{2,1,0:T(8,128)(2,1)S(1)}, bf16[2,128,640]{2,1,0:T(8,128)(2,1)S(1)}, bf16[2,128,640]{2,1,0:T(8,128)(2,1)S(1)}, bf16[2,128,640]{2,1...) custom-call(s32[3]{0:T(128)S(1)} %pad_add_fusion.info, ...), custom_call_target="tpu_custom_call" | custom-call | flops 16000000000 | bytes 8388608 | tf_op jit(solution)/shard_map/backward/pallas_call | solution.py:275
  88.2 0.7 copy-done
  88.9 0.7 copy-done.1
  89.7 0.6 dynamic-slice_bitcast_fusion
  90.3 1.5 %collective-permute-start.22 = (bf16[2,48,128]{2,1,0:T(8,128)(2,1)S(1)}, bf16[2,48,128]{2,1,0:T(8,128)(2,1)S(1)}, u32[]{:S(2)}, u32[]{:S(2)}) collective-permute-start(bf16[2,48,128]{2,1,0:T(8,128)(2,1)S(1)} %get-tuple-element.107), channel_id=1, source_target_pairs={{0,128},{16,144},{32,160},{48,176},{64,192},{80,208},{96,224},{112... | collective-permute-start | bytes 73736 | tf_op jit(solution)/shard_map/ppermute | solution.py:346
  91.9 1.1 collective-permute-done.23.p3
  93.0 1.5 %collective-permute-done.22.p2 = bf16[2,48,128]{2,1,0:T(8,128)(2,1)S(1)} collective-permute-done((bf16[2,48,128]{2,1,0:T(8,128)(2,1)S(1)}, bf16[2,48,128]{2,1,0:T(8,128)(2,1)S(1)}, u32[]{:S(2)}, u32[]{:S(2)}) %collective-permute-start.22) | collective-permute-done | bytes 24608 | tf_op jit(solution)/shard_map/ppermute | solution.py:346
  94.5 1.2 collective-permute-done.21.p1
  95.8 0.6 copy-done.16
  96.4 1.5 %place.3 = (f32[48,512]{1,0:T(8,128)}, f32[48,512]{1,0:T(8,128)}) custom-call(s32[3]{0:T(128)} %copy-done.2, bf16[2,48,128]{2,1,0:T(8,128)(2,1)} %get-tuple-element.109.p0, bf16[2,48,128]{2,1,0:T(8,128)(2,1)} %copy-done.16, bf16[2,48,128]{2,1,0:T(8,128)(2,1)} %copy-done.15, bf16[2,48,128]{2,1,0:T(8,128)(2,1)} %copy-done.14), custom_call_target="tpu_custom_call" | custom-call | tf_op jit(solution)/shard_map/place/pallas_call | solution.py:335
  97.9 0.9 broadcast_select_fusion.2
  98.9 1.3 collective-permute-done.24
  100.2 0.9 add_convert_fusion.2
  101.5 1.1 collective-permute-start.26
  103.0 1.1 collective-permute-done.27
  104.1 1.0 collective-permute-start.13
  105.1 0.6 collective-permute-done.26
  105.7 1.1 collective-permute-start.14
  107.1 8.4 %collective-permute-start.28 = (bf16[48,512]{1,0:T(8,128)(2,1)S(1)}, bf16[48,512]{1,0:T(8,128)(2,1)S(1)}, u32[]{:S(2)}, u32[]{:S(2)}) collective-permute-start(bf16[48,512]{1,0:T(8,128)(2,1)S(1)} %add_convert_fusion.1), channel_id=1, source_target_pairs={{0,8},{1,9},{2,10},{3,11},{4,12},{5,13},{6,14},{7,15},{8,0},{9,1},... | collective-permute-start | bytes 147464 | tf_op jit(solution)/shard_map/ppermute | solution.py:364
  116.0 1.7 %collective-permute-done.28 = bf16[48,512]{1,0:T(8,128)(2,1)S(1)} collective-permute-done((bf16[48,512]{1,0:T(8,128)(2,1)S(1)}, bf16[48,512]{1,0:T(8,128)(2,1)S(1)}, u32[]{:S(2)}, u32[]{:S(2)}) %collective-permute-start.28) | collective-permute-done | bytes 49184 | tf_op jit(solution)/shard_map/ppermute | solution.py:364
  117.7 2.9 %collective-permute-start.17 = (bf16[4,2,128,128]{3,2,1,0:T(8,128)(2,1)S(1)}, bf16[4,2,128,128]{3,2,1,0:T(8,128)(2,1)S(1)}, u32[]{:S(2)}, u32[]{:S(2)}) collective-permute-start(bf16[4,2,128,128]{3,2,1,0:T(8,128)(2,1)S(1)} %get-tuple-element.77), channel_id=1, source_target_pairs={{0,48},{16,0},{32,16},{48,32},{64,112},{80,64},{96,80},{112,96},{1... | collective-permute-start | bytes 786440 | tf_op jit(solution)/shard_map/ppermute | solution.py:351
  120.6 11.0 %collective-permute-done.16.r2 = bf16[4,2,128,128]{3,2,1,0:T(8,128)(2,1)S(1)} collective-permute-done((bf16[4,2,128,128]{3,2,1,0:T(8,128)(2,1)S(1)}, bf16[4,2,128,128]{3,2,1,0:T(8,128)(2,1)S(1)}, u32[]{:S(2)}, u32[]{:S(2)}) %collective-permute-start.16) | collective-permute-done | bytes 262176 | tf_op jit(solution)/shard_map/ppermute | solution.py:351
  131.6 0.6 collective-permute-start.29
  132.2 2.1 %collective-permute-done.17.r3 = bf16[4,2,128,128]{3,2,1,0:T(8,128)(2,1)S(1)} collective-permute-done((bf16[4,2,128,128]{3,2,1,0:T(8,128)(2,1)S(1)}, bf16[4,2,128,128]{3,2,1,0:T(8,128)(2,1)S(1)}, u32[]{:S(2)}, u32[]{:S(2)}) %collective-permute-start.17) | collective-permute-done | bytes 262176 | tf_op jit(solution)/shard_map/ppermute | solution.py:351
  134.4 0.7 copy-done.10
  135.3 0.7 copy-done.7
  136.0 2.8 %settle.1 = (bf16[128,2560]{1,0:T(8,128)(2,1)}, bf16[128,2560]{1,0:T(8,128)(2,1)}, bf16[2,128,128]{2,1,0:T(8,128)(2,1)}, bf16[2,128,128]{2,1,0:T(8,128)(2,1)}, b...) custom-call(s32[3]{0:T(128)} %copy-done.2, bf16[2,128,640]{2,1,0:T(8,128)(2,1)} %copy-done, ...), custom_call_target="tpu_custom_call" | custom-call | tf_op jit(solution)/shard_map/settle/pallas_call | solution.py:315
  138.9 2.1 %collective-permute-start.19 = (bf16[2,128,128]{2,1,0:T(8,128)(2,1)}, bf16[2,128,128]{2,1,0:T(8,128)(2,1)S(1)}, u32[]{:S(2)}, u32[]{:S(2)}) collective-permute-start(bf16[2,128,128]{2,1,0:T(8,128)(2,1)} %get-tuple-element.82), channel_id=1, source_target_pairs={{0,128},{16,144},{32,160},{48,176},{64,192},{80,208},{96,224},{112... | collective-permute-start | bytes 196616 | tf_op jit(solution)/shard_map/ppermute | solution.py:346
  141.5 2.5 %collective-permute-done.18.p1 = bf16[2,128,128]{2,1,0:T(8,128)(2,1)S(1)} collective-permute-done((bf16[2,128,128]{2,1,0:T(8,128)(2,1)}, bf16[2,128,128]{2,1,0:T(8,128)(2,1)S(1)}, u32[]{:S(2)}, u32[]{:S(2)}) %collective-permute-start.18) | collective-permute-done | bytes 65568 | tf_op jit(solution)/shard_map/ppermute | solution.py:346
  144.2 0.8 collective-permute-done.20.p3
  145.0 0.6 copy-done.13
  145.6 1.8 %place.2 = (f32[128,512]{1,0:T(8,128)}, f32[128,512]{1,0:T(8,128)}) custom-call(s32[3]{0:T(128)} %copy-done.2, bf16[2,128,128]{2,1,0:T(8,128)(2,1)} %get-tuple-element.80.p0, bf16[2,128,128]{2,1,0:T(8,128)(2,1)} %copy-done.11, bf16[2,128,128]{2,1,0:T(8,128)(2,1)} %copy-done.12, bf16[2,128,128]{2,1,0:T(8,128)(2,1)} %copy-done.13), custom_call_target="tpu_custom_call" | custom-call | tf_op jit(solution)/shard_map/place/pallas_call | solution.py:335
  147.4 0.7 broadcast_select_fusion
  (68 shorter events, 4.4 us)
Async XLA Ops:
  0.6 10.8 %copy-start.4 = (bf16[1,128,2560]{2,1,0:T(8,128)(2,1)S(1)}, bf16[1,128,2560]{2,1,0:T(8,128)(2,1)}, u32[]{:S(2)}) copy-start(bf16[1,128,2560]{2,1,0:T(8,128)(2,1)} %param.12) | copy-start | bytes 1966084
  0.6 10.8 %copy-start.3 = (bf16[1,128,2560]{2,1,0:T(8,128)(2,1)S(1)}, bf16[1,128,2560]{2,1,0:T(8,128)(2,1)}, u32[]{:S(2)}) copy-start(bf16[1,128,2560]{2,1,0:T(8,128)(2,1)} %param.7) | copy-start | bytes 1966084
  1.9 5.3 %collective-permute-start.2 = (bf16[2,176,128]{2,1,0:T(8,128)(2,1)S(1)}, bf16[2,176,128]{2,1,0:T(8,128)(2,1)S(1)}, u32[]{:S(2)}, u32[]{:S(2)}) collective-permute-start(bf16[2,176,128]{2,1,0:T(8,128)(2,1)S(1)} %get-tuple-element.100), channel_id=1, source_target_pairs={{0,192},{16,208},{32,224},{48,240},{64,0},{80,16},{96,32},{112,48}... | collective-permute-start | bytes 270344 | tf_op jit(solution)/shard_map/ppermute | solution.py:346
  5.6 5.8 %collective-permute-start = (bf16[2,176,128]{2,1,0:T(8,128)(2,1)S(1)}, bf16[2,176,128]{2,1,0:T(8,128)(2,1)S(1)}, u32[]{:S(2)}, u32[]{:S(2)}) collective-permute-start(bf16[2,176,128]{2,1,0:T(8,128)(2,1)S(1)} %get-tuple-element.102), channel_id=1, source_target_pairs={{0,64},{16,80},{32,96},{48,112},{64,128},{80,144},{96,160},{112,17... | collective-permute-start | bytes 270344 | tf_op jit(solution)/shard_map/ppermute | solution.py:346
  5.6 5.8 %collective-permute-start.1 = (bf16[2,176,128]{2,1,0:T(8,128)(2,1)S(1)}, bf16[2,176,128]{2,1,0:T(8,128)(2,1)S(1)}, u32[]{:S(2)}, u32[]{:S(2)}) collective-permute-start(bf16[2,176,128]{2,1,0:T(8,128)(2,1)S(1)} %get-tuple-element.103), channel_id=1, source_target_pairs={{0,128},{16,144},{32,160},{48,176},{64,192},{80,208},{96,224},{112... | collective-permute-start | bytes 270344 | tf_op jit(solution)/shard_map/ppermute | solution.py:346
  11.6 8.6 %copy-start.17 = (s32[16]{0:T(128)S(1)}, s32[16]{0:T(128)}, u32[]{:S(2)}) copy-start(s32[16]{0:T(128)} %param.13) | copy-start | bytes 196
  11.6 6.9 %collective-permute-start.5 = (bf16[2,128,640]{2,1,0:T(8,128)(2,1)S(1)}, bf16[2,128,640]{2,1,0:T(8,128)(2,1)S(1)}, u32[]{:S(2)}, u32[]{:S(2)}) collective-permute-start(bf16[2,128,640]{2,1,0:T(8,128)(2,1)S(1)} %get-tuple-element.92), channel_id=1, source_target_pairs={{0,192},{16,208},{32,224},{48,240},{64,0},{80,16},{96,32},{112,48}... | collective-permute-start | bytes 983048 | tf_op jit(solution)/shard_map/ppermute | solution.py:346
  13.5 17.8 %collective-permute-start.8 = (bf16[4,2,176,128]{3,2,1,0:T(8,128)(2,1)S(1)}, bf16[4,2,176,128]{3,2,1,0:T(8,128)(2,1)S(1)}, u32[]{:S(2)}, u32[]{:S(2)}) collective-permute-start(bf16[4,2,176,128]{3,2,1,0:T(8,128)(2,1)S(1)} %pad_maximum_fusion.1.kv0), channel_id=1, source_target_pairs={{0,48},{16,0},{32,16},{48,32},{64,112},{80,64},{96,80},{112,96},{1... | collective-permute-start | bytes 1081352 | tf_op jit(solution)/shard_map/ppermute | solution.py:351
  17.9 27.8 %collective-permute-start.7 = (bf16[4,2,176,128]{3,2,1,0:T(8,128)(2,1)S(1)}, bf16[4,2,176,128]{3,2,1,0:T(8,128)(2,1)S(1)}, u32[]{:S(2)}, u32[]{:S(2)}) collective-permute-start(bf16[4,2,176,128]{3,2,1,0:T(8,128)(2,1)S(1)} %pad_maximum_fusion.1.kv0), channel_id=1, source_target_pairs={{0,32},{16,48},{32,0},{48,16},{64,96},{80,112},{96,64},{112,80},{1... | collective-permute-start | bytes 1081352 | tf_op jit(solution)/shard_map/ppermute | solution.py:351
  17.9 27.8 %collective-permute-start.6 = (bf16[4,2,176,128]{3,2,1,0:T(8,128)(2,1)S(1)}, bf16[4,2,176,128]{3,2,1,0:T(8,128)(2,1)S(1)}, u32[]{:S(2)}, u32[]{:S(2)}) collective-permute-start(bf16[4,2,176,128]{3,2,1,0:T(8,128)(2,1)S(1)} %pad_maximum_fusion.1.kv0), channel_id=1, source_target_pairs={{0,16},{16,32},{32,48},{48,0},{64,80},{80,96},{96,112},{112,64},{1... | collective-permute-start | bytes 1081352 | tf_op jit(solution)/shard_map/ppermute | solution.py:351
  18.3 10.0 %collective-permute-start.3 = (bf16[2,128,640]{2,1,0:T(8,128)(2,1)S(1)}, bf16[2,128,640]{2,1,0:T(8,128)(2,1)S(1)}, u32[]{:S(2)}, u32[]{:S(2)}) collective-permute-start(bf16[2,128,640]{2,1,0:T(8,128)(2,1)S(1)} %get-tuple-element.94), channel_id=1, source_target_pairs={{0,64},{16,80},{32,96},{48,112},{64,128},{80,144},{96,160},{112,17... | collective-permute-start | bytes 983048 | tf_op jit(solution)/shard_map/ppermute | solution.py:346
  18.5 12.8 %collective-permute-start.4 = (bf16[2,128,640]{2,1,0:T(8,128)(2,1)S(1)}, bf16[2,128,640]{2,1,0:T(8,128)(2,1)S(1)}, u32[]{:S(2)}, u32[]{:S(2)}) collective-permute-start(bf16[2,128,640]{2,1,0:T(8,128)(2,1)S(1)} %get-tuple-element.95), channel_id=1, source_target_pairs={{0,128},{16,144},{32,160},{48,176},{64,192},{80,208},{96,224},{112... | collective-permute-start | bytes 983048 | tf_op jit(solution)/shard_map/ppermute | solution.py:346
  21.5 51.1 %copy-start.2 = (s32[3]{0:T(128)}, s32[3]{0:T(128)S(1)}, u32[]{:S(2)}) copy-start(s32[3]{0:T(128)S(1)} %pad_add_fusion.info) | copy-start | bytes 40
  65.1 24.5 %collective-permute-start.9 = (bf16[4,2,48,128]{3,2,1,0:T(8,128)(2,1)S(1)}, bf16[4,2,48,128]{3,2,1,0:T(8,128)(2,1)S(1)}, u32[]{:S(2)}, u32[]{:S(2)}) collective-permute-start(bf16[4,2,48,128]{3,2,1,0:T(8,128)(2,1)S(1)} %get-tuple-element.56), channel_id=1, source_target_pairs={{0,16},{16,32},{32,48},{48,0},{64,80},{80,96},{96,112},{112,64},{1... | collective-permute-start | bytes 294920 | tf_op jit(solution)/shard_map/ppermute | solution.py:351
  68.2 21.4 %collective-permute-start.10 = (bf16[4,2,48,128]{3,2,1,0:T(8,128)(2,1)S(1)}, bf16[4,2,48,128]{3,2,1,0:T(8,128)(2,1)S(1)}, u32[]{:S(2)}, u32[]{:S(2)}) collective-permute-start(bf16[4,2,48,128]{3,2,1,0:T(8,128)(2,1)S(1)} %get-tuple-element.57), channel_id=1, source_target_pairs={{0,32},{16,48},{32,0},{48,16},{64,96},{80,112},{96,64},{112,80},{1... | collective-permute-start | bytes 294920 | tf_op jit(solution)/shard_map/ppermute | solution.py:351
  70.3 19.3 %collective-permute-start.11 = (bf16[4,2,48,128]{3,2,1,0:T(8,128)(2,1)S(1)}, bf16[4,2,48,128]{3,2,1,0:T(8,128)(2,1)S(1)}, u32[]{:S(2)}, u32[]{:S(2)}) collective-permute-start(bf16[4,2,48,128]{3,2,1,0:T(8,128)(2,1)S(1)} %get-tuple-element.58), channel_id=1, source_target_pairs={{0,48},{16,0},{32,16},{48,32},{64,112},{80,64},{96,80},{112,96},{1... | collective-permute-start | bytes 294920 | tf_op jit(solution)/shard_map/ppermute | solution.py:351
  88.2 0.7 copy-start
  88.9 0.7 copy-start.1
  90.3 2.7 %collective-permute-start.23 = (bf16[2,48,128]{2,1,0:T(8,128)(2,1)S(1)}, bf16[2,48,128]{2,1,0:T(8,128)(2,1)S(1)}, u32[]{:S(2)}, u32[]{:S(2)}) collective-permute-start(bf16[2,48,128]{2,1,0:T(8,128)(2,1)S(1)} %get-tuple-element.106), channel_id=1, source_target_pairs={{0,192},{16,208},{32,224},{48,240},{64,0},{80,16},{96,32},{112,48}... | collective-permute-start | bytes 73736 | tf_op jit(solution)/shard_map/ppermute | solution.py:346
  90.3 4.2 %collective-permute-start.22 = (bf16[2,48,128]{2,1,0:T(8,128)(2,1)S(1)}, bf16[2,48,128]{2,1,0:T(8,128)(2,1)S(1)}, u32[]{:S(2)}, u32[]{:S(2)}) collective-permute-start(bf16[2,48,128]{2,1,0:T(8,128)(2,1)S(1)} %get-tuple-element.107), channel_id=1, source_target_pairs={{0,128},{16,144},{32,160},{48,176},{64,192},{80,208},{96,224},{112... | collective-permute-start | bytes 73736 | tf_op jit(solution)/shard_map/ppermute | solution.py:346
  91.9 3.9 %collective-permute-start.21 = (bf16[2,48,128]{2,1,0:T(8,128)(2,1)S(1)}, bf16[2,48,128]{2,1,0:T(8,128)(2,1)S(1)}, u32[]{:S(2)}, u32[]{:S(2)}) collective-permute-start(bf16[2,48,128]{2,1,0:T(8,128)(2,1)S(1)} %get-tuple-element.108), channel_id=1, source_target_pairs={{0,64},{16,80},{32,96},{48,112},{64,128},{80,144},{96,160},{112,17... | collective-permute-start | bytes 73736 | tf_op jit(solution)/shard_map/ppermute | solution.py:346
  93.0 2.8 %copy-start.14 = (bf16[2,48,128]{2,1,0:T(8,128)(2,1)}, bf16[2,48,128]{2,1,0:T(8,128)(2,1)S(1)}, u32[]{:S(2)}) copy-start(bf16[2,48,128]{2,1,0:T(8,128)(2,1)S(1)} %collective-permute-done.23.p3) | copy-start | bytes 73732
  94.5 1.2 copy-start.15
  95.7 0.6 copy-start.16
  98.8 1.4 collective-permute-start.24
  101.1 3.0 %collective-permute-start.27 = (bf16[48,512]{1,0:T(8,128)(2,1)S(1)}, bf16[48,512]{1,0:T(8,128)(2,1)S(1)}, u32[]{:S(2)}, u32[]{:S(2)}) collective-permute-start(bf16[48,512]{1,0:T(8,128)(2,1)S(1)} %add_convert_fusion.2), channel_id=1, source_target_pairs={{0,6},{1,7},{2,0},{3,1},{4,2},{5,3},{6,4},{7,5},{8,14},{9,15},{10,... | collective-permute-start | bytes 147464 | tf_op jit(solution)/shard_map/ppermute | solution.py:360
  101.5 4.2 %collective-permute-start.26 = (bf16[48,512]{1,0:T(8,128)(2,1)S(1)}, bf16[48,512]{1,0:T(8,128)(2,1)S(1)}, u32[]{:S(2)}, u32[]{:S(2)}) collective-permute-start(bf16[48,512]{1,0:T(8,128)(2,1)S(1)} %add_convert_fusion.2), channel_id=1, source_target_pairs={{0,2},{1,3},{2,4},{3,5},{4,6},{5,7},{6,0},{7,1},{8,10},{9,11},{10,... | collective-permute-start | bytes 147464 | tf_op jit(solution)/shard_map/ppermute | solution.py:360
  102.6 4.5 %collective-permute-start.25 = (bf16[48,512]{1,0:T(8,128)(2,1)S(1)}, bf16[48,512]{1,0:T(8,128)(2,1)S(1)}, u32[]{:S(2)}, u32[]{:S(2)}) collective-permute-start(bf16[48,512]{1,0:T(8,128)(2,1)S(1)} %add_convert_fusion.2), channel_id=1, source_target_pairs={{0,4},{1,5},{2,6},{3,7},{4,0},{5,1},{6,2},{7,3},{8,12},{9,13},{10,... | collective-permute-start | bytes 147464 | tf_op jit(solution)/shard_map/ppermute | solution.py:360
  102.8 12.8 %collective-permute-start.15 = (bf16[4,2,128,128]{3,2,1,0:T(8,128)(2,1)S(1)}, bf16[4,2,128,128]{3,2,1,0:T(8,128)(2,1)S(1)}, u32[]{:S(2)}, u32[]{:S(2)}) collective-permute-start(bf16[4,2,128,128]{3,2,1,0:T(8,128)(2,1)S(1)} %get-tuple-element.75), channel_id=1, source_target_pairs={{0,16},{16,32},{32,48},{48,0},{64,80},{80,96},{96,112},{112,64},{1... | collective-permute-start | bytes 786440 | tf_op jit(solution)/shard_map/ppermute | solution.py:351
  102.8 31.5 %collective-permute-start.12 = (bf16[2,128,640]{2,1,0:T(8,128)(2,1)S(1)}, bf16[2,128,640]{2,1,0:T(8,128)(2,1)S(1)}, u32[]{:S(2)}, u32[]{:S(2)}) collective-permute-start(bf16[2,128,640]{2,1,0:T(8,128)(2,1)S(1)} %get-tuple-element.71), channel_id=1, source_target_pairs={{0,64},{16,80},{32,96},{48,112},{64,128},{80,144},{96,160},{112,17... | collective-permute-start | bytes 983048 | tf_op jit(solution)/shard_map/ppermute | solution.py:346
  104.1 30.2 %collective-permute-start.13 = (bf16[2,128,640]{2,1,0:T(8,128)(2,1)S(1)}, bf16[2,128,640]{2,1,0:T(8,128)(2,1)S(1)}, u32[]{:S(2)}, u32[]{:S(2)}) collective-permute-start(bf16[2,128,640]{2,1,0:T(8,128)(2,1)S(1)} %get-tuple-element.72), channel_id=1, source_target_pairs={{0,128},{16,144},{32,160},{48,176},{64,192},{80,208},{96,224},{112... | collective-permute-start | bytes 983048 | tf_op jit(solution)/shard_map/ppermute | solution.py:346
  105.7 28.6 %collective-permute-start.14 = (bf16[2,128,640]{2,1,0:T(8,128)(2,1)S(1)}, bf16[2,128,640]{2,1,0:T(8,128)(2,1)S(1)}, u32[]{:S(2)}, u32[]{:S(2)}) collective-permute-start(bf16[2,128,640]{2,1,0:T(8,128)(2,1)S(1)} %get-tuple-element.73), channel_id=1, source_target_pairs={{0,192},{16,208},{32,224},{48,240},{64,0},{80,16},{96,32},{112,48}... | collective-permute-start | bytes 983048 | tf_op jit(solution)/shard_map/ppermute | solution.py:346
  107.1 10.5 %collective-permute-start.28 = (bf16[48,512]{1,0:T(8,128)(2,1)S(1)}, bf16[48,512]{1,0:T(8,128)(2,1)S(1)}, u32[]{:S(2)}, u32[]{:S(2)}) collective-permute-start(bf16[48,512]{1,0:T(8,128)(2,1)S(1)} %add_convert_fusion.1), channel_id=1, source_target_pairs={{0,8},{1,9},{2,10},{3,11},{4,12},{5,13},{6,14},{7,15},{8,0},{9,1},... | collective-permute-start | bytes 147464 | tf_op jit(solution)/shard_map/ppermute | solution.py:364
  115.6 18.8 %copy-start.8 = (bf16[4,2,128,128]{3,2,1,0:T(8,128)(2,1)}, bf16[4,2,128,128]{3,2,1,0:T(8,128)(2,1)S(1)}, u32[]{:S(2)}) copy-start(bf16[4,2,128,128]{3,2,1,0:T(8,128)(2,1)S(1)} %collective-permute-done.15.r1) | copy-start | bytes 786436
  115.6 16.0 %collective-permute-start.16 = (bf16[4,2,128,128]{3,2,1,0:T(8,128)(2,1)S(1)}, bf16[4,2,128,128]{3,2,1,0:T(8,128)(2,1)S(1)}, u32[]{:S(2)}, u32[]{:S(2)}) collective-permute-start(bf16[4,2,128,128]{3,2,1,0:T(8,128)(2,1)S(1)} %get-tuple-element.76), channel_id=1, source_target_pairs={{0,32},{16,48},{32,0},{48,16},{64,96},{80,112},{96,64},{112,80},{1... | collective-permute-start | bytes 786440 | tf_op jit(solution)/shard_map/ppermute | solution.py:351
  117.7 16.6 %collective-permute-start.17 = (bf16[4,2,128,128]{3,2,1,0:T(8,128)(2,1)S(1)}, bf16[4,2,128,128]{3,2,1,0:T(8,128)(2,1)S(1)}, u32[]{:S(2)}, u32[]{:S(2)}) collective-permute-start(bf16[4,2,128,128]{3,2,1,0:T(8,128)(2,1)S(1)} %get-tuple-element.77), channel_id=1, source_target_pairs={{0,48},{16,0},{32,16},{48,32},{64,112},{80,64},{96,80},{112,96},{1... | collective-permute-start | bytes 786440 | tf_op jit(solution)/shard_map/ppermute | solution.py:351
  131.6 2.7 %copy-start.9 = (bf16[4,2,128,128]{3,2,1,0:T(8,128)(2,1)}, bf16[4,2,128,128]{3,2,1,0:T(8,128)(2,1)S(1)}, u32[]{:S(2)}) copy-start(bf16[4,2,128,128]{3,2,1,0:T(8,128)(2,1)S(1)} %collective-permute-done.16.r2) | copy-start | bytes 786436
  131.6 15.8 %collective-permute-start.29 = (f32[48,512]{1,0:T(8,128)S(1)}, f32[48,512]{1,0:T(8,128)S(1)}, u32[]{:S(2)}, u32[]{:S(2)}) collective-permute-start(f32[48,512]{1,0:T(8,128)S(1)} %convert_add_fusion), channel_id=1, source_target_pairs={{0,1},{1,0},{2,3},{3,2},{4,5},{5,4},{6,7},{7,6},{8,9},{9,8},{10,11... | collective-permute-start | bytes 294920 | tf_op jit(solution)/shard_map/ppermute | solution.py:355
  134.3 0.7 copy-start.10
  134.3 0.8 copy-start.5
  134.3 0.9 copy-start.6
  135.3 0.7 copy-start.7
  138.8 5.2 %collective-permute-start.18 = (bf16[2,128,128]{2,1,0:T(8,128)(2,1)}, bf16[2,128,128]{2,1,0:T(8,128)(2,1)S(1)}, u32[]{:S(2)}, u32[]{:S(2)}) collective-permute-start(bf16[2,128,128]{2,1,0:T(8,128)(2,1)} %get-tuple-element.81), channel_id=1, source_target_pairs={{0,64},{16,80},{32,96},{48,112},{64,128},{80,144},{96,160},{112,17... | collective-permute-start | bytes 196616 | tf_op jit(solution)/shard_map/ppermute | solution.py:346
  138.9 5.3 %collective-permute-start.19 = (bf16[2,128,128]{2,1,0:T(8,128)(2,1)}, bf16[2,128,128]{2,1,0:T(8,128)(2,1)S(1)}, u32[]{:S(2)}, u32[]{:S(2)}) collective-permute-start(bf16[2,128,128]{2,1,0:T(8,128)(2,1)} %get-tuple-element.82), channel_id=1, source_target_pairs={{0,128},{16,144},{32,160},{48,176},{64,192},{80,208},{96,224},{112... | collective-permute-start | bytes 196616 | tf_op jit(solution)/shard_map/ppermute | solution.py:346
  141.0 4.0 %collective-permute-start.20 = (bf16[2,128,128]{2,1,0:T(8,128)(2,1)}, bf16[2,128,128]{2,1,0:T(8,128)(2,1)S(1)}, u32[]{:S(2)}, u32[]{:S(2)}) collective-permute-start(bf16[2,128,128]{2,1,0:T(8,128)(2,1)} %get-tuple-element.83), channel_id=1, source_target_pairs={{0,192},{16,208},{32,224},{48,240},{64,0},{80,16},{96,32},{112,48}... | collective-permute-start | bytes 196616 | tf_op jit(solution)/shard_map/ppermute | solution.py:346
  144.0 1.0 copy-start.11
  144.2 0.8 copy-start.12
  145.0 0.6 copy-start.13
where the time goes:
time: 150 us; the launch traced here: 148 us
  waiting for transfers between devices  54 us (36%)
  starting transfers between devices  41.7 us (28%)
  Pallas kernels  41.1 us (27%)
  local copies, waits for them, and re-layouts  5.59 us (4%)
  other arithmetic  4.74 us (3%)
    ppermute x9, waiting for transfers between devices, z_shift(): return lax.ppermute(a, 'prefix', pairs)  27.5 us
    ppermute x15, waiting for transfers between devices, y_shift(): return lax.ppermute(a, 'prefix', pairs)  21.5 us
    pallas_call x1, Pallas kernels, forward(): pl.pallas_call(forward_kernel, out_shape=[shaped((NY, 2, PROMPT_ROWS, HD)...  19.4 us
    pallas_call x1, Pallas kernels, backward(): pl.pallas_call(backward_kernel, out_shape=[shaped((2, BLOCK, HEADS * HD),...  15.6 us
    ppermute x9, starting transfers between devices, z_shift(): return lax.ppermute(a, 'prefix', pairs)  15.6 us
    ppermute x15, starting transfers between devices, y_shift(): return lax.ppermute(a, 'prefix', pairs)  15.3 us
    ppermute x1, starting transfers between devices, far_swap(): return lax.ppermute(a, 'resp', [(i, i ^ 8) for i in range(16)])  8.43 us
    unnamed x36, local copies, waits for them, and re-layouts  4.34 us
  transfers between devices with their start and end apart: 30, of which 18 were waited for; matrix products, arithmetic and copies ran while one was open for 1% of the time, Pallas kernels for 14%

commit v1 on v0

--- a/solution.py
+++ b/solution.py
@@ -28,6 +28,7 @@
 PROMPT_CHUNKS = PROMPT // CHUNK
 TILES = ROWS // TILE
 RESP = KEYS - PROMPT
+GROUP = HEADS * BLOCK
 VMEM = pl.BlockSpec(memory_space=pltpu.VMEM)
 SMEM = pl.BlockSpec(memory_space=pltpu.SMEM)
 
@@ -38,6 +39,10 @@
 
 def aligned(start, size):
     return pl.ds(pl.multiple_of(start, size), size)
+
+
+def head_rows(block):
+    return aligned(lax.rem(block, NY) * GROUP, GROUP)
 
 
 def tile_positions(tile, z):
@@ -76,7 +81,7 @@
     x0, x1, x2, x3,
     kv0, kv1, kv2, kv3,
     r0, r1, r2, r3,
-    os, qs, gs, ks, vs, kt, tops, deltas, dq_part,
+    a1, a3, os, qs, gs, ks, vs, kt, tops, deltas, dq_part,
     kp, vp, kpt, vpt, vt, sc, pm, dk, dv,
 ):
     y = info[0]
@@ -168,6 +173,8 @@
             os[at, :] = jnp.zeros((TILE, HD), BF16)
 
     over_tiles(tile_step)
+    a1[...] = os[head_rows(y + 1), :]
+    a3[...] = os[head_rows(y + 3), :]
     for s, r in enumerate((r0, r1, r2, r3)):
         zp = lax.rem(z + s, NZ)
         for b in range(NY):
@@ -180,6 +187,7 @@
     return pl.pallas_call(
         forward_kernel,
         out_shape=[shaped((NY, 2, PROMPT_ROWS, HD), BF16)] * 4
+        + [shaped((GROUP, HD), BF16)] * 2
         + [
             shaped((ROWS, HD), BF16),
             shaped((ROWS, HD), BF16),
@@ -192,7 +200,7 @@
             shaped((TILES * HD, TILE), F32),
         ],
         in_specs=[SMEM] + [VMEM] * 8,
-        out_specs=[VMEM] * 13,
+        out_specs=[VMEM] * 15,
         scratch_shapes=[
             pltpu.VMEM((PROMPT, HD), BF16),
             pltpu.VMEM((PROMPT, HD), BF16),
@@ -256,13 +264,11 @@
             dq[at, :] = jnp.zeros((TILE, HD), BF16)
 
     over_tiles(tile_step)
-    for s, d in enumerate((d0, d1, d2, d3)):
-        block = lax.rem(y + s, NY)
-        for j in range(HEADS):
-            at = aligned((block * HEADS + j) * BLOCK, BLOCK)
-            cols = slice(j * HD, (j + 1) * HD)
-            d[0, :, cols] = os[at, :]
-            d[1, :, cols] = dq[at, :]
+    for s, d in ((0, d0), (2, d2)):
+        d[:GROUP, :] = os[head_rows(y + s), :]
+        d[GROUP:, :] = dq[head_rows(y + s), :]
+    d1[...] = dq[head_rows(y + 1), :]
+    d3[...] = dq[head_rows(y + 3), :]
     for s, r in enumerate((r0, r1, r2, r3)):
         zp = lax.rem(z + s, NZ)
         for b in range(NY):
@@ -274,7 +280,7 @@
 def backward(info, state):
     return pl.pallas_call(
         backward_kernel,
-        out_shape=[shaped((2, BLOCK, HEADS * HD), BF16)] * 4
+        out_shape=[shaped((rows, HD), BF16) for rows in (2 * GROUP, GROUP, 2 * GROUP, GROUP)]
         + [shaped((NY, 2, BLOCK, HD), BF16)] * 4,
         in_specs=[SMEM] + [VMEM] * 9,
         out_specs=[VMEM] * 8,
@@ -291,54 +297,63 @@
     )(info, *state)
 
 
+def lay_heads(y, pieces, out):
+    for s, (piece, first) in enumerate(pieces):
+        block = lax.rem(y - s + NY, NY)
+        for j in range(HEADS):
+            at = aligned((block * HEADS + j) * HD, HD)
+            out[:, at] = piece[first + j * BLOCK : first + (j + 1) * BLOCK, :]
+
+
 def settle_kernel(
-    info,
-    d0, d1, d2, d3,
-    r0, r1, r2, r3,
-    a, d, p0, p1, p2, p3,
+    info, d0, d1, d2, d3, a1, a3, r0, r1, r2, r3, prompt, a, p0, p1, p2, p3
 ):
     y = info[0]
-    width = HEADS * HD
-    for s, rows in enumerate((d0, d1, d2, d3)):
-        at = aligned(lax.rem(y - s + NY, NY) * width, width)
-        a[:, at] = rows[0]
-        d[:, at] = rows[1]
+    lay_heads(y, ((d0, 0), (a1, 0), (d2, 0), (a3, 0)), a)
     for s, p in enumerate((p0, p1, p2, p3)):
         b = lax.rem(y + s, NY)
-        p[...] = (
-            (r0[b].astype(F32) + r1[b].astype(F32)) + (r2[b].astype(F32) + r3[b].astype(F32))
-        ).astype(BF16)
-
-
-def settle(info, rows, terms):
-    out = shaped((BLOCK, NY * HEADS * HD), BF16)
+        for i in range(2):
+            p[i * PIECE : i * PIECE + PROMPT_ROWS, :] = prompt[b, i].astype(BF16)
+            p[i * PIECE + PROMPT_ROWS : (i + 1) * PIECE, :] = (
+                (r0[b, i].astype(F32) + r1[b, i].astype(F32))
+                + (r2[b, i].astype(F32) + r3[b, i].astype(F32))
+            ).astype(BF16)
+    p1[2 * PIECE :, :] = d1[...]
+    p3[2 * PIECE :, :] = d3[...]
+
+
+def settle(info, rows, att, terms, prompt):
     return pl.pallas_call(
         settle_kernel,
-        out_shape=[out, out] + [shaped((2, BLOCK, HD), BF16)] * 4,
-        in_specs=[SMEM] + [VMEM] * 8,
-        out_specs=[VMEM] * 6,
+        out_shape=[shaped((BLOCK, NY * HEADS * HD), BF16)]
+        + [shaped((2 * PIECE + s % 2 * GROUP, HD), BF16) for s in range(NY)],
+        in_specs=[SMEM] + [VMEM] * 11,
+        out_specs=[VMEM] * 5,
         name="settle",
-    )(info, *rows, *terms)
-
-
-def place_kernel(info, p0, p1, p2, p3, dk, dv):
+    )(info, *rows, *att, *terms, prompt)
+
+
+def place_kernel(info, d0, d2, p0, p1, p2, p3, d, dk, dv, pk, pv):
     y = info[0]
+    lay_heads(y, ((d0, GROUP), (p1, 2 * PIECE), (d2, GROUP), (p3, 2 * PIECE)), d)
     for s, p in enumerate((p0, p1, p2, p3)):
         at = aligned(lax.rem(y - s + NY, NY) * HD, HD)
-        dk[:, at] = p[0].astype(F32)
-        dv[:, at] = p[1].astype(F32)
-
-
-def place(info, pieces):
-    rows = pieces[0].shape[1]
-    out = shaped((rows, NY * HD), F32)
+        pk[:, at] = p[:PROMPT_ROWS, :].astype(F32)
+        dk[:, at] = p[PROMPT_ROWS:PIECE, :].astype(F32)
+        pv[:, at] = p[PIECE : PIECE + PROMPT_ROWS, :].astype(F32)
+        dv[:, at] = p[PIECE + PROMPT_ROWS : 2 * PIECE, :].astype(F32)
+
+
+def place(info, rows, pieces):
+    out = shaped((BLOCK, NY * HD), F32)
+    prompt_out = shaped((PROMPT_ROWS, NY * HD), F32)
     return pl.pallas_call(
         place_kernel,
-        out_shape=[out, out],
-        in_specs=[SMEM] + [VMEM] * 4,
-        out_specs=[VMEM] * 2,
+        out_shape=[shaped((BLOCK, NY * HEADS * HD), BF16), out, out, prompt_out, prompt_out],
+        in_specs=[SMEM] + [VMEM] * 6,
+        out_specs=[VMEM] * 5,
         name="place",
-    )(info, *pieces)
+    )(info, *rows, *pieces)
 
 
 def y_shift(a, s):
@@ -355,23 +370,24 @@
     return lax.ppermute(a, "resp", [(i, i ^ 1) for i in range(16)])
 
 
-def x_shift(a, s):
-    pairs = [(h * 8 + x * 2 + c, h * 8 + (x + s) % 4 * 2 + c) for h in range(2) for x in range(4) for c in range(2)]
-    return lax.ppermute(a, "resp", pairs)
+def x_swap(a, bit):
+    return lax.ppermute(a, "resp", [(i, i ^ (2 * bit)) for i in range(16)])
 
 
 def far_swap(a):
     return lax.ppermute(a, "resp", [(i, i ^ 8) for i in range(16)])
 
 
-def over_responses(dk, dv):
+def over_responses(terms):
     core = lax.axis_index("resp") % 2
-    half = (jnp.where(core == 0, dk, dv) + core_swap(jnp.where(core == 0, dv, dk))).astype(BF16)
-    near, across, back = (x_shift(half, s).astype(F32) for s in (1, 2, 3))
-    low = ((half.astype(F32) + across) + (near + back)).astype(BF16)
-    half = low.astype(F32) + far_swap(low).astype(F32)
-    other = core_swap(half)
-    return jnp.where(core == 0, half, other), jnp.where(core == 0, other, half)
+    dk, dv = terms[0], terms[1]
+    half = jnp.where(core == 0, dk, dv) + core_swap(jnp.where(core == 0, dv, dk))
+    for swap in (lambda a: x_swap(a, 1), lambda a: x_swap(a, 2), far_swap):
+        low = half.astype(BF16)
+        half = low.astype(F32) + swap(low).astype(F32)
+    other = core_swap(half.astype(BF16)).astype(F32)
+    half = half.astype(BF16).astype(F32)
+    return jnp.stack([jnp.where(core == 0, half, other), jnp.where(core == 0, other, half)])
 
 
 def by_y(pieces):
@@ -417,19 +433,24 @@
     keyvals = by_z([keyvals] * NZ)
     rows = by_y(split(jnp.stack([queries, grads]), HEADS * HD))
 
-    *prompt_terms, os, qs, gs, ks, vs, kt, tops, deltas, dq_part = forward(info, rows, keyvals)
-    prompt_terms = by_z(prompt_terms)
-    back = backward(info, (os, qs, gs, ks, vs, kt, tops, deltas, dq_part))
-    *prompt_terms, rows_first, back_first = lax.optimization_barrier(
-        (*prompt_terms, back[0], back[4])
-    )
-    rows = by_y([rows_first, *back[1:4]])
-    terms = by_z([back_first, *back[5:]])
-    prompt = sum(t.astype(F32) for t in prompt_terms).astype(BF16)
-    prompt = by_y([pick(prompt, (y + s) % NY, 0, keepdims=False) for s in range(NY)])
-    prompt_key_grad, prompt_value_grad = over_responses(*place(info, prompt))
-    attention_out, query_grad, *pieces = settle(info, rows, terms)
-    key_own, value_own = place(info, by_y(pieces))
+    results = forward(info, rows, keyvals)
+    prompt_terms = by_z(results[:4])
+    att = [y_shift(results[4], 1), y_shift(results[5], 3)]
+    d0, d1, d2, d3, *terms = backward(info, results[6:])
+    *prompt_terms, att[0], att[1], d2, terms[1], terms[2], terms[3] = lax.optimization_barrier(
+        (*prompt_terms, *att, d2, terms[1], terms[2], terms[3])
+    )
+    prompt = sum(t.astype(F32) for t in prompt_terms)
+    prompt = prompt.transpose(1, 0, 2, 3).reshape(2, NY * PROMPT_ROWS, HD)
+    once = jnp.minimum(lengths[0], 1)
+    terms = by_z(terms)
+    d2 = y_shift(d2, 2)
+    prompt = lax.fori_loop(0, once, lambda i, terms: over_responses(terms), prompt)
+    prompt = prompt.reshape(2, NY, PROMPT_ROWS, HD).transpose(1, 0, 2, 3)
+    attention_out, *pieces = settle(info, (d0, d1, d2, d3), att, terms, prompt)
+    query_grad, key_own, value_own, prompt_key_grad, prompt_value_grad = place(
+        info, (d0, d2), by_y(pieces)
+    )
     return (
         attention_out[None],
         query_grad[None],

time: 150 us -> 138 us (0.920); the launches traced: 148 us -> 138 us
  starting transfers between devices: 41.7 us -> 57.9 us
  waiting for transfers between devices: 54 us -> 38.6 us
  Pallas kernels: 41.1 us -> 32 us
  other arithmetic: 4.74 us -> 2.28 us
    ppermute x2, starting transfers between devices: 0.68 us -> 20.1 us  [core_swap(): return lax.ppermute(a, 'resp', [(i, i ^ 1) for i in range(16)])]
    ppermute x9, waiting for transfers between devices: 27.5 us -> 10.6 us  [z_shift(): return lax.ppermute(a, 'prefix', pairs)]
    pallas_call x4 -> x3, Pallas kernels: 21.7 us -> 16.9 us  [the longest x1 11.3 us: backward(): pl.pallas_call(backward_kernel, out_shape=[shaped((rows, HD), BF16) for r...]
    pallas_call x1, Pallas kernels: 19.4 us -> 15.1 us  [forward(): pl.pallas_call(forward_kernel, out_shape=[shaped((NY, 2, PROMPT_ROWS, HD)...]
    ppermute x3 -> x2, waiting for transfers between devices: 2 us -> 5.76 us  [x_swap(): return lax.ppermute(a, 'resp', [(i, i ^ 2 * bit) for i in range(16)])]
    ppermute x1, starting transfers between devices: 8.43 us -> 5.56 us  [far_swap(): return lax.ppermute(a, 'resp', [(i, i ^ 8) for i in range(16)])]
    ppermute x15 -> x12, waiting for transfers between devices: 21.5 us -> 18.9 us  [y_shift(): return lax.ppermute(a, 'prefix', pairs)]
    ppermute x9, starting transfers between devices: 15.6 us -> 13.3 us  [z_shift(): return lax.ppermute(a, 'prefix', pairs)]
  transfers between devices with their start and end apart: 30 -> 26, of which waited for: 18 -> 10; matrix products, arithmetic and copies ran while one was open for 1% -> 2% of each run, Pallas kernels for 14% -> 8%
where the time goes in v1:
time: 138 us
  starting transfers between devices  57.9 us (42%)
  waiting for transfers between devices  38.6 us (28%)
  Pallas kernels  32 us (23%)
  local copies, waits for them, and re-layouts  5.83 us (4%)
  other arithmetic  2.28 us (2%)
  between operations  1.65 us (1%)
    ppermute x2, starting transfers between devices, core_swap(): return lax.ppermute(a, 'resp', [(i, i ^ 1) for i in range(16)])  20.1 us
    ppermute x12, waiting for transfers between devices, y_shift(): return lax.ppermute(a, 'prefix', pairs)  18.9 us
    ppermute x12, starting transfers between devices, y_shift(): return lax.ppermute(a, 'prefix', pairs)  16.9 us
    pallas_call x1, Pallas kernels, forward(): pl.pallas_call(forward_kernel, out_shape=[shaped((NY, 2, PROMPT_ROWS, HD)...  15.1 us
    ppermute x9, starting transfers between devices, z_shift(): return lax.ppermute(a, 'prefix', pairs)  13.3 us
    pallas_call x1, Pallas kernels, backward(): pl.pallas_call(backward_kernel, out_shape=[shaped((rows, HD), BF16) for r...  11.3 us
    ppermute x9, waiting for transfers between devices, z_shift(): return lax.ppermute(a, 'prefix', pairs)  10.6 us
    ppermute x2, waiting for transfers between devices, x_swap(): return lax.ppermute(a, 'resp', [(i, i ^ 2 * bit) for i in range(16)])  5.76 us
  transfers between devices with their start and end apart: 26, of which 10 were waited for; matrix products, arithmetic and copies ran while one was open for 2% of the time, Pallas kernels for 8%

profile of v1, /device:TPU:1, one launch (start us, length us, event | category | flops | bytes accessed | tf_op | source)
XLA Modules:
  0.0 138.3 jit_solution(16674382247931564974)
XLA Ops:
  0.8 1.1 maximum_bitcast_fusion
  1.9 2.2 %collective-permute-start.5 = (bf16[2,176,128]{2,1,0:T(8,128)(2,1)S(1)}, bf16[2,176,128]{2,1,0:T(8,128)(2,1)S(1)}, u32[]{:S(2)}, u32[]{:S(2)}) collective-permute-start(bf16[2,176,128]{2,1,0:T(8,128)(2,1)S(1)} %get-tuple-element.168), channel_id=1, source_target_pairs={{0,64},{16,80},{32,96},{48,112},{64,128},{80,144},{96,160},{112,17... | collective-permute-start | bytes 270344 | tf_op jit(solution)/shard_map/ppermute | solution.py:361
  4.1 2.6 %collective-permute-start.6 = (bf16[2,176,128]{2,1,0:T(8,128)(2,1)S(1)}, bf16[2,176,128]{2,1,0:T(8,128)(2,1)S(1)}, u32[]{:S(2)}, u32[]{:S(2)}) collective-permute-start(bf16[2,176,128]{2,1,0:T(8,128)(2,1)S(1)} %get-tuple-element.169), channel_id=1, source_target_pairs={{0,128},{16,144},{32,160},{48,176},{64,192},{80,208},{96,224},{112... | collective-permute-start | bytes 270344 | tf_op jit(solution)/shard_map/ppermute | solution.py:361
  6.8 1.1 collective-permute-start.7
  7.8 2.6 %collective-permute-done.6 = bf16[2,176,128]{2,1,0:T(8,128)(2,1)S(1)} collective-permute-done((bf16[2,176,128]{2,1,0:T(8,128)(2,1)S(1)}, bf16[2,176,128]{2,1,0:T(8,128)(2,1)S(1)}, u32[]{:S(2)}, u32[]{:S(2)}) %collective-permute-start.6) | collective-permute-done | bytes 90144 | tf_op jit(solution)/shard_map/ppermute | solution.py:361
  10.4 0.1 fusion.3
  10.6 2.1 %collective-permute-start.10 = (bf16[2,128,640]{2,1,0:T(8,128)(2,1)S(1)}, bf16[2,128,640]{2,1,0:T(8,128)(2,1)S(1)}, u32[]{:S(2)}, u32[]{:S(2)}) collective-permute-start(bf16[2,128,640]{2,1,0:T(8,128)(2,1)S(1)} %get-tuple-element.158), channel_id=1, source_target_pairs={{0,192},{16,208},{32,224},{48,240},{64,0},{80,16},{96,32},{112,48}... | collective-permute-start | bytes 983048 | tf_op jit(solution)/shard_map/ppermute | solution.py:361
  12.8 2.1 %collective-permute-start.11 = (bf16[4,2,176,128]{3,2,1,0:T(8,128)(2,1)S(1)}, bf16[4,2,176,128]{3,2,1,0:T(8,128)(2,1)S(1)}, u32[]{:S(2)}, u32[]{:S(2)}) collective-permute-start(bf16[4,2,176,128]{3,2,1,0:T(8,128)(2,1)S(1)} %pad_maximum_fusion.2.kv0), channel_id=1, source_target_pairs={{0,16},{16,32},{32,48},{48,0},{64,80},{80,96},{96,112},{112,64},{1... | collective-permute-start | bytes 1081352 | tf_op jit(solution)/shard_map/ppermute | solution.py:366
  14.9 3.0 %collective-permute-start.12 = (bf16[4,2,176,128]{3,2,1,0:T(8,128)(2,1)S(1)}, bf16[4,2,176,128]{3,2,1,0:T(8,128)(2,1)S(1)}, u32[]{:S(2)}, u32[]{:S(2)}) collective-permute-start(bf16[4,2,176,128]{3,2,1,0:T(8,128)(2,1)S(1)} %pad_maximum_fusion.2.kv0), channel_id=1, source_target_pairs={{0,32},{16,48},{32,0},{48,16},{64,96},{80,112},{96,64},{112,80},{1... | collective-permute-start | bytes 1081352 | tf_op jit(solution)/shard_map/ppermute | solution.py:366
  17.9 0.7 collective-permute-start.13
  18.6 1.5 %collective-permute-start.9 = (bf16[2,128,640]{2,1,0:T(8,128)(2,1)S(1)}, bf16[2,128,640]{2,1,0:T(8,128)(2,1)S(1)}, u32[]{:S(2)}, u32[]{:S(2)}) collective-permute-start(bf16[2,128,640]{2,1,0:T(8,128)(2,1)S(1)} %get-tuple-element.161), channel_id=1, source_target_pairs={{0,128},{16,144},{32,160},{48,176},{64,192},{80,208},{96,224},{112... | collective-permute-start | bytes 983048 | tf_op jit(solution)/shard_map/ppermute | solution.py:361
  20.1 0.6 fusion.11
  21.3 0.7 pad_add_fusion.info
  22.0 6.5 %collective-permute-done.8.x1 = bf16[2,128,640]{2,1,0:T(8,128)(2,1)S(1)} collective-permute-done((bf16[2,128,640]{2,1,0:T(8,128)(2,1)S(1)}, bf16[2,128,640]{2,1,0:T(8,128)(2,1)S(1)}, u32[]{:S(2)}, u32[]{:S(2)}) %collective-permute-start.8) | collective-permute-done | bytes 327712 | tf_op jit(solution)/shard_map/ppermute | solution.py:361
  28.5 2.9 %collective-permute-done.9.x2 = bf16[2,128,640]{2,1,0:T(8,128)(2,1)S(1)} collective-permute-done((bf16[2,128,640]{2,1,0:T(8,128)(2,1)S(1)}, bf16[2,128,640]{2,1,0:T(8,128)(2,1)S(1)}, u32[]{:S(2)}, u32[]{:S(2)}) %collective-permute-start.9) | collective-permute-done | bytes 327712 | tf_op jit(solution)/shard_map/ppermute | solution.py:361
  31.4 10.5 %collective-permute-done.12.kv2 = bf16[4,2,176,128]{3,2,1,0:T(8,128)(2,1)S(1)} collective-permute-done((bf16[4,2,176,128]{3,2,1,0:T(8,128)(2,1)S(1)}, bf16[4,2,176,128]{3,2,1,0:T(8,128)(2,1)S(1)}, u32[]{:S(2)}, u32[]{:S(2)}) %collective-permute-start.12) | collective-permute-done | bytes 360480 | tf_op jit(solution)/shard_map/ppermute | solution.py:366
  41.9 15.1 %forward.1 = (bf16[4,2,48,128]{3,2,1,0:T(8,128)(2,1)S(1)}, bf16[4,2,48,128]{3,2,1,0:T(8,128)(2,1)S(1)}, bf16[4,2,48,128]{3,2,1,0:T(8,128)(2,1)S(1)}, bf16[4,2,48...) custom-call(s32[3]{0:T(128)S(1)} %pad_add_fusion.info, ...), custom_call_target="tpu_custom_call" | custom-call | flops 16000000000 | bytes 8388608 | tf_op jit(solution)/shard_map/forward/pallas_call | solution.py:187
  57.1 2.7 %collective-permute-start.18 = (bf16[640,128]{1,0:T(8,128)(2,1)S(1)}, bf16[640,128]{1,0:T(8,128)(2,1)S(1)}, u32[]{:S(2)}, u32[]{:S(2)}) collective-permute-start(bf16[640,128]{1,0:T(8,128)(2,1)S(1)} %get-tuple-element.122), channel_id=1, source_target_pairs={{0,192},{16,208},{32,224},{48,240},{64,0},{80,16},{96,32},{112,48}... | collective-permute-start | bytes 491528 | tf_op jit(solution)/shard_map/ppermute | solution.py:361
  59.8 2.1 %collective-permute-start.14 = (bf16[4,2,48,128]{3,2,1,0:T(8,128)(2,1)S(1)}, bf16[4,2,48,128]{3,2,1,0:T(8,128)(2,1)S(1)}, u32[]{:S(2)}, u32[]{:S(2)}) collective-permute-start(bf16[4,2,48,128]{3,2,1,0:T(8,128)(2,1)S(1)} %get-tuple-element.118), channel_id=1, source_target_pairs={{0,16},{16,32},{32,48},{48,0},{64,80},{80,96},{96,112},{112,64},{1... | collective-permute-start | bytes 294920 | tf_op jit(solution)/shard_map/ppermute | solution.py:366
  61.8 2.1 %collective-permute-start.16 = (bf16[4,2,48,128]{3,2,1,0:T(8,128)(2,1)S(1)}, bf16[4,2,48,128]{3,2,1,0:T(8,128)(2,1)S(1)}, u32[]{:S(2)}, u32[]{:S(2)}) collective-permute-start(bf16[4,2,48,128]{3,2,1,0:T(8,128)(2,1)S(1)} %get-tuple-element.120), channel_id=1, source_target_pairs={{0,48},{16,0},{32,16},{48,32},{64,112},{80,64},{96,80},{112,96},{1... | collective-permute-start | bytes 294920 | tf_op jit(solution)/shard_map/ppermute | solution.py:366
  63.9 11.3 %backward.1 = (bf16[1280,128]{1,0:T(8,128)(2,1)S(1)}, bf16[640,128]{1,0:T(8,128)(2,1)S(1)}, bf16[1280,128]{1,0:T(8,128)(2,1)S(1)}, bf16[640,128]{1,0:T(8,128)(2,...) custom-call(s32[3]{0:T(128)S(1)} %pad_add_fusion.info, ...), custom_call_target="tpu_custom_call" | custom-call | flops 16000000000 | bytes 8388608 | tf_op jit(solution)/shard_map/backward/pallas_call | solution.py:281
  75.3 0.7 copy-done
  76.0 0.7 copy-done.1
  76.7 0.7 copy-done.2
  77.3 0.7 copy-done.3
  78.3 0.1 collective-permute-start.21
  78.4 3.2 %collective-permute-start.22 = (bf16[4,2,128,128]{3,2,1,0:T(8,128)(2,1)S(1)}, bf16[4,2,128,128]{3,2,1,0:T(8,128)(2,1)S(1)}, u32[]{:S(2)}, u32[]{:S(2)}) collective-permute-start(bf16[4,2,128,128]{3,2,1,0:T(8,128)(2,1)S(1)} %get-tuple-element.134), channel_id=1, source_target_pairs={{0,48},{16,0},{32,16},{48,32},{64,112},{80,64},{96,80},{112,96},{1... | collective-permute-start | bytes 786440 | tf_op jit(solution)/shard_map/ppermute | solution.py:366
  81.6 37.1 %while.12 = (s32[]{:T(128)}, f32[2,192,128]{2,1,0:T(8,128)S(1)}, s32[]{:T(128)}, s32[]{:T(128)}, u32[]{:T(128)}, /*index=5*/s32[]{:T(128)}, s32[]{:T(128)}) while((s32[]{:T(128)}, f32[2,192,128]{2,1,0:T(8,128)S(1)}, s32[]{:T(128)}, s32[]{:T(128)}, u32[]{:T(128)}, /*index=5*/s32[]{:T(128)}, s32[]{:T(128)}) %tuple.51), condition=%wide.region_1.2_spmd, body=%wide.region_0.1_spmd.sunk | while | flops 540688 | bytes 2949538 | solution.py:448
  81.6 16.6 %collective-permute-start = (f32[192,128]{1,0:T(8,128)S(1)}, f32[192,128]{1,0:T(8,128)S(1)}, u32[]{:S(2)}, u32[]{:S(2)}) collective-permute-start(f32[192,128]{1,0:T(8,128)S(1)} %select_bitcast_fusion.2), channel_id=1, source_target_pairs={{0,1},{1,0},{2,3},{3,2},{4,5},{5,4},{6,7},{7,6},{8,9},{9,8},{10,11... | collective-permute-start | bytes 294920 | tf_op jit(solution)/shard_map/while/body/ppermute | solution.py:370
  98.2 0.9 collective-permute-done
  99.3 3.2 %collective-permute-done.1 = bf16[192,128]{1,0:T(8,128)(2,1)S(1)} collective-permute-done((bf16[192,128]{1,0:T(8,128)(2,1)S(1)}, bf16[192,128]{1,0:T(8,128)(2,1)S(1)}, u32[]{:S(2)}, u32[]{:S(2)}) %collective-permute-start.1) | collective-permute-done | bytes 49184 | tf_op jit(solution)/shard_map/while/body/ppermute | solution.py:374
  102.5 2.0 %collective-permute-start.2 = (bf16[192,128]{1,0:T(8,128)(2,1)S(1)}, bf16[192,128]{1,0:T(8,128)(2,1)S(1)}, u32[]{:S(2)}, u32[]{:S(2)}) collective-permute-start(bf16[192,128]{1,0:T(8,128)(2,1)S(1)} %add_convert_fusion.6), channel_id=1, source_target_pairs={{0,4},{1,5},{2,6},{3,7},{4,0},{5,1},{6,2},{7,3},{8,12},{9,13},{10,... | collective-permute-start | bytes 147464 | tf_op jit(solution)/shard_map/while/body/ppermute | solution.py:374
  104.5 2.5 %collective-permute-done.2 = bf16[192,128]{1,0:T(8,128)(2,1)S(1)} collective-permute-done((bf16[192,128]{1,0:T(8,128)(2,1)S(1)}, bf16[192,128]{1,0:T(8,128)(2,1)S(1)}, u32[]{:S(2)}, u32[]{:S(2)}) %collective-permute-start.2) | collective-permute-done | bytes 49184 | tf_op jit(solution)/shard_map/while/body/ppermute | solution.py:374
  107.1 5.6 %collective-permute-start.3 = (bf16[192,128]{1,0:T(8,128)(2,1)S(1)}, bf16[192,128]{1,0:T(8,128)(2,1)S(1)}, u32[]{:S(2)}, u32[]{:S(2)}) collective-permute-start(bf16[192,128]{1,0:T(8,128)(2,1)S(1)} %add_convert_fusion.7), channel_id=1, source_target_pairs={{0,8},{1,9},{2,10},{3,11},{4,12},{5,13},{6,14},{7,15},{8,0},{9,1},... | collective-permute-start | bytes 147464 | tf_op jit(solution)/shard_map/while/body/ppermute | solution.py:378
  112.6 1.6 %collective-permute-done.3 = bf16[192,128]{1,0:T(8,128)(2,1)S(1)} collective-permute-done((bf16[192,128]{1,0:T(8,128)(2,1)S(1)}, bf16[192,128]{1,0:T(8,128)(2,1)S(1)}, u32[]{:S(2)}, u32[]{:S(2)}) %collective-permute-start.3) | collective-permute-done | bytes 49184 | tf_op jit(solution)/shard_map/while/body/ppermute | solution.py:378
  114.2 3.5 %collective-permute-start.4 = (bf16[192,128]{1,0:T(8,128)(2,1)S(1)}, bf16[192,128]{1,0:T(8,128)(2,1)S(1)}, u32[]{:S(2)}, u32[]{:S(2)}) collective-permute-start(bf16[192,128]{1,0:T(8,128)(2,1)S(1)} %add_convert_fusion.8), channel_id=1, source_target_pairs={{0,1},{1,0},{2,3},{3,2},{4,5},{5,4},{6,7},{7,6},{8,9},{9,8},{10,11... | collective-permute-start | bytes 147464 | tf_op jit(solution)/shard_map/while/body/ppermute | solution.py:370
  117.7 0.9 collective-permute-done.4
  118.7 0.7 copy.16
  119.4 0.6 copy-done.8
  120.2 0.1 copy-done.5
  120.4 3.0 %settle.1 = (bf16[128,2560]{1,0:T(8,128)(2,1)}, bf16[352,128]{1,0:T(8,128)(2,1)}, bf16[992,128]{1,0:T(8,128)(2,1)}, bf16[352,128]{1,0:T(8,128)(2,1)}, bf16[992,128]{1,0:T(8,128)(2,1)}) custom-call(s32[3]{0:T(128)} %copy-done.4, bf16[1280,128]{1,0:T(8,128)(2,1)} %copy-done, bf16[640,128]{1,0:T(8,128)(2,1)} %copy-done.2, bf16[1280,128]{1,0:T(8,128)(2,1)} %copy-done.5, ...), custom_call_target="tpu_custom_call" | custom-call | tf_op jit(solution)/shard_map/settle/pallas_call | solution.py:326
  123.4 0.5 collective-permute-start.23
  123.9 2.2 %collective-permute-start.25 = (bf16[992,128]{1,0:T(8,128)(2,1)}, bf16[992,128]{1,0:T(8,128)(2,1)S(1)}, u32[]{:S(2)}, u32[]{:S(2)}) collective-permute-start(bf16[992,128]{1,0:T(8,128)(2,1)} %get-tuple-element.144), channel_id=1, source_target_pairs={{0,192},{16,208},{32,224},{48,240},{64,0},{80,16},{96,32},{112,48}... | collective-permute-start | bytes 761864 | tf_op jit(solution)/shard_map/ppermute | solution.py:361
  126.0 1.9 %collective-permute-start.24 = (bf16[352,128]{1,0:T(8,128)(2,1)}, bf16[352,128]{1,0:T(8,128)(2,1)S(1)}, u32[]{:S(2)}, u32[]{:S(2)}) collective-permute-start(bf16[352,128]{1,0:T(8,128)(2,1)} %get-tuple-element.143), channel_id=1, source_target_pairs={{0,128},{16,144},{32,160},{48,176},{64,192},{80,208},{96,224},{112... | collective-permute-start | bytes 270344 | tf_op jit(solution)/shard_map/ppermute | solution.py:361
  128.0 6.9 %collective-permute-done.24.p2 = bf16[352,128]{1,0:T(8,128)(2,1)S(1)} collective-permute-done((bf16[352,128]{1,0:T(8,128)(2,1)}, bf16[352,128]{1,0:T(8,128)(2,1)S(1)}, u32[]{:S(2)}, u32[]{:S(2)}) %collective-permute-start.24) | collective-permute-done | bytes 90144 | tf_op jit(solution)/shard_map/ppermute | solution.py:361
  134.9 0.6 copy-done.15
  135.5 0.1 copy-done.11
  135.7 2.6 %place.1 = (bf16[128,2560]{1,0:T(8,128)(2,1)}, f32[128,512]{1,0:T(8,128)}, f32[128,512]{1,0:T(8,128)}, f32[48,512]{1,0:T(8,128)}, f32[48,512]{1,0:T(8,128)}) custom-call(s32[3]{0:T(128)} %copy-done.4, bf16[1280,128]{1,0:T(8,128)(2,1)} %copy-done, bf16[1280,128]{1,0:T(8,128)(2,1)} %copy-done.5, bf16[352,128]{1,0:T(8,128)(2,1)} %get-tuple-element.141.p0, ...), custom_call_target="tpu_custom_call" | custom-call | tf_op jit(solution)/shard_map/place/pallas_call | solution.py:350
  (61 shorter events, 1.1 us)
Async XLA Ops:
  0.6 9.8 %copy-start.6 = (bf16[1,128,2560]{2,1,0:T(8,128)(2,1)S(1)}, bf16[1,128,2560]{2,1,0:T(8,128)(2,1)}, u32[]{:S(2)}) copy-start(bf16[1,128,2560]{2,1,0:T(8,128)(2,1)} %param.9) | copy-start | bytes 1966084
  0.6 9.8 %copy-start.7 = (bf16[1,128,2560]{2,1,0:T(8,128)(2,1)S(1)}, bf16[1,128,2560]{2,1,0:T(8,128)(2,1)}, u32[]{:S(2)}) copy-start(bf16[1,128,2560]{2,1,0:T(8,128)(2,1)} %param.14) | copy-start | bytes 1966084
  1.9 5.9 %collective-permute-start.5 = (bf16[2,176,128]{2,1,0:T(8,128)(2,1)S(1)}, bf16[2,176,128]{2,1,0:T(8,128)(2,1)S(1)}, u32[]{:S(2)}, u32[]{:S(2)}) collective-permute-start(bf16[2,176,128]{2,1,0:T(8,128)(2,1)S(1)} %get-tuple-element.168), channel_id=1, source_target_pairs={{0,64},{16,80},{32,96},{48,112},{64,128},{80,144},{96,160},{112,17... | collective-permute-start | bytes 270344 | tf_op jit(solution)/shard_map/ppermute | solution.py:361
  4.1 6.3 %collective-permute-start.6 = (bf16[2,176,128]{2,1,0:T(8,128)(2,1)S(1)}, bf16[2,176,128]{2,1,0:T(8,128)(2,1)S(1)}, u32[]{:S(2)}, u32[]{:S(2)}) collective-permute-start(bf16[2,176,128]{2,1,0:T(8,128)(2,1)S(1)} %get-tuple-element.169), channel_id=1, source_target_pairs={{0,128},{16,144},{32,160},{48,176},{64,192},{80,208},{96,224},{112... | collective-permute-start | bytes 270344 | tf_op jit(solution)/shard_map/ppermute | solution.py:361
  6.8 3.7 %collective-permute-start.7 = (bf16[2,176,128]{2,1,0:T(8,128)(2,1)S(1)}, bf16[2,176,128]{2,1,0:T(8,128)(2,1)S(1)}, u32[]{:S(2)}, u32[]{:S(2)}) collective-permute-start(bf16[2,176,128]{2,1,0:T(8,128)(2,1)S(1)} %get-tuple-element.166), channel_id=1, source_target_pairs={{0,192},{16,208},{32,224},{48,240},{64,0},{80,16},{96,32},{112,48}... | collective-permute-start | bytes 270344 | tf_op jit(solution)/shard_map/ppermute | solution.py:361
  10.6 9.5 %copy-start.16 = (s32[16]{0:T(128)S(1)}, s32[16]{0:T(128)}, u32[]{:S(2)}) copy-start(s32[16]{0:T(128)} %param.15) | copy-start | bytes 196
  10.6 8.0 %collective-permute-start.10 = (bf16[2,128,640]{2,1,0:T(8,128)(2,1)S(1)}, bf16[2,128,640]{2,1,0:T(8,128)(2,1)S(1)}, u32[]{:S(2)}, u32[]{:S(2)}) collective-permute-start(bf16[2,128,640]{2,1,0:T(8,128)(2,1)S(1)} %get-tuple-element.158), channel_id=1, source_target_pairs={{0,192},{16,208},{32,224},{48,240},{64,0},{80,16},{96,32},{112,48}... | collective-permute-start | bytes 983048 | tf_op jit(solution)/shard_map/ppermute | solution.py:361
  12.8 18.6 %collective-permute-start.11 = (bf16[4,2,176,128]{3,2,1,0:T(8,128)(2,1)S(1)}, bf16[4,2,176,128]{3,2,1,0:T(8,128)(2,1)S(1)}, u32[]{:S(2)}, u32[]{:S(2)}) collective-permute-start(bf16[4,2,176,128]{3,2,1,0:T(8,128)(2,1)S(1)} %pad_maximum_fusion.2.kv0), channel_id=1, source_target_pairs={{0,16},{16,32},{32,48},{48,0},{64,80},{80,96},{96,112},{112,64},{1... | collective-permute-start | bytes 1081352 | tf_op jit(solution)/shard_map/ppermute | solution.py:366
  14.9 27.1 %collective-permute-start.12 = (bf16[4,2,176,128]{3,2,1,0:T(8,128)(2,1)S(1)}, bf16[4,2,176,128]{3,2,1,0:T(8,128)(2,1)S(1)}, u32[]{:S(2)}, u32[]{:S(2)}) collective-permute-start(bf16[4,2,176,128]{3,2,1,0:T(8,128)(2,1)S(1)} %pad_maximum_fusion.2.kv0), channel_id=1, source_target_pairs={{0,32},{16,48},{32,0},{48,16},{64,96},{80,112},{96,64},{112,80},{1... | collective-permute-start | bytes 1081352 | tf_op jit(solution)/shard_map/ppermute | solution.py:366
  17.9 24.1 %collective-permute-start.13 = (bf16[4,2,176,128]{3,2,1,0:T(8,128)(2,1)S(1)}, bf16[4,2,176,128]{3,2,1,0:T(8,128)(2,1)S(1)}, u32[]{:S(2)}, u32[]{:S(2)}) collective-permute-start(bf16[4,2,176,128]{3,2,1,0:T(8,128)(2,1)S(1)} %pad_maximum_fusion.2.kv0), channel_id=1, source_target_pairs={{0,48},{16,0},{32,16},{48,32},{64,112},{80,64},{96,80},{112,96},{1... | collective-permute-start | bytes 1081352 | tf_op jit(solution)/shard_map/ppermute | solution.py:366
  18.6 9.9 %collective-permute-start.8 = (bf16[2,128,640]{2,1,0:T(8,128)(2,1)S(1)}, bf16[2,128,640]{2,1,0:T(8,128)(2,1)S(1)}, u32[]{:S(2)}, u32[]{:S(2)}) collective-permute-start(bf16[2,128,640]{2,1,0:T(8,128)(2,1)S(1)} %get-tuple-element.160), channel_id=1, source_target_pairs={{0,64},{16,80},{32,96},{48,112},{64,128},{80,144},{96,160},{112,17... | collective-permute-start | bytes 983048 | tf_op jit(solution)/shard_map/ppermute | solution.py:361
  18.6 12.8 %collective-permute-start.9 = (bf16[2,128,640]{2,1,0:T(8,128)(2,1)S(1)}, bf16[2,128,640]{2,1,0:T(8,128)(2,1)S(1)}, u32[]{:S(2)}, u32[]{:S(2)}) collective-permute-start(bf16[2,128,640]{2,1,0:T(8,128)(2,1)S(1)} %get-tuple-element.161), channel_id=1, source_target_pairs={{0,128},{16,144},{32,160},{48,176},{64,192},{80,208},{96,224},{112... | collective-permute-start | bytes 983048 | tf_op jit(solution)/shard_map/ppermute | solution.py:361
  22.0 41.9 %copy-start.4 = (s32[3]{0:T(128)}, s32[3]{0:T(128)S(1)}, u32[]{:S(2)}) copy-start(s32[3]{0:T(128)S(1)} %pad_add_fusion.info) | copy-start | bytes 40
  57.0 21.0 %collective-permute-start.17 = (bf16[640,128]{1,0:T(8,128)(2,1)S(1)}, bf16[640,128]{1,0:T(8,128)(2,1)S(1)}, u32[]{:S(2)}, u32[]{:S(2)}) collective-permute-start(bf16[640,128]{1,0:T(8,128)(2,1)S(1)} %get-tuple-element.121), channel_id=1, source_target_pairs={{0,64},{16,80},{32,96},{48,112},{64,128},{80,144},{96,160},{112,17... | collective-permute-start | bytes 491528 | tf_op jit(solution)/shard_map/ppermute | solution.py:361
  57.1 20.9 %collective-permute-start.18 = (bf16[640,128]{1,0:T(8,128)(2,1)S(1)}, bf16[640,128]{1,0:T(8,128)(2,1)S(1)}, u32[]{:S(2)}, u32[]{:S(2)}) collective-permute-start(bf16[640,128]{1,0:T(8,128)(2,1)S(1)} %get-tuple-element.122), channel_id=1, source_target_pairs={{0,192},{16,208},{32,224},{48,240},{64,0},{80,16},{96,32},{112,48}... | collective-permute-start | bytes 491528 | tf_op jit(solution)/shard_map/ppermute | solution.py:361
  59.8 18.2 %collective-permute-start.14 = (bf16[4,2,48,128]{3,2,1,0:T(8,128)(2,1)S(1)}, bf16[4,2,48,128]{3,2,1,0:T(8,128)(2,1)S(1)}, u32[]{:S(2)}, u32[]{:S(2)}) collective-permute-start(bf16[4,2,48,128]{3,2,1,0:T(8,128)(2,1)S(1)} %get-tuple-element.118), channel_id=1, source_target_pairs={{0,16},{16,32},{32,48},{48,0},{64,80},{80,96},{96,112},{112,64},{1... | collective-permute-start | bytes 294920 | tf_op jit(solution)/shard_map/ppermute | solution.py:366
  61.8 16.2 %collective-permute-start.15 = (bf16[4,2,48,128]{3,2,1,0:T(8,128)(2,1)S(1)}, bf16[4,2,48,128]{3,2,1,0:T(8,128)(2,1)S(1)}, u32[]{:S(2)}, u32[]{:S(2)}) collective-permute-start(bf16[4,2,48,128]{3,2,1,0:T(8,128)(2,1)S(1)} %get-tuple-element.119), channel_id=1, source_target_pairs={{0,32},{16,48},{32,0},{48,16},{64,96},{80,112},{96,64},{112,80},{1... | collective-permute-start | bytes 294920 | tf_op jit(solution)/shard_map/ppermute | solution.py:366
  61.8 16.2 %collective-permute-start.16 = (bf16[4,2,48,128]{3,2,1,0:T(8,128)(2,1)S(1)}, bf16[4,2,48,128]{3,2,1,0:T(8,128)(2,1)S(1)}, u32[]{:S(2)}, u32[]{:S(2)}) collective-permute-start(bf16[4,2,48,128]{3,2,1,0:T(8,128)(2,1)S(1)} %get-tuple-element.120), channel_id=1, source_target_pairs={{0,48},{16,0},{32,16},{48,32},{64,112},{80,64},{96,80},{112,96},{1... | collective-permute-start | bytes 294920 | tf_op jit(solution)/shard_map/ppermute | solution.py:366
  75.3 0.7 copy-start
  76.0 0.7 copy-start.1
  76.7 0.7 copy-start.2
  77.3 0.7 copy-start.3
  78.0 3.6 %copy-start.13 = (bf16[640,128]{1,0:T(8,128)(2,1)}, bf16[640,128]{1,0:T(8,128)(2,1)S(1)}, u32[]{:S(2)}) copy-start(bf16[640,128]{1,0:T(8,128)(2,1)S(1)} %collective-permute-done.17.a1) | copy-start | bytes 491524
  78.0 3.5 %copy-start.14 = (bf16[640,128]{1,0:T(8,128)(2,1)}, bf16[640,128]{1,0:T(8,128)(2,1)S(1)}, u32[]{:S(2)}) copy-start(bf16[640,128]{1,0:T(8,128)(2,1)S(1)} %collective-permute-done.18.a3) | copy-start | bytes 491524
  78.1 41.3 %collective-permute-start.19 = (bf16[1280,128]{1,0:T(8,128)(2,1)S(1)}, bf16[1280,128]{1,0:T(8,128)(2,1)S(1)}, u32[]{:S(2)}, u32[]{:S(2)}) collective-permute-start(bf16[1280,128]{1,0:T(8,128)(2,1)S(1)} %get-tuple-element.127), channel_id=1, source_target_pairs={{0,128},{16,144},{32,160},{48,176},{64,192},{80,208},{96,224},{112... | collective-permute-start | bytes 983048 | tf_op jit(solution)/shard_map/ppermute | solution.py:361
  78.2 41.1 %collective-permute-start.20 = (bf16[4,2,128,128]{3,2,1,0:T(8,128)(2,1)S(1)}, bf16[4,2,128,128]{3,2,1,0:T(8,128)(2,1)S(1)}, u32[]{:S(2)}, u32[]{:S(2)}) collective-permute-start(bf16[4,2,128,128]{3,2,1,0:T(8,128)(2,1)S(1)} %get-tuple-element.132), channel_id=1, source_target_pairs={{0,16},{16,32},{32,48},{48,0},{64,80},{80,96},{96,112},{112,64},{1... | collective-permute-start | bytes 786440 | tf_op jit(solution)/shard_map/ppermute | solution.py:366
  78.3 41.0 %collective-permute-start.21 = (bf16[4,2,128,128]{3,2,1,0:T(8,128)(2,1)S(1)}, bf16[4,2,128,128]{3,2,1,0:T(8,128)(2,1)S(1)}, u32[]{:S(2)}, u32[]{:S(2)}) collective-permute-start(bf16[4,2,128,128]{3,2,1,0:T(8,128)(2,1)S(1)} %get-tuple-element.133), channel_id=1, source_target_pairs={{0,32},{16,48},{32,0},{48,16},{64,96},{80,112},{96,64},{112,80},{1... | collective-permute-start | bytes 786440 | tf_op jit(solution)/shard_map/ppermute | solution.py:366
  78.4 41.0 %collective-permute-start.22 = (bf16[4,2,128,128]{3,2,1,0:T(8,128)(2,1)S(1)}, bf16[4,2,128,128]{3,2,1,0:T(8,128)(2,1)S(1)}, u32[]{:S(2)}, u32[]{:S(2)}) collective-permute-start(bf16[4,2,128,128]{3,2,1,0:T(8,128)(2,1)S(1)} %get-tuple-element.134), channel_id=1, source_target_pairs={{0,48},{16,0},{32,16},{48,32},{64,112},{80,64},{96,80},{112,96},{1... | collective-permute-start | bytes 786440 | tf_op jit(solution)/shard_map/ppermute | solution.py:366
  81.6 17.6 %collective-permute-start = (f32[192,128]{1,0:T(8,128)S(1)}, f32[192,128]{1,0:T(8,128)S(1)}, u32[]{:S(2)}, u32[]{:S(2)}) collective-permute-start(f32[192,128]{1,0:T(8,128)S(1)} %select_bitcast_fusion.2), channel_id=1, source_target_pairs={{0,1},{1,0},{2,3},{3,2},{4,5},{5,4},{6,7},{7,6},{8,9},{9,8},{10,11... | collective-permute-start | bytes 294920 | tf_op jit(solution)/shard_map/while/body/ppermute | solution.py:370
  99.2 3.3 %collective-permute-start.1 = (bf16[192,128]{1,0:T(8,128)(2,1)S(1)}, bf16[192,128]{1,0:T(8,128)(2,1)S(1)}, u32[]{:S(2)}, u32[]{:S(2)}) collective-permute-start(bf16[192,128]{1,0:T(8,128)(2,1)S(1)} %fusion.14), channel_id=1, source_target_pairs={{0,2},{1,3},{2,0},{3,1},{4,6},{5,7},{6,4},{7,5},{8,10},{9,11},{10,... | collective-permute-start | bytes 147464 | tf_op jit(solution)/shard_map/while/body/ppermute | solution.py:374
  102.5 4.5 %collective-permute-start.2 = (bf16[192,128]{1,0:T(8,128)(2,1)S(1)}, bf16[192,128]{1,0:T(8,128)(2,1)S(1)}, u32[]{:S(2)}, u32[]{:S(2)}) collective-permute-start(bf16[192,128]{1,0:T(8,128)(2,1)S(1)} %add_convert_fusion.6), channel_id=1, source_target_pairs={{0,4},{1,5},{2,6},{3,7},{4,0},{5,1},{6,2},{7,3},{8,12},{9,13},{10,... | collective-permute-start | bytes 147464 | tf_op jit(solution)/shard_map/while/body/ppermute | solution.py:374
  107.1 7.1 %collective-permute-start.3 = (bf16[192,128]{1,0:T(8,128)(2,1)S(1)}, bf16[192,128]{1,0:T(8,128)(2,1)S(1)}, u32[]{:S(2)}, u32[]{:S(2)}) collective-permute-start(bf16[192,128]{1,0:T(8,128)(2,1)S(1)} %add_convert_fusion.7), channel_id=1, source_target_pairs={{0,8},{1,9},{2,10},{3,11},{4,12},{5,13},{6,14},{7,15},{8,0},{9,1},... | collective-permute-start | bytes 147464 | tf_op jit(solution)/shard_map/while/body/ppermute | solution.py:378
  114.2 4.4 %collective-permute-start.4 = (bf16[192,128]{1,0:T(8,128)(2,1)S(1)}, bf16[192,128]{1,0:T(8,128)(2,1)S(1)}, u32[]{:S(2)}, u32[]{:S(2)}) collective-permute-start(bf16[192,128]{1,0:T(8,128)(2,1)S(1)} %add_convert_fusion.8), channel_id=1, source_target_pairs={{0,1},{1,0},{2,3},{3,2},{4,5},{5,4},{6,7},{7,6},{8,9},{9,8},{10,11... | collective-permute-start | bytes 147464 | tf_op jit(solution)/shard_map/while/body/ppermute | solution.py:370
  119.4 0.7 copy-start.8
  119.4 0.8 copy-start.9
  119.4 0.8 copy-start.10
  119.4 1.0 copy-start.5
  123.4 11.5 %collective-permute-start.23 = (bf16[992,128]{1,0:T(8,128)(2,1)}, bf16[992,128]{1,0:T(8,128)(2,1)S(1)}, u32[]{:S(2)}, u32[]{:S(2)}) collective-permute-start(bf16[992,128]{1,0:T(8,128)(2,1)} %get-tuple-element.142), channel_id=1, source_target_pairs={{0,64},{16,80},{32,96},{48,112},{64,128},{80,144},{96,160},{112,17... | collective-permute-start | bytes 761864 | tf_op jit(solution)/shard_map/ppermute | solution.py:361
  123.9 11.0 %collective-permute-start.25 = (bf16[992,128]{1,0:T(8,128)(2,1)}, bf16[992,128]{1,0:T(8,128)(2,1)S(1)}, u32[]{:S(2)}, u32[]{:S(2)}) collective-permute-start(bf16[992,128]{1,0:T(8,128)(2,1)} %get-tuple-element.144), channel_id=1, source_target_pairs={{0,192},{16,208},{32,224},{48,240},{64,0},{80,16},{96,32},{112,48}... | collective-permute-start | bytes 761864 | tf_op jit(solution)/shard_map/ppermute | solution.py:361
  126.0 8.8 %collective-permute-start.24 = (bf16[352,128]{1,0:T(8,128)(2,1)}, bf16[352,128]{1,0:T(8,128)(2,1)S(1)}, u32[]{:S(2)}, u32[]{:S(2)}) collective-permute-start(bf16[352,128]{1,0:T(8,128)(2,1)} %get-tuple-element.143), channel_id=1, source_target_pairs={{0,128},{16,144},{32,160},{48,176},{64,192},{80,208},{96,224},{112... | collective-permute-start | bytes 270344 | tf_op jit(solution)/shard_map/ppermute | solution.py:361
  134.9 0.6 copy-start.15
  134.9 0.7 copy-start.11
  134.9 0.8 copy-start.12

commit v2 on v1

--- a/solution.py
+++ b/solution.py
@@ -76,17 +76,17 @@
         lax.fori_loop(first, last, step, 0)
 
 
-def forward_kernel(
+def prompt_kernel(
     info,
     x0, x1, x2, x3,
-    kv0, kv1, kv2, kv3,
-    r0, r1, r2, r3,
-    a1, a3, os, qs, gs, ks, vs, kt, tops, deltas, dq_part,
-    kp, vp, kpt, vpt, vt, sc, pm, dk, dv,
+    mine, other,
+    qs, gs, kpt, vp, pm, tops, totals, outs,
+    kp, vpt, sc,
 ):
     y = info[0]
     z = info[1]
     length = info[2]
+    core = info[3]
     for s, x in enumerate((x0, x1, x2, x3)):
         block = lax.rem(y - s + NY, NY)
         start = (block * NZ + z) * BLOCK
@@ -96,23 +96,101 @@
             cols = slice(j * HD, (j + 1) * HD)
             qs[at, :] = x[0, :, cols]
             gs[at, :] = jnp.where(valid, x[1, :, cols].astype(F32), 0.0).astype(BF16)
+
+    @pl.when(core == 0)
+    def _():
+        kp[...] = mine[...]
+        vp[...] = other[...]
+
+    @pl.when(core != 0)
+    def _():
+        kp[...] = other[...]
+        vp[...] = mine[...]
+
+    for c in range(PROMPT_CHUNKS):
+        rows = chunk_rows(c)
+        kpt[:, rows] = kp[rows, :].T
+        vpt[:, rows] = vp[rows, :].T
+
+    def step(tile, carry):
+        low_pos, _ = tile_positions(tile, z)
+
+        @pl.when(low_pos < length)
+        def _():
+            qt = qs[aligned(tile * TILE, TILE), :].T
+            top = jnp.full((8, TILE), MASKED, F32)
+            for c in range(PROMPT_CHUNKS):
+                s = jnp.dot(kp[chunk_rows(c), :], qt, preferred_element_type=F32)
+                sc[chunk_rows(c), :] = s
+                top = jnp.maximum(top, jnp.max(fold(s), axis=0))
+            top = jnp.max(top, axis=0, keepdims=True)
+            total = jnp.zeros((8, TILE), F32)
+            out_t = jnp.zeros((HD, TILE), F32)
+            for c in range(PROMPT_CHUNKS):
+                p = jnp.exp2((sc[chunk_rows(c), :] - top) * SCALE2)
+                total = total + jnp.sum(fold(p), axis=0)
+                low = p.astype(BF16)
+                pm[aligned(tile * PROMPT + c * CHUNK, CHUNK), :] = low
+                out_t = out_t + jnp.dot(vpt[:, chunk_rows(c)], low, preferred_element_type=F32)
+            stat = aligned(tile * 8, 8)
+            tops[stat, :] = jnp.broadcast_to(top, (8, TILE))
+            totals[stat, :] = total
+            outs[aligned(tile * HD, HD), :] = out_t
+
+        return carry
+
+    lax.fori_loop(0, TILES, step, 0)
+
+
+def prompt_forward(info, rows, mine, other):
+    return pl.pallas_call(
+        prompt_kernel,
+        out_shape=[
+            shaped((ROWS, HD), BF16),
+            shaped((ROWS, HD), BF16),
+            shaped((HD, PROMPT), BF16),
+            shaped((PROMPT, HD), BF16),
+            shaped((TILES * PROMPT, TILE), BF16),
+            shaped((TILES * 8, TILE), F32),
+            shaped((TILES * 8, TILE), F32),
+            shaped((TILES * HD, TILE), F32),
+        ],
+        in_specs=[SMEM] + [VMEM] * 6,
+        out_specs=[VMEM] * 8,
+        scratch_shapes=[
+            pltpu.VMEM((PROMPT, HD), BF16),
+            pltpu.VMEM((HD, PROMPT), BF16),
+            pltpu.VMEM((PROMPT, TILE), F32),
+        ],
+        cost_estimate=pl.CostEstimate(
+            flops=10**6, bytes_accessed=2**10, transcendentals=0
+        ),
+        compiler_params=pltpu.CompilerParams(vmem_limit_bytes=32 * 2**20),
+        name="prompt_forward",
+    )(info, *rows, mine, other)
+
+
+def forward_kernel(
+    info,
+    qs, gs_in, kpt, vp, pm, tops_in, totals, outs,
+    kv0, kv1, kv2, kv3,
+    r0, r1, r2, r3,
+    a1, a3, os, gs, ks, vs, kt, tops, deltas, dq_part,
+    vt, sc, dk, dv,
+):
+    y = info[0]
+    z = info[1]
+    length = info[2]
     for s, kv in enumerate((kv0, kv1, kv2, kv3)):
         zp = lax.rem(z - s + NZ, NZ)
         for b in range(NY):
-            at = aligned((zp * NY + b) * PROMPT_ROWS, PROMPT_ROWS)
-            kp[at, :] = kv[b, 0, :PROMPT_ROWS, :]
-            vp[at, :] = kv[b, 1, :PROMPT_ROWS, :]
             at = aligned((b * NZ + zp) * BLOCK, BLOCK)
-            k = kv[b, 0, PROMPT_ROWS:, :]
-            v = kv[b, 1, PROMPT_ROWS:, :]
+            k = kv[b, 0]
+            v = kv[b, 1]
             ks[at, :] = k
             vs[at, :] = v
             kt[:, at] = k.T
             vt[:, at] = v.T
-    for c in range(PROMPT_CHUNKS):
-        rows = chunk_rows(c)
-        kpt[:, rows] = kp[rows, :].T
-        vpt[:, rows] = vp[rows, :].T
     dk[...] = jnp.zeros_like(dk)
     dv[...] = jnp.zeros_like(dv)
 
@@ -124,44 +202,42 @@
         def _():
             q = qs[at, :]
             qt = q.T
-            top = jnp.full((8, TILE), MASKED, F32)
-            for c in range(-PROMPT_CHUNKS, chunks):
-                k = kp[chunk_rows(c + PROMPT_CHUNKS), :] if c < 0 else ks[chunk_rows(c), :]
-                s = jnp.dot(k, qt, preferred_element_type=F32)
+            stat = aligned(tile * 8, 8)
+            first_top = tops_in[stat, :]
+            top = first_top
+            for c in range(chunks):
+                s = jnp.dot(ks[chunk_rows(c), :], qt, preferred_element_type=F32)
                 if c >= first_masked:
                     s = causal(s, c, query_pos)
-                sc[chunk_rows(c + PROMPT_CHUNKS), :] = s
+                sc[chunk_rows(c), :] = s
                 top = jnp.maximum(top, jnp.max(fold(s), axis=0))
             top = jnp.max(top, axis=0, keepdims=True)
-            total = jnp.zeros((8, TILE), F32)
-            out_t = jnp.zeros((HD, TILE), F32)
-            for c in range(-PROMPT_CHUNKS, chunks):
-                p = jnp.exp2((sc[chunk_rows(c + PROMPT_CHUNKS), :] - top) * SCALE2)
+            alpha = jnp.exp2((first_top[:1] - top) * SCALE2)
+            total = totals[stat, :] * alpha
+            out_t = outs[aligned(tile * HD, HD), :] * alpha
+            for c in range(chunks):
+                p = jnp.exp2((sc[chunk_rows(c), :] - top) * SCALE2)
                 total = total + jnp.sum(fold(p), axis=0)
                 low = p.astype(BF16)
-                if c < 0:
-                    pm[chunk_rows(c + PROMPT_CHUNKS), :] = low
-                    v = vpt[:, chunk_rows(c + PROMPT_CHUNKS)]
-                else:
-                    v = vt[:, chunk_rows(c)]
-                out_t = out_t + jnp.dot(v, low, preferred_element_type=F32)
+                out_t = out_t + jnp.dot(vt[:, chunk_rows(c)], low, preferred_element_type=F32)
             inv = 1.0 / jnp.sum(total, axis=0, keepdims=True)
             out_t = out_t * inv
             os[at, :] = jnp.where(query_pos < length, out_t, 0.0).T.astype(BF16)
-            grad_t = gs[at, :].astype(F32).T
+            grad_t = gs_in[at, :].astype(F32).T
             delta = jnp.sum(grad_t * out_t, axis=0, keepdims=True) * inv
             grad_t = grad_t * inv
+            gs[at, :] = grad_t.T.astype(BF16)
+            tops[stat, :] = jnp.broadcast_to(top, (8, TILE))
+            deltas[stat, :] = jnp.broadcast_to(delta, (8, TILE))
+            grad_t = grad_t * alpha
             grad = grad_t.T.astype(BF16)
             grad_t = grad_t.astype(BF16)
-            gs[at, :] = grad
-            stat = aligned(tile * 8, 8)
-            tops[stat, :] = jnp.broadcast_to(top, (8, TILE))
-            deltas[stat, :] = jnp.broadcast_to(delta, (8, TILE))
+            delta = delta * alpha
             dq_t = jnp.zeros((HD, TILE), F32)
             for c in range(PROMPT_CHUNKS):
                 rows = chunk_rows(c)
                 dp = jnp.dot(vp[rows, :], grad_t, preferred_element_type=F32)
-                low = pm[rows, :]
+                low = pm[aligned(tile * PROMPT + c * CHUNK, CHUNK), :]
                 ds = (low.astype(F32) * (dp - delta)).astype(BF16)
                 dv[rows, :] += jnp.dot(low, grad, preferred_element_type=F32)
                 dk[rows, :] += jnp.dot(ds, q, preferred_element_type=F32)
@@ -176,20 +252,19 @@
     a1[...] = os[head_rows(y + 1), :]
     a3[...] = os[head_rows(y + 3), :]
     for s, r in enumerate((r0, r1, r2, r3)):
-        zp = lax.rem(z + s, NZ)
+        slot = z ^ lax.rem(z + s, NZ)
         for b in range(NY):
-            at = aligned((zp * NY + b) * PROMPT_ROWS, PROMPT_ROWS)
+            at = aligned((slot * NY + b) * PROMPT_ROWS, PROMPT_ROWS)
             r[b, 0] = (dk[at, :] * SCALE).astype(BF16)
             r[b, 1] = dv[at, :].astype(BF16)
 
 
-def forward(info, rows, keyvals):
+def forward(info, state, keyvals):
     return pl.pallas_call(
         forward_kernel,
         out_shape=[shaped((NY, 2, PROMPT_ROWS, HD), BF16)] * 4
         + [shaped((GROUP, HD), BF16)] * 2
         + [
-            shaped((ROWS, HD), BF16),
             shaped((ROWS, HD), BF16),
             shaped((ROWS, HD), BF16),
             shaped((RESP, HD), BF16),
@@ -199,25 +274,20 @@
             shaped((TILES * 8, TILE), F32),
             shaped((TILES * HD, TILE), F32),
         ],
-        in_specs=[SMEM] + [VMEM] * 8,
-        out_specs=[VMEM] * 15,
+        in_specs=[SMEM] + [VMEM] * 12,
+        out_specs=[VMEM] * 14,
         scratch_shapes=[
-            pltpu.VMEM((PROMPT, HD), BF16),
-            pltpu.VMEM((PROMPT, HD), BF16),
-            pltpu.VMEM((HD, PROMPT), BF16),
-            pltpu.VMEM((HD, PROMPT), BF16),
             pltpu.VMEM((HD, RESP), BF16),
-            pltpu.VMEM((KEYS, TILE), F32),
-            pltpu.VMEM((PROMPT, TILE), BF16),
+            pltpu.VMEM((RESP, TILE), F32),
             pltpu.VMEM((PROMPT, HD), F32),
             pltpu.VMEM((PROMPT, HD), F32),
         ],
         cost_estimate=pl.CostEstimate(
             flops=16 * 10**9, bytes_accessed=8 * 2**20, transcendentals=5 * 10**6
         ),
-        compiler_params=pltpu.CompilerParams(vmem_limit_bytes=40 * 2**20),
+        compiler_params=pltpu.CompilerParams(vmem_limit_bytes=32 * 2**20),
         name="forward",
-    )(info, *rows, *keyvals)
+    )(info, *state, *keyvals)
 
 
 def backward_kernel(
@@ -366,6 +436,10 @@
     return lax.ppermute(a, "prefix", pairs)
 
 
+def z_swap(a, bit):
+    return lax.ppermute(a, "prefix", [(i, i ^ bit) for i in range(NY * NZ)])
+
+
 def core_swap(a):
     return lax.ppermute(a, "resp", [(i, i ^ 1) for i in range(16)])
 
@@ -388,6 +462,19 @@
     other = core_swap(half.astype(BF16)).astype(F32)
     half = half.astype(BF16).astype(F32)
     return jnp.stack([jnp.where(core == 0, half, other), jnp.where(core == 0, other, half)])
+
+
+def bring_first(state):
+    mine, other, x1, x2, x3 = state
+    part = NY * PROMPT_ROWS
+    pair = jnp.concatenate([mine[:part], z_swap(mine[:part], 1)])
+    mine = jnp.concatenate([pair, z_swap(pair, 2)])
+    other = core_swap(mine)
+    x1, other = lax.optimization_barrier((x1, other))
+    x1 = y_shift(x1, 1)
+    x2 = y_shift(x2, 2)
+    x3, x2 = lax.optimization_barrier((x3, x2))
+    return mine, other, x1, x2, y_shift(x3, 3)
 
 
 def by_y(pieces):
@@ -409,7 +496,9 @@
 ):
     prefix = lax.axis_index("prefix")
     y, z = prefix // NZ, prefix % NZ
-    info = jnp.stack([y, z, lengths[lax.axis_index("resp")]]).astype(jnp.int32)
+    resp = lax.axis_index("resp")
+    core = resp % 2
+    info = jnp.stack([y, z, lengths[resp], core]).astype(jnp.int32)
     pick = lax.dynamic_index_in_dim
 
     def split(a, width):
@@ -425,24 +514,28 @@
         ]
     )
     keyvals = by_y(split(keyvals, HD))
-    *keyvals, queries, grads = lax.optimization_barrier(
-        (*keyvals, response_queries[0], output_grad[0])
+    stacked = jnp.stack(keyvals)
+    stacked = jnp.stack([pick(stacked, (y - b) % NY, 0, keepdims=False) for b in range(NY)])
+    half = pick(stacked[:, :, :PROMPT_ROWS], core, 1, keepdims=False)
+    half = half.reshape(NY * PROMPT_ROWS, HD)
+    mine = jnp.concatenate([half] * NZ)
+    keyvals = by_z([stacked[:, :, PROMPT_ROWS:]] * NZ)
+    x0, *rows = split(jnp.stack([response_queries[0], output_grad[0]]), HEADS * HD)
+    once = jnp.minimum(lengths[0], 1)
+    mine, other, *rows = lax.fori_loop(
+        0, once, lambda i, state: bring_first(state), (mine, mine, *rows)
     )
-    stacked = jnp.stack(keyvals)
-    keyvals = jnp.stack([pick(stacked, (y - b) % NY, 0, keepdims=False) for b in range(NY)])
-    keyvals = by_z([keyvals] * NZ)
-    rows = by_y(split(jnp.stack([queries, grads]), HEADS * HD))
-
-    results = forward(info, rows, keyvals)
+
+    qs, *state = prompt_forward(info, (x0, *rows), mine, other)
+    results = forward(info, (qs, *state), keyvals)
     prompt_terms = by_z(results[:4])
     att = [y_shift(results[4], 1), y_shift(results[5], 3)]
-    d0, d1, d2, d3, *terms = backward(info, results[6:])
+    d0, d1, d2, d3, *terms = backward(info, (results[6], qs, *results[7:]))
     *prompt_terms, att[0], att[1], d2, terms[1], terms[2], terms[3] = lax.optimization_barrier(
         (*prompt_terms, *att, d2, terms[1], terms[2], terms[3])
     )
     prompt = sum(t.astype(F32) for t in prompt_terms)
     prompt = prompt.transpose(1, 0, 2, 3).reshape(2, NY * PROMPT_ROWS, HD)
-    once = jnp.minimum(lengths[0], 1)
     terms = by_z(terms)
     d2 = y_shift(d2, 2)
     prompt = lax.fori_loop(0, once, lambda i, terms: over_responses(terms), prompt)

time: 138 us -> 154 us (1.12)
  Pallas kernels: 32 us -> 17.8 us
  starting transfers between devices: 57.9 us -> 70.7 us
  waiting for transfers between devices: 38.6 us -> 51.2 us
  local copies, waits for them, and re-layouts: 5.83 us -> 8.04 us
  other arithmetic: 2.28 us -> 3.83 us
    ppermute x0 -> x2, waiting for transfers between devices: none -> 22.8 us  [z_swap(): return lax.ppermute(a, 'prefix', [(i, i ^ bit) for i in range(NY * NZ)])]
    ppermute x2 -> x3, starting transfers between devices: 20.1 us -> 35.2 us  [core_swap(): return lax.ppermute(a, 'resp', [(i, i ^ 1) for i in range(16)])]
    ppermute x9, waiting for transfers between devices: 10.6 us -> 0.02 us  [z_shift(): return lax.ppermute(a, 'prefix', pairs)]
    pallas_call x1, Pallas kernels: 15.1 us -> 4.79 us  [forward(): pl.pallas_call(forward_kernel, out_shape=[shaped((NY, 2, PROMPT_ROWS, HD)...]
    pallas_call x1, Pallas kernels: 11.3 us -> 3.79 us  [backward(): pl.pallas_call(backward_kernel, out_shape=[shaped((rows, HD), BF16) for r...]
    ppermute x1, waiting for transfers between devices: 1.57 us -> 6.47 us  [far_swap(): return lax.ppermute(a, 'resp', [(i, i ^ 8) for i in range(16)])]
    ppermute x1, starting transfers between devices: 5.56 us -> 0.76 us  [far_swap(): return lax.ppermute(a, 'resp', [(i, i ^ 8) for i in range(16)])]
    pallas_call x0 -> x1, Pallas kernels: none -> 3.68 us  [prompt_forward(): pl.pallas_call(prompt_kernel, out_shape=[shaped((ROWS, HD), BF16), shaped...]
  transfers between devices with their start and end apart: 26 -> 29, of which waited for: 10 -> 11; matrix products, arithmetic and copies ran while one was open for 2% -> 2% of each run, Pallas kernels for 8% -> 5%
where the time goes in v2:
time: 154 us; the launch traced here: 153 us
  starting transfers between devices  70.7 us (46%)
  waiting for transfers between devices  51.2 us (33%)
  Pallas kernels  17.8 us (12%)
  local copies, waits for them, and re-layouts  8.04 us (5%)
  other arithmetic  3.83 us (2%)
  between operations  1.75 us (1%)
    ppermute x3, starting transfers between devices, core_swap(): return lax.ppermute(a, 'resp', [(i, i ^ 1) for i in range(16)])  35.2 us
    ppermute x2, waiting for transfers between devices, z_swap(): return lax.ppermute(a, 'prefix', [(i, i ^ bit) for i in range(NY * NZ)])  22.8 us
    ppermute x12, starting transfers between devices, y_shift(): return lax.ppermute(a, 'prefix', pairs)  18.1 us
    ppermute x12, waiting for transfers between devices, y_shift(): return lax.ppermute(a, 'prefix', pairs)  15.4 us
    ppermute x9, starting transfers between devices, z_shift(): return lax.ppermute(a, 'prefix', pairs)  12.6 us
    ppermute x1, waiting for transfers between devices, far_swap(): return lax.ppermute(a, 'resp', [(i, i ^ 8) for i in range(16)])  6.47 us
    unnamed x38, local copies, waits for them, and re-layouts  5.73 us
    pallas_call x1, Pallas kernels, forward(): pl.pallas_call(forward_kernel, out_shape=[shaped((NY, 2, PROMPT_ROWS, HD)...  4.79 us
  transfers between devices with their start and end apart: 29, of which 11 were waited for; matrix products, arithmetic and copies ran while one was open for 2% of the time, Pallas kernels for 5%

profile of v2, /device:TPU:1, one launch (start us, length us, event | category | flops | bytes accessed | tf_op | source)
XLA Modules:
  0.0 153.4 jit_solution(5358587912038925091)
XLA Ops:
  0.8 1.1 maximum_bitcast_fusion
  1.9 0.8 fusion.5
  2.6 2.1 %collective-permute-start.11 = (bf16[2,176,128]{2,1,0:T(8,128)(2,1)}, bf16[2,176,128]{2,1,0:T(8,128)(2,1)}, u32[]{:S(2)}, u32[]{:S(2)}) collective-permute-start(bf16[2,176,128]{2,1,0:T(8,128)(2,1)} %get-tuple-element.233), channel_id=1, source_target_pairs={{0,64},{16,80},{32,96},{48,112},{64,128},{80,144},{96,160},{112,17... | collective-permute-start | bytes 270344 | tf_op jit(solution)/shard_map/ppermute | solution.py:431
  4.8 2.6 %collective-permute-start.12 = (bf16[2,176,128]{2,1,0:T(8,128)(2,1)}, bf16[2,176,128]{2,1,0:T(8,128)(2,1)}, u32[]{:S(2)}, u32[]{:S(2)}) collective-permute-start(bf16[2,176,128]{2,1,0:T(8,128)(2,1)} %get-tuple-element.234), channel_id=1, source_target_pairs={{0,128},{16,144},{32,160},{48,176},{64,192},{80,208},{96,224},{112... | collective-permute-start | bytes 270344 | tf_op jit(solution)/shard_map/ppermute | solution.py:431
  7.4 1.1 collective-permute-start.13
  10.5 0.7 pad_add_fusion.info
  11.4 1.0 pad_maximum_fusion.3
  12.5 1.7 %collective-permute-start.14 = (bf16[4,2,128,128]{3,2,1,0:T(8,128)(2,1)S(1)}, bf16[4,2,128,128]{3,2,1,0:T(8,128)(2,1)S(1)}, u32[]{:S(2)}, u32[]{:S(2)}) collective-permute-start(bf16[4,2,128,128]{3,2,1,0:T(8,128)(2,1)S(1)} %pad_maximum_fusion.4.kv0), channel_id=1, source_target_pairs={{0,16},{16,32},{32,48},{48,0},{64,80},{80,96},{96,112},{112,64},{1... | collective-permute-start | bytes 786440 | tf_op jit(solution)/shard_map/ppermute | solution.py:436
  14.2 3.0 %collective-permute-start.15 = (bf16[4,2,128,128]{3,2,1,0:T(8,128)(2,1)S(1)}, bf16[4,2,128,128]{3,2,1,0:T(8,128)(2,1)S(1)}, u32[]{:S(2)}, u32[]{:S(2)}) collective-permute-start(bf16[4,2,128,128]{3,2,1,0:T(8,128)(2,1)S(1)} %pad_maximum_fusion.4.kv0), channel_id=1, source_target_pairs={{0,32},{16,48},{32,0},{48,16},{64,96},{80,112},{96,64},{112,80},{1... | collective-permute-start | bytes 786440 | tf_op jit(solution)/shard_map/ppermute | solution.py:436
  17.2 0.7 collective-permute-start.16
  17.9 0.7 copy.20
  18.6 38.3 %while.30 = (s32[]{:T(128)}, bf16[768,128]{1,0:T(8,128)(2,1)S(1)}, bf16[768,128]{1,0:T(8,128)(2,1)}, bf16[2,128,640]{2,1,0:T(8,128)(2,1)S(1)}, bf16[2,128,640]{2...) while((s32[]{:T(128)}, bf16[768,128]{1,0:T(8,128)(2,1)S(1)}, ...), condition=%wide.region_1.2_spmd, body=%wide.region_0.1_spmd.sunk | while | flops 786434 | bytes 8749409 | solution.py:525
  18.6 0.7 collective-permute-start
  19.3 15.9 %collective-permute-done = bf16[192,128]{1,0:T(8,128)(2,1)S(1)} collective-permute-done((bf16[192,128]{1,0:T(8,128)(2,1)S(1)}, bf16[192,128]{1,0:T(8,128)(2,1)S(1)}, u32[]{:S(2)}, u32[]{:S(2)}) %collective-permute-start) | collective-permute-done | bytes 49184 | tf_op jit(solution)/shard_map/while/body/ppermute | solution.py:440
  35.3 2.5 %collective-permute-start.4 = (bf16[2,128,640]{2,1,0:T(8,128)(2,1)S(1)}, bf16[2,128,640]{2,1,0:T(8,128)(2,1)S(1)}, u32[]{:S(2)}, u32[]{:S(2)}) collective-permute-start(bf16[2,128,640]{2,1,0:T(8,128)(2,1)S(1)} %get-tuple-element.326), channel_id=1, source_target_pairs={{0,128},{16,144},{32,160},{48,176},{64,192},{80,208},{96,224},{112... | collective-permute-start | bytes 983048 | tf_op jit(solution)/shard_map/while/body/ppermute | solution.py:431
  37.9 6.9 %collective-permute-done.1 = bf16[384,128]{1,0:T(8,128)(2,1)S(1)} collective-permute-done((bf16[384,128]{1,0:T(8,128)(2,1)S(1)}, bf16[384,128]{1,0:T(8,128)(2,1)S(1)}, u32[]{:S(2)}, u32[]{:S(2)}) %collective-permute-start.1) | collective-permute-done | bytes 98336 | tf_op jit(solution)/shard_map/while/body/ppermute | solution.py:440
  45.4 2.4 %collective-permute-start.5 = (bf16[2,128,640]{2,1,0:T(8,128)(2,1)S(1)}, bf16[2,128,640]{2,1,0:T(8,128)(2,1)S(1)}, u32[]{:S(2)}, u32[]{:S(2)}) collective-permute-start(bf16[2,128,640]{2,1,0:T(8,128)(2,1)S(1)} %get-tuple-element.308), channel_id=1, source_target_pairs={{0,192},{16,208},{32,224},{48,240},{64,0},{80,16},{96,32},{112,48}... | collective-permute-start | bytes 983048 | tf_op jit(solution)/shard_map/while/body/ppermute | solution.py:431
  47.8 0.7 copy-done.6
  48.5 4.5 %collective-permute-done.5 = bf16[2,128,640]{2,1,0:T(8,128)(2,1)S(1)} collective-permute-done((bf16[2,128,640]{2,1,0:T(8,128)(2,1)S(1)}, bf16[2,128,640]{2,1,0:T(8,128)(2,1)S(1)}, u32[]{:S(2)}, u32[]{:S(2)}) %collective-permute-start.5) | collective-permute-done | bytes 327712 | tf_op jit(solution)/shard_map/while/body/ppermute | solution.py:431
  53.0 3.8 %collective-permute-done.3 = bf16[2,128,640]{2,1,0:T(8,128)(2,1)S(1)} collective-permute-done((bf16[2,128,640]{2,1,0:T(8,128)(2,1)S(1)}, bf16[2,128,640]{2,1,0:T(8,128)(2,1)S(1)}, u32[]{:S(2)}, u32[]{:S(2)}) %collective-permute-start.3) | collective-permute-done | bytes 327712 | tf_op jit(solution)/shard_map/while/body/ppermute | solution.py:431
  56.9 3.7 %prompt_forward.1 = (bf16[2560,128]{1,0:T(8,128)(2,1)S(1)}, bf16[2560,128]{1,0:T(8,128)(2,1)S(1)}, bf16[128,768]{1,0:T(8,128)(2,1)S(1)}, bf16[768,128]{1,0:T(8,1...) custom-call(s32[4]{0:T(128)S(1)} %pad_add_fusion.info, ...), custom_call_target="tpu_custom_call" | custom-call | flops 1000000 | bytes 1024 | tf_op jit(solution)/shard_map/prompt_forward/pallas_call | solution.py:146
  60.6 4.8 %forward.1 = (bf16[4,2,48,128]{3,2,1,0:T(8,128)(2,1)S(1)}, bf16[4,2,48,128]{3,2,1,0:T(8,128)(2,1)S(1)}, bf16[4,2,48,128]{3,2,1,0:T(8,128)(2,1)S(1)}, bf16[4,2,48...) custom-call(s32[4]{0:T(128)S(1)} %pad_add_fusion.info, ...), custom_call_target="tpu_custom_call" | custom-call | flops 16000000000 | bytes 8388608 | tf_op jit(solution)/shard_map/forward/pallas_call | solution.py:263
  65.5 2.7 %collective-permute-start.21 = (bf16[640,128]{1,0:T(8,128)(2,1)S(1)}, bf16[640,128]{1,0:T(8,128)(2,1)S(1)}, u32[]{:S(2)}, u32[]{:S(2)}) collective-permute-start(bf16[640,128]{1,0:T(8,128)(2,1)S(1)} %get-tuple-element.174), channel_id=1, source_target_pairs={{0,192},{16,208},{32,224},{48,240},{64,0},{80,16},{96,32},{112,48}... | collective-permute-start | bytes 491528 | tf_op jit(solution)/shard_map/ppermute | solution.py:431
  68.1 1.1 collective-permute-start.18
  69.2 2.4 %collective-permute-start.19 = (bf16[4,2,48,128]{3,2,1,0:T(8,128)(2,1)S(1)}, bf16[4,2,48,128]{3,2,1,0:T(8,128)(2,1)S(1)}, u32[]{:S(2)}, u32[]{:S(2)}) collective-permute-start(bf16[4,2,48,128]{3,2,1,0:T(8,128)(2,1)S(1)} %get-tuple-element.172), channel_id=1, source_target_pairs={{0,48},{16,0},{32,16},{48,32},{64,112},{80,64},{96,80},{112,96},{1... | collective-permute-start | bytes 294920 | tf_op jit(solution)/shard_map/ppermute | solution.py:436
  71.6 3.8 %backward.1 = (bf16[1280,128]{1,0:T(8,128)(2,1)S(1)}, bf16[640,128]{1,0:T(8,128)(2,1)S(1)}, bf16[1280,128]{1,0:T(8,128)(2,1)S(1)}, bf16[640,128]{1,0:T(8,128)(2,...) custom-call(s32[4]{0:T(128)S(1)} %pad_add_fusion.info, ...), custom_call_target="tpu_custom_call" | custom-call | flops 16000000000 | bytes 8388608 | tf_op jit(solution)/shard_map/backward/pallas_call | solution.py:351
  75.4 0.7 copy-done
  76.1 0.7 copy-done.1
  76.8 0.7 copy-done.2
  77.5 0.7 copy-done.3
  78.5 1.3 collective-permute-start.24
  79.8 2.3 %collective-permute-start.25 = (bf16[4,2,128,128]{3,2,1,0:T(8,128)(2,1)S(1)}, bf16[4,2,128,128]{3,2,1,0:T(8,128)(2,1)S(1)}, u32[]{:S(2)}, u32[]{:S(2)}) collective-permute-start(bf16[4,2,128,128]{3,2,1,0:T(8,128)(2,1)S(1)} %get-tuple-element.186), channel_id=1, source_target_pairs={{0,48},{16,0},{32,16},{48,32},{64,112},{80,64},{96,80},{112,96},{1... | collective-permute-start | bytes 786440 | tf_op jit(solution)/shard_map/ppermute | solution.py:436
  82.1 51.8 %while.31 = (s32[]{:T(128)}, f32[2,192,128]{2,1,0:T(8,128)S(1)}, s32[]{:T(128)}, s32[]{:T(128)}, u32[]{:T(128)}, /*index=5*/s32[]{:T(128)}, s32[]{:T(128)}) while((s32[]{:T(128)}, f32[2,192,128]{2,1,0:T(8,128)S(1)}, s32[]{:T(128)}, s32[]{:T(128)}, u32[]{:T(128)}, /*index=5*/s32[]{:T(128)}, s32[]{:T(128)}) %tuple.71), condition=%wide.region_3.4_spmd, body=%wide.region_2.3_spmd.sunk | while | flops 540688 | bytes 2949538 | solution.py:541
  82.1 31.2 %collective-permute-start.6 = (f32[192,128]{1,0:T(8,128)S(1)}, f32[192,128]{1,0:T(8,128)S(1)}, u32[]{:S(2)}, u32[]{:S(2)}) collective-permute-start(f32[192,128]{1,0:T(8,128)S(1)} %select_bitcast_fusion.2), channel_id=1, source_target_pairs={{0,1},{1,0},{2,3},{3,2},{4,5},{5,4},{6,7},{7,6},{8,9},{9,8},{10,11... | collective-permute-start | bytes 294920 | tf_op jit(solution)/shard_map/while/body/ppermute | solution.py:444
  113.3 0.9 collective-permute-done.6
  114.4 3.2 %collective-permute-done.7 = bf16[192,128]{1,0:T(8,128)(2,1)S(1)} collective-permute-done((bf16[192,128]{1,0:T(8,128)(2,1)S(1)}, bf16[192,128]{1,0:T(8,128)(2,1)S(1)}, u32[]{:S(2)}, u32[]{:S(2)}) %collective-permute-start.7) | collective-permute-done | bytes 49184 | tf_op jit(solution)/shard_map/while/body/ppermute | solution.py:448
  117.6 3.1 %collective-permute-start.8 = (bf16[192,128]{1,0:T(8,128)(2,1)S(1)}, bf16[192,128]{1,0:T(8,128)(2,1)S(1)}, u32[]{:S(2)}, u32[]{:S(2)}) collective-permute-start(bf16[192,128]{1,0:T(8,128)(2,1)S(1)} %add_convert_fusion.6), channel_id=1, source_target_pairs={{0,4},{1,5},{2,6},{3,7},{4,0},{5,1},{6,2},{7,3},{8,12},{9,13},{10,... | collective-permute-start | bytes 147464 | tf_op jit(solution)/shard_map/while/body/ppermute | solution.py:448
  120.8 1.5 collective-permute-done.8
  122.3 0.8 collective-permute-start.9
  123.0 6.5 %collective-permute-done.9 = bf16[192,128]{1,0:T(8,128)(2,1)S(1)} collective-permute-done((bf16[192,128]{1,0:T(8,128)(2,1)S(1)}, bf16[192,128]{1,0:T(8,128)(2,1)S(1)}, u32[]{:S(2)}, u32[]{:S(2)}) %collective-permute-start.9) | collective-permute-done | bytes 49184 | tf_op jit(solution)/shard_map/while/body/ppermute | solution.py:452
  129.5 3.4 %collective-permute-start.10 = (bf16[192,128]{1,0:T(8,128)(2,1)S(1)}, bf16[192,128]{1,0:T(8,128)(2,1)S(1)}, u32[]{:S(2)}, u32[]{:S(2)}) collective-permute-start(bf16[192,128]{1,0:T(8,128)(2,1)S(1)} %add_convert_fusion.8), channel_id=1, source_target_pairs={{0,1},{1,0},{2,3},{3,2},{4,5},{5,4},{6,7},{7,6},{8,9},{9,8},{10,11... | collective-permute-start | bytes 147464 | tf_op jit(solution)/shard_map/while/body/ppermute | solution.py:444
  132.9 0.9 collective-permute-done.10
  133.9 0.7 copy.16
  135.6 3.0 %settle.1 = (bf16[128,2560]{1,0:T(8,128)(2,1)}, bf16[352,128]{1,0:T(8,128)(2,1)}, bf16[992,128]{1,0:T(8,128)(2,1)}, bf16[352,128]{1,0:T(8,128)(2,1)}, bf16[992,128]{1,0:T(8,128)(2,1)}) custom-call(s32[4]{0:T(128)} %copy-done.4, bf16[1280,128]{1,0:T(8,128)(2,1)} %copy-done, bf16[640,128]{1,0:T(8,128)(2,1)} %copy-done.2, bf16[1280,128]{1,0:T(8,128)(2,1)} %copy-done.5, ...), custom_call_target="tpu_custom_call" | custom-call | tf_op jit(solution)/shard_map/settle/pallas_call | solution.py:396
  139.1 2.2 %collective-permute-start.28 = (bf16[992,128]{1,0:T(8,128)(2,1)}, bf16[992,128]{1,0:T(8,128)(2,1)S(1)}, u32[]{:S(2)}, u32[]{:S(2)}) collective-permute-start(bf16[992,128]{1,0:T(8,128)(2,1)} %get-tuple-element.196), channel_id=1, source_target_pairs={{0,192},{16,208},{32,224},{48,240},{64,0},{80,16},{96,32},{112,48}... | collective-permute-start | bytes 761864 | tf_op jit(solution)/shard_map/ppermute | solution.py:431
  141.3 1.9 %collective-permute-start.27 = (bf16[352,128]{1,0:T(8,128)(2,1)}, bf16[352,128]{1,0:T(8,128)(2,1)S(1)}, u32[]{:S(2)}, u32[]{:S(2)}) collective-permute-start(bf16[352,128]{1,0:T(8,128)(2,1)} %get-tuple-element.195), channel_id=1, source_target_pairs={{0,128},{16,144},{32,160},{48,176},{64,192},{80,208},{96,224},{112... | collective-permute-start | bytes 270344 | tf_op jit(solution)/shard_map/ppermute | solution.py:431
  143.1 6.9 %collective-permute-done.27.p2 = bf16[352,128]{1,0:T(8,128)(2,1)S(1)} collective-permute-done((bf16[352,128]{1,0:T(8,128)(2,1)}, bf16[352,128]{1,0:T(8,128)(2,1)S(1)}, u32[]{:S(2)}, u32[]{:S(2)}) %collective-permute-start.27) | collective-permute-done | bytes 90144 | tf_op jit(solution)/shard_map/ppermute | solution.py:431
  150.8 2.6 %place.1 = (bf16[128,2560]{1,0:T(8,128)(2,1)}, f32[128,512]{1,0:T(8,128)}, f32[128,512]{1,0:T(8,128)}, f32[48,512]{1,0:T(8,128)}, f32[48,512]{1,0:T(8,128)}) custom-call(s32[4]{0:T(128)} %copy-done.4, bf16[1280,128]{1,0:T(8,128)(2,1)} %copy-done, bf16[1280,128]{1,0:T(8,128)(2,1)} %copy-done.5, bf16[352,128]{1,0:T(8,128)(2,1)} %get-tuple-element.193.p0, ...), custom_call_target="tpu_custom_call" | custom-call | tf_op jit(solution)/shard_map/place/pallas_call | solution.py:420
  (84 shorter events, 5.3 us)
Async XLA Ops:
  0.6 7.8 %copy-start.7 = (bf16[1,128,2560]{2,1,0:T(8,128)(2,1)S(1)}, bf16[1,128,2560]{2,1,0:T(8,128)(2,1)}, u32[]{:S(2)}) copy-start(bf16[1,128,2560]{2,1,0:T(8,128)(2,1)} %param.11) | copy-start | bytes 1966084
  0.7 7.8 %copy-start.8 = (bf16[1,128,2560]{2,1,0:T(8,128)(2,1)S(1)}, bf16[1,128,2560]{2,1,0:T(8,128)(2,1)}, u32[]{:S(2)}) copy-start(bf16[1,128,2560]{2,1,0:T(8,128)(2,1)} %param.16) | copy-start | bytes 1966084
  2.6 8.6 %collective-permute-start.11 = (bf16[2,176,128]{2,1,0:T(8,128)(2,1)}, bf16[2,176,128]{2,1,0:T(8,128)(2,1)}, u32[]{:S(2)}, u32[]{:S(2)}) collective-permute-start(bf16[2,176,128]{2,1,0:T(8,128)(2,1)} %get-tuple-element.233), channel_id=1, source_target_pairs={{0,64},{16,80},{32,96},{48,112},{64,128},{80,144},{96,160},{112,17... | collective-permute-start | bytes 270344 | tf_op jit(solution)/shard_map/ppermute | solution.py:431
  4.8 6.6 %collective-permute-start.12 = (bf16[2,176,128]{2,1,0:T(8,128)(2,1)}, bf16[2,176,128]{2,1,0:T(8,128)(2,1)}, u32[]{:S(2)}, u32[]{:S(2)}) collective-permute-start(bf16[2,176,128]{2,1,0:T(8,128)(2,1)} %get-tuple-element.234), channel_id=1, source_target_pairs={{0,128},{16,144},{32,160},{48,176},{64,192},{80,208},{96,224},{112... | collective-permute-start | bytes 270344 | tf_op jit(solution)/shard_map/ppermute | solution.py:431
  7.4 4.0 %collective-permute-start.13 = (bf16[2,176,128]{2,1,0:T(8,128)(2,1)}, bf16[2,176,128]{2,1,0:T(8,128)(2,1)}, u32[]{:S(2)}, u32[]{:S(2)}) collective-permute-start(bf16[2,176,128]{2,1,0:T(8,128)(2,1)} %get-tuple-element.235), channel_id=1, source_target_pairs={{0,192},{16,208},{32,224},{48,240},{64,0},{80,16},{96,32},{112,48}... | collective-permute-start | bytes 270344 | tf_op jit(solution)/shard_map/ppermute | solution.py:431
  8.5 0.7 copy-start.18
  10.4 1.0 copy-start.9
  11.2 60.4 %copy-start.4 = (s32[4]{0:T(128)}, s32[4]{0:T(128)S(1)}, u32[]{:S(2)}) copy-start(s32[4]{0:T(128)S(1)} %pad_add_fusion.info) | copy-start | bytes 52
  12.5 48.1 %collective-permute-start.14 = (bf16[4,2,128,128]{3,2,1,0:T(8,128)(2,1)S(1)}, bf16[4,2,128,128]{3,2,1,0:T(8,128)(2,1)S(1)}, u32[]{:S(2)}, u32[]{:S(2)}) collective-permute-start(bf16[4,2,128,128]{3,2,1,0:T(8,128)(2,1)S(1)} %pad_maximum_fusion.4.kv0), channel_id=1, source_target_pairs={{0,16},{16,32},{32,48},{48,0},{64,80},{80,96},{96,112},{112,64},{1... | collective-permute-start | bytes 786440 | tf_op jit(solution)/shard_map/ppermute | solution.py:436
  14.2 46.4 %collective-permute-start.15 = (bf16[4,2,128,128]{3,2,1,0:T(8,128)(2,1)S(1)}, bf16[4,2,128,128]{3,2,1,0:T(8,128)(2,1)S(1)}, u32[]{:S(2)}, u32[]{:S(2)}) collective-permute-start(bf16[4,2,128,128]{3,2,1,0:T(8,128)(2,1)S(1)} %pad_maximum_fusion.4.kv0), channel_id=1, source_target_pairs={{0,32},{16,48},{32,0},{48,16},{64,96},{80,112},{96,64},{112,80},{1... | collective-permute-start | bytes 786440 | tf_op jit(solution)/shard_map/ppermute | solution.py:436
  17.2 43.4 %collective-permute-start.16 = (bf16[4,2,128,128]{3,2,1,0:T(8,128)(2,1)S(1)}, bf16[4,2,128,128]{3,2,1,0:T(8,128)(2,1)S(1)}, u32[]{:S(2)}, u32[]{:S(2)}) collective-permute-start(bf16[4,2,128,128]{3,2,1,0:T(8,128)(2,1)S(1)} %pad_maximum_fusion.4.kv0), channel_id=1, source_target_pairs={{0,48},{16,0},{32,16},{48,32},{64,112},{80,64},{96,80},{112,96},{1... | collective-permute-start | bytes 786440 | tf_op jit(solution)/shard_map/ppermute | solution.py:436
  18.6 16.6 %collective-permute-start = (bf16[192,128]{1,0:T(8,128)(2,1)S(1)}, bf16[192,128]{1,0:T(8,128)(2,1)S(1)}, u32[]{:S(2)}, u32[]{:S(2)}) collective-permute-start(bf16[192,128]{1,0:T(8,128)(2,1)S(1)} %slice.38), channel_id=1, source_target_pairs={{0,16},{16,0},{32,48},{48,32},{64,80},{80,64},{96,112},{112,96},{1... | collective-permute-start | bytes 147464 | tf_op jit(solution)/shard_map/while/body/ppermute | solution.py:440
  35.2 9.5 %collective-permute-start.1 = (bf16[384,128]{1,0:T(8,128)(2,1)S(1)}, bf16[384,128]{1,0:T(8,128)(2,1)S(1)}, u32[]{:S(2)}, u32[]{:S(2)}) collective-permute-start(bf16[384,128]{1,0:T(8,128)(2,1)S(1)} %pad_maximum_fusion.11), channel_id=1, source_target_pairs={{0,32},{16,48},{32,0},{48,16},{64,96},{80,112},{96,64},{112,80},{1... | collective-permute-start | bytes 294920 | tf_op jit(solution)/shard_map/while/body/ppermute | solution.py:440
  35.3 10.0 %collective-permute-start.4 = (bf16[2,128,640]{2,1,0:T(8,128)(2,1)S(1)}, bf16[2,128,640]{2,1,0:T(8,128)(2,1)S(1)}, u32[]{:S(2)}, u32[]{:S(2)}) collective-permute-start(bf16[2,128,640]{2,1,0:T(8,128)(2,1)S(1)} %get-tuple-element.326), channel_id=1, source_target_pairs={{0,128},{16,144},{32,160},{48,176},{64,192},{80,208},{96,224},{112... | collective-permute-start | bytes 983048 | tf_op jit(solution)/shard_map/while/body/ppermute | solution.py:431
  44.8 3.0 %collective-permute-start.2 = (bf16[768,128]{1,0:T(8,128)(2,1)S(1)}, bf16[768,128]{1,0:T(8,128)(2,1)S(1)}, u32[]{:S(2)}, u32[]{:S(2)}) collective-permute-start(bf16[768,128]{1,0:T(8,128)(2,1)S(1)} %pad_maximum_fusion.12), channel_id=1, source_target_pairs={{0,1},{1,0},{2,3},{3,2},{4,5},{5,4},{6,7},{7,6},{8,9},{9,8},{10,11... | collective-permute-start | bytes 589832 | tf_op jit(solution)/shard_map/while/body/ppermute | solution.py:444
  45.4 7.6 %collective-permute-start.5 = (bf16[2,128,640]{2,1,0:T(8,128)(2,1)S(1)}, bf16[2,128,640]{2,1,0:T(8,128)(2,1)S(1)}, u32[]{:S(2)}, u32[]{:S(2)}) collective-permute-start(bf16[2,128,640]{2,1,0:T(8,128)(2,1)S(1)} %get-tuple-element.308), channel_id=1, source_target_pairs={{0,192},{16,208},{32,224},{48,240},{64,0},{80,16},{96,32},{112,48}... | collective-permute-start | bytes 983048 | tf_op jit(solution)/shard_map/while/body/ppermute | solution.py:431
  47.8 0.7 copy-start.6
  48.4 8.4 %collective-permute-start.3 = (bf16[2,128,640]{2,1,0:T(8,128)(2,1)S(1)}, bf16[2,128,640]{2,1,0:T(8,128)(2,1)S(1)}, u32[]{:S(2)}, u32[]{:S(2)}) collective-permute-start(bf16[2,128,640]{2,1,0:T(8,128)(2,1)S(1)} %get-tuple-element.306), channel_id=1, source_target_pairs={{0,64},{16,80},{32,96},{48,112},{64,128},{80,144},{96,160},{112,17... | collective-permute-start | bytes 983048 | tf_op jit(solution)/shard_map/while/body/ppermute | solution.py:431
  65.4 12.8 %collective-permute-start.20 = (bf16[640,128]{1,0:T(8,128)(2,1)S(1)}, bf16[640,128]{1,0:T(8,128)(2,1)S(1)}, u32[]{:S(2)}, u32[]{:S(2)}) collective-permute-start(bf16[640,128]{1,0:T(8,128)(2,1)S(1)} %get-tuple-element.173), channel_id=1, source_target_pairs={{0,64},{16,80},{32,96},{48,112},{64,128},{80,144},{96,160},{112,17... | collective-permute-start | bytes 491528 | tf_op jit(solution)/shard_map/ppermute | solution.py:431
  65.5 12.7 %collective-permute-start.21 = (bf16[640,128]{1,0:T(8,128)(2,1)S(1)}, bf16[640,128]{1,0:T(8,128)(2,1)S(1)}, u32[]{:S(2)}, u32[]{:S(2)}) collective-permute-start(bf16[640,128]{1,0:T(8,128)(2,1)S(1)} %get-tuple-element.174), channel_id=1, source_target_pairs={{0,192},{16,208},{32,224},{48,240},{64,0},{80,16},{96,32},{112,48}... | collective-permute-start | bytes 491528 | tf_op jit(solution)/shard_map/ppermute | solution.py:431
  68.1 10.0 %collective-permute-start.17 = (bf16[4,2,48,128]{3,2,1,0:T(8,128)(2,1)S(1)}, bf16[4,2,48,128]{3,2,1,0:T(8,128)(2,1)S(1)}, u32[]{:S(2)}, u32[]{:S(2)}) collective-permute-start(bf16[4,2,48,128]{3,2,1,0:T(8,128)(2,1)S(1)} %get-tuple-element.170), channel_id=1, source_target_pairs={{0,16},{16,32},{32,48},{48,0},{64,80},{80,96},{96,112},{112,64},{1... | collective-permute-start | bytes 294920 | tf_op jit(solution)/shard_map/ppermute | solution.py:436
  68.1 10.0 %collective-permute-start.18 = (bf16[4,2,48,128]{3,2,1,0:T(8,128)(2,1)S(1)}, bf16[4,2,48,128]{3,2,1,0:T(8,128)(2,1)S(1)}, u32[]{:S(2)}, u32[]{:S(2)}) collective-permute-start(bf16[4,2,48,128]{3,2,1,0:T(8,128)(2,1)S(1)} %get-tuple-element.171), channel_id=1, source_target_pairs={{0,32},{16,48},{32,0},{48,16},{64,96},{80,112},{96,64},{112,80},{1... | collective-permute-start | bytes 294920 | tf_op jit(solution)/shard_map/ppermute | solution.py:436
  69.2 8.9 %collective-permute-start.19 = (bf16[4,2,48,128]{3,2,1,0:T(8,128)(2,1)S(1)}, bf16[4,2,48,128]{3,2,1,0:T(8,128)(2,1)S(1)}, u32[]{:S(2)}, u32[]{:S(2)}) collective-permute-start(bf16[4,2,48,128]{3,2,1,0:T(8,128)(2,1)S(1)} %get-tuple-element.172), channel_id=1, source_target_pairs={{0,48},{16,0},{32,16},{48,32},{64,112},{80,64},{96,80},{112,96},{1... | collective-permute-start | bytes 294920 | tf_op jit(solution)/shard_map/ppermute | solution.py:436
  75.4 0.7 copy-start
  76.1 0.7 copy-start.1
  76.8 0.7 copy-start.2
  77.5 0.7 copy-start.3
  78.2 3.9 %copy-start.15 = (bf16[640,128]{1,0:T(8,128)(2,1)}, bf16[640,128]{1,0:T(8,128)(2,1)S(1)}, u32[]{:S(2)}) copy-start(bf16[640,128]{1,0:T(8,128)(2,1)S(1)} %collective-permute-done.20.a1) | copy-start | bytes 491524
  78.2 3.9 %copy-start.16 = (bf16[640,128]{1,0:T(8,128)(2,1)}, bf16[640,128]{1,0:T(8,128)(2,1)S(1)}, u32[]{:S(2)}) copy-start(bf16[640,128]{1,0:T(8,128)(2,1)S(1)} %collective-permute-done.21.a3) | copy-start | bytes 491524
  78.3 56.3 %collective-permute-start.22 = (bf16[1280,128]{1,0:T(8,128)(2,1)S(1)}, bf16[1280,128]{1,0:T(8,128)(2,1)S(1)}, u32[]{:S(2)}, u32[]{:S(2)}) collective-permute-start(bf16[1280,128]{1,0:T(8,128)(2,1)S(1)} %get-tuple-element.179), channel_id=1, source_target_pairs={{0,128},{16,144},{32,160},{48,176},{64,192},{80,208},{96,224},{112... | collective-permute-start | bytes 983048 | tf_op jit(solution)/shard_map/ppermute | solution.py:431
  78.4 56.2 %collective-permute-start.23 = (bf16[4,2,128,128]{3,2,1,0:T(8,128)(2,1)S(1)}, bf16[4,2,128,128]{3,2,1,0:T(8,128)(2,1)S(1)}, u32[]{:S(2)}, u32[]{:S(2)}) collective-permute-start(bf16[4,2,128,128]{3,2,1,0:T(8,128)(2,1)S(1)} %get-tuple-element.184), channel_id=1, source_target_pairs={{0,16},{16,32},{32,48},{48,0},{64,80},{80,96},{96,112},{112,64},{1... | collective-permute-start | bytes 786440 | tf_op jit(solution)/shard_map/ppermute | solution.py:436
  78.5 56.0 %collective-permute-start.24 = (bf16[4,2,128,128]{3,2,1,0:T(8,128)(2,1)S(1)}, bf16[4,2,128,128]{3,2,1,0:T(8,128)(2,1)S(1)}, u32[]{:S(2)}, u32[]{:S(2)}) collective-permute-start(bf16[4,2,128,128]{3,2,1,0:T(8,128)(2,1)S(1)} %get-tuple-element.185), channel_id=1, source_target_pairs={{0,32},{16,48},{32,0},{48,16},{64,96},{80,112},{96,64},{112,80},{1... | collective-permute-start | bytes 786440 | tf_op jit(solution)/shard_map/ppermute | solution.py:436
  79.8 54.8 %collective-permute-start.25 = (bf16[4,2,128,128]{3,2,1,0:T(8,128)(2,1)S(1)}, bf16[4,2,128,128]{3,2,1,0:T(8,128)(2,1)S(1)}, u32[]{:S(2)}, u32[]{:S(2)}) collective-permute-start(bf16[4,2,128,128]{3,2,1,0:T(8,128)(2,1)S(1)} %get-tuple-element.186), channel_id=1, source_target_pairs={{0,48},{16,0},{32,16},{48,32},{64,112},{80,64},{96,80},{112,96},{1... | collective-permute-start | bytes 786440 | tf_op jit(solution)/shard_map/ppermute | solution.py:436
  82.1 32.2 %collective-permute-start.6 = (f32[192,128]{1,0:T(8,128)S(1)}, f32[192,128]{1,0:T(8,128)S(1)}, u32[]{:S(2)}, u32[]{:S(2)}) collective-permute-start(f32[192,128]{1,0:T(8,128)S(1)} %select_bitcast_fusion.2), channel_id=1, source_target_pairs={{0,1},{1,0},{2,3},{3,2},{4,5},{5,4},{6,7},{7,6},{8,9},{9,8},{10,11... | collective-permute-start | bytes 294920 | tf_op jit(solution)/shard_map/while/body/ppermute | solution.py:444
  114.3 3.3 %collective-permute-start.7 = (bf16[192,128]{1,0:T(8,128)(2,1)S(1)}, bf16[192,128]{1,0:T(8,128)(2,1)S(1)}, u32[]{:S(2)}, u32[]{:S(2)}) collective-permute-start(bf16[192,128]{1,0:T(8,128)(2,1)S(1)} %fusion.14), channel_id=1, source_target_pairs={{0,2},{1,3},{2,0},{3,1},{4,6},{5,7},{6,4},{7,5},{8,10},{9,11},{10,... | collective-permute-start | bytes 147464 | tf_op jit(solution)/shard_map/while/body/ppermute | solution.py:448
  117.6 4.6 %collective-permute-start.8 = (bf16[192,128]{1,0:T(8,128)(2,1)S(1)}, bf16[192,128]{1,0:T(8,128)(2,1)S(1)}, u32[]{:S(2)}, u32[]{:S(2)}) collective-permute-start(bf16[192,128]{1,0:T(8,128)(2,1)S(1)} %add_convert_fusion.6), channel_id=1, source_target_pairs={{0,4},{1,5},{2,6},{3,7},{4,0},{5,1},{6,2},{7,3},{8,12},{9,13},{10,... | collective-permute-start | bytes 147464 | tf_op jit(solution)/shard_map/while/body/ppermute | solution.py:448
  122.3 7.2 %collective-permute-start.9 = (bf16[192,128]{1,0:T(8,128)(2,1)S(1)}, bf16[192,128]{1,0:T(8,128)(2,1)S(1)}, u32[]{:S(2)}, u32[]{:S(2)}) collective-permute-start(bf16[192,128]{1,0:T(8,128)(2,1)S(1)} %add_convert_fusion.7), channel_id=1, source_target_pairs={{0,8},{1,9},{2,10},{3,11},{4,12},{5,13},{6,14},{7,15},{8,0},{9,1},... | collective-permute-start | bytes 147464 | tf_op jit(solution)/shard_map/while/body/ppermute | solution.py:452
  129.5 4.3 %collective-permute-start.10 = (bf16[192,128]{1,0:T(8,128)(2,1)S(1)}, bf16[192,128]{1,0:T(8,128)(2,1)S(1)}, u32[]{:S(2)}, u32[]{:S(2)}) collective-permute-start(bf16[192,128]{1,0:T(8,128)(2,1)S(1)} %add_convert_fusion.8), channel_id=1, source_target_pairs={{0,1},{1,0},{2,3},{3,2},{4,5},{5,4},{6,7},{7,6},{8,9},{9,8},{10,11... | collective-permute-start | bytes 147464 | tf_op jit(solution)/shard_map/while/body/ppermute | solution.py:444
  134.6 0.7 copy-start.10
  134.6 0.8 copy-start.11
  134.6 0.8 copy-start.12
  134.6 1.0 copy-start.5
  138.6 11.4 %collective-permute-start.26 = (bf16[992,128]{1,0:T(8,128)(2,1)}, bf16[992,128]{1,0:T(8,128)(2,1)S(1)}, u32[]{:S(2)}, u32[]{:S(2)}) collective-permute-start(bf16[992,128]{1,0:T(8,128)(2,1)} %get-tuple-element.194), channel_id=1, source_target_pairs={{0,64},{16,80},{32,96},{48,112},{64,128},{80,144},{96,160},{112,17... | collective-permute-start | bytes 761864 | tf_op jit(solution)/shard_map/ppermute | solution.py:431
  139.1 10.9 %collective-permute-start.28 = (bf16[992,128]{1,0:T(8,128)(2,1)}, bf16[992,128]{1,0:T(8,128)(2,1)S(1)}, u32[]{:S(2)}, u32[]{:S(2)}) collective-permute-start(bf16[992,128]{1,0:T(8,128)(2,1)} %get-tuple-element.196), channel_id=1, source_target_pairs={{0,192},{16,208},{32,224},{48,240},{64,0},{80,16},{96,32},{112,48}... | collective-permute-start | bytes 761864 | tf_op jit(solution)/shard_map/ppermute | solution.py:431
  141.3 8.8 %collective-permute-start.27 = (bf16[352,128]{1,0:T(8,128)(2,1)}, bf16[352,128]{1,0:T(8,128)(2,1)S(1)}, u32[]{:S(2)}, u32[]{:S(2)}) collective-permute-start(bf16[352,128]{1,0:T(8,128)(2,1)} %get-tuple-element.195), channel_id=1, source_target_pairs={{0,128},{16,144},{32,160},{48,176},{64,192},{80,208},{96,224},{112... | collective-permute-start | bytes 270344 | tf_op jit(solution)/shard_map/ppermute | solution.py:431
  150.0 0.6 copy-start.17
  150.0 0.7 copy-start.13
  150.0 0.8 copy-start.14

commit v3 on v1

--- a/solution.py
+++ b/solution.py
@@ -91,20 +91,22 @@
         block = lax.rem(y - s + NY, NY)
         start = (block * NZ + z) * BLOCK
         valid = (lax.broadcasted_iota(jnp.int32, (BLOCK, HD), 0) + start) < length
+        qs[head_rows(block), :] = x[:GROUP, :]
         for j in range(HEADS):
             at = aligned((block * HEADS + j) * BLOCK, BLOCK)
-            cols = slice(j * HD, (j + 1) * HD)
-            qs[at, :] = x[0, :, cols]
-            gs[at, :] = jnp.where(valid, x[1, :, cols].astype(F32), 0.0).astype(BF16)
+            g = x[GROUP + j * BLOCK : GROUP + (j + 1) * BLOCK, :]
+            gs[at, :] = jnp.where(valid, g.astype(F32), 0.0).astype(BF16)
+        for slot in range(NZ):
+            at = aligned((slot * NY + block) * PROMPT_ROWS, PROMPT_ROWS)
+            first = 2 * GROUP + slot * 2 * PROMPT_ROWS
+            kp[at, :] = x[first : first + PROMPT_ROWS, :]
+            vp[at, :] = x[first + PROMPT_ROWS : first + 2 * PROMPT_ROWS, :]
     for s, kv in enumerate((kv0, kv1, kv2, kv3)):
         zp = lax.rem(z - s + NZ, NZ)
         for b in range(NY):
-            at = aligned((zp * NY + b) * PROMPT_ROWS, PROMPT_ROWS)
-            kp[at, :] = kv[b, 0, :PROMPT_ROWS, :]
-            vp[at, :] = kv[b, 1, :PROMPT_ROWS, :]
             at = aligned((b * NZ + zp) * BLOCK, BLOCK)
-            k = kv[b, 0, PROMPT_ROWS:, :]
-            v = kv[b, 1, PROMPT_ROWS:, :]
+            k = kv[b, 0]
+            v = kv[b, 1]
             ks[at, :] = k
             vs[at, :] = v
             kt[:, at] = k.T
@@ -176,11 +178,37 @@
     a1[...] = os[head_rows(y + 1), :]
     a3[...] = os[head_rows(y + 3), :]
     for s, r in enumerate((r0, r1, r2, r3)):
-        zp = lax.rem(z + s, NZ)
+        slot = -s % NZ
         for b in range(NY):
-            at = aligned((zp * NY + b) * PROMPT_ROWS, PROMPT_ROWS)
+            at = slice((slot * NY + b) * PROMPT_ROWS, (slot * NY + b + 1) * PROMPT_ROWS)
             r[b, 0] = (dk[at, :] * SCALE).astype(BF16)
             r[b, 1] = dv[at, :].astype(BF16)
+
+
+def pack_kernel(info, q, g, k0, k1, k2, k3, x0, x1, x2, x3):
+    y = info[0]
+    for s, x in enumerate((x0, x1, x2, x3)):
+        dest = lax.rem(y + s, NY)
+        for j in range(HEADS):
+            at = aligned((dest * HEADS + j) * HD, HD)
+            x[j * BLOCK : (j + 1) * BLOCK, :] = q[:, at]
+            x[GROUP + j * BLOCK : GROUP + (j + 1) * BLOCK, :] = g[:, at]
+        for slot, k in enumerate((k0, k1, k2, k3)):
+            first = 2 * GROUP + slot * 2 * PROMPT_ROWS
+            for i in range(2):
+                rows = slice(first + i * PROMPT_ROWS, first + (i + 1) * PROMPT_ROWS)
+                x[rows, :] = k[i, :, aligned(dest * HD, HD)]
+
+
+def pack(info, queries, grads, prompt):
+    out = shaped((2 * GROUP + 2 * NZ * PROMPT_ROWS, HD), BF16)
+    return pl.pallas_call(
+        pack_kernel,
+        out_shape=[out] * NY,
+        in_specs=[SMEM] + [VMEM] * 6,
+        out_specs=[VMEM] * NY,
+        name="pack",
+    )(info, queries, grads, *prompt)
 
 
 def forward(info, rows, keyvals):
@@ -390,6 +418,14 @@
     return jnp.stack([jnp.where(core == 0, half, other), jnp.where(core == 0, other, half)])
 
 
+def bring_rows(state):
+    x1, x2, x3 = state
+    x2 = y_shift(x2, 2)
+    x3 = y_shift(x3, 3)
+    x1, x3 = lax.optimization_barrier((x1, x3))
+    return y_shift(x1, 1), x2, x3
+
+
 def by_y(pieces):
     return [pieces[0]] + [y_shift(pieces[s], s) for s in range(1, NY)]
 
@@ -418,22 +454,17 @@
             for s in range(NY)
         ]
 
-    keyvals = jnp.stack(
-        [
-            jnp.concatenate([prompt_keys, response_keys[0]], axis=0),
-            jnp.concatenate([prompt_values, response_values[0]], axis=0),
-        ]
-    )
-    keyvals = by_y(split(keyvals, HD))
-    *keyvals, queries, grads = lax.optimization_barrier(
-        (*keyvals, response_queries[0], output_grad[0])
-    )
+    prompt = by_z([jnp.stack([prompt_keys, prompt_values])] * NZ)
+    keyvals = by_y(split(jnp.concatenate([response_keys, response_values]), HD))
     stacked = jnp.stack(keyvals)
     keyvals = jnp.stack([pick(stacked, (y - b) % NY, 0, keepdims=False) for b in range(NY)])
+    keyvals, *prompt = lax.optimization_barrier((keyvals, *prompt))
     keyvals = by_z([keyvals] * NZ)
-    rows = by_y(split(jnp.stack([queries, grads]), HEADS * HD))
-
-    results = forward(info, rows, keyvals)
+    x0, *rows = pack(info, response_queries[0], output_grad[0], prompt)
+    once = jnp.minimum(lengths[0], 1)
+    rows = lax.fori_loop(0, once, lambda i, state: bring_rows(state), tuple(rows))
+
+    results = forward(info, (x0, *rows), keyvals)
     prompt_terms = by_z(results[:4])
     att = [y_shift(results[4], 1), y_shift(results[5], 3)]
     d0, d1, d2, d3, *terms = backward(info, results[6:])
@@ -442,7 +473,6 @@
     )
     prompt = sum(t.astype(F32) for t in prompt_terms)
     prompt = prompt.transpose(1, 0, 2, 3).reshape(2, NY * PROMPT_ROWS, HD)
-    once = jnp.minimum(lengths[0], 1)
     terms = by_z(terms)
     d2 = y_shift(d2, 2)
     prompt = lax.fori_loop(0, once, lambda i, terms: over_responses(terms), prompt)

time: 138 us -> 153 us (1.11)
  starting transfers between devices: 57.9 us -> 64.2 us
  local copies, waits for them, and re-layouts: 5.83 us -> 9.31 us
  Pallas kernels: 32 us -> 35.3 us
    ppermute x2, starting transfers between devices: 20.1 us -> 3.41 us  [core_swap(): return lax.ppermute(a, 'resp', [(i, i ^ 1) for i in range(16)])]
    ppermute x1, starting transfers between devices: 5.56 us -> 18.1 us  [far_swap(): return lax.ppermute(a, 'resp', [(i, i ^ 8) for i in range(16)])]
    ppermute x2, starting transfers between devices: 2.09 us -> 9.27 us  [x_swap(): return lax.ppermute(a, 'resp', [(i, i ^ 2 * bit) for i in range(16)])]
    ppermute x9 -> x12, waiting for transfers between devices: 10.6 us -> 6.39 us  [z_shift(): return lax.ppermute(a, 'prefix', pairs)]
    ppermute x12, waiting for transfers between devices: 18.9 us -> 23 us  [y_shift(): return lax.ppermute(a, 'prefix', pairs)]
    ppermute x9 -> x12, starting transfers between devices: 13.3 us -> 17 us  [z_shift(): return lax.ppermute(a, 'prefix', pairs)]
    pallas_call x0 -> x1, Pallas kernels: none -> 2.67 us  [pack(): pl.pallas_call(pack_kernel, out_shape=[out] * NY, in_specs=[SMEM] + [VMEM...]
    while x0 -> x3, local copies, waits for them, and re-layouts: none -> 1.54 us
  transfers between devices with their start and end apart: 26 -> 29, of which waited for: 10 -> 11; matrix products, arithmetic and copies ran while one was open for 2% -> 3% of each run, Pallas kernels for 8% -> 9%
where the time goes in v3:
time: 153 us; the launch traced here: 152 us
  starting transfers between devices  64.2 us (42%)
  waiting for transfers between devices  39.4 us (26%)
  Pallas kernels  35.3 us (23%)
  local copies, waits for them, and re-layouts  9.31 us (6%)
  other arithmetic  2.32 us (2%)
  between operations  1.68 us (1%)
    ppermute x12, waiting for transfers between devices, y_shift(): return lax.ppermute(a, 'prefix', pairs)  23 us
    ppermute x1, starting transfers between devices, far_swap(): return lax.ppermute(a, 'resp', [(i, i ^ 8) for i in range(16)])  18.1 us
    ppermute x12, starting transfers between devices, z_shift(): return lax.ppermute(a, 'prefix', pairs)  17 us
    ppermute x12, starting transfers between devices, y_shift(): return lax.ppermute(a, 'prefix', pairs)  16.4 us
    pallas_call x1, Pallas kernels, forward(): pl.pallas_call(forward_kernel, out_shape=[shaped((NY, 2, PROMPT_ROWS, HD)...  15.7 us
    pallas_call x1, Pallas kernels, backward(): pl.pallas_call(backward_kernel, out_shape=[shaped((rows, HD), BF16) for r...  11.3 us
    ppermute x2, starting transfers between devices, x_swap(): return lax.ppermute(a, 'resp', [(i, i ^ 2 * bit) for i in range(16)])  9.27 us
    ppermute x2, waiting for transfers between devices, x_swap(): return lax.ppermute(a, 'resp', [(i, i ^ 2 * bit) for i in range(16)])  6.4 us
  transfers between devices with their start and end apart: 29, of which 11 were waited for; matrix products, arithmetic and copies ran while one was open for 3% of the time, Pallas kernels for 9%

profile of v3, /device:TPU:1, one launch (start us, length us, event | category | flops | bytes accessed | tf_op | source)
XLA Modules:
  0.0 152.5 jit_solution(9835424976951292548)
XLA Ops:
  0.7 0.9 constant_dynamic-update-slice_fusion.1
  1.7 0.9 constant_dynamic-update-slice_fusion
  2.7 3.8 %collective-permute-start.9 = (bf16[2,128,128]{2,1,0:T(8,128)(2,1)S(1)}, bf16[2,128,128]{2,1,0:T(8,128)(2,1)S(1)}, u32[]{:S(2)}, u32[]{:S(2)}) collective-permute-start(bf16[2,128,128]{2,1,0:T(8,128)(2,1)S(1)} %get-tuple-element.215), channel_id=1, source_target_pairs={{0,128},{16,144},{32,160},{48,176},{64,192},{80,208},{96,224},{112... | collective-permute-start | bytes 196616 | tf_op jit(solution)/shard_map/ppermute | solution.py:389
  6.5 0.8 collective-permute-start.10
  8.0 0.8 pad_maximum_fusion.3.k0
  8.8 1.7 %collective-permute-start.11 = (bf16[2,48,512]{2,1,0:T(8,128)(2,1)S(1)}, bf16[2,48,512]{2,1,0:T(8,128)(2,1)S(1)}, u32[]{:S(2)}, u32[]{:S(2)}) collective-permute-start(bf16[2,48,512]{2,1,0:T(8,128)(2,1)S(1)} %pad_maximum_fusion.3.k0), channel_id=1, source_target_pairs={{0,16},{16,32},{32,48},{48,0},{64,80},{80,96},{96,112},{112,64},{1... | collective-permute-start | bytes 294920 | tf_op jit(solution)/shard_map/ppermute | solution.py:394
  10.5 3.0 %collective-permute-start.12 = (bf16[2,48,512]{2,1,0:T(8,128)(2,1)S(1)}, bf16[2,48,512]{2,1,0:T(8,128)(2,1)S(1)}, u32[]{:S(2)}, u32[]{:S(2)}) collective-permute-start(bf16[2,48,512]{2,1,0:T(8,128)(2,1)S(1)} %pad_maximum_fusion.3.k0), channel_id=1, source_target_pairs={{0,32},{16,48},{32,0},{48,16},{64,96},{80,112},{96,64},{112,80},{1... | collective-permute-start | bytes 294920 | tf_op jit(solution)/shard_map/ppermute | solution.py:394
  13.5 0.7 collective-permute-start.13
  14.4 0.9 collective-permute-done.11.k1
  15.3 5.4 %collective-permute-done.12.k2 = bf16[2,48,512]{2,1,0:T(8,128)(2,1)S(1)} collective-permute-done((bf16[2,48,512]{2,1,0:T(8,128)(2,1)S(1)}, bf16[2,48,512]{2,1,0:T(8,128)(2,1)S(1)}, u32[]{:S(2)}, u32[]{:S(2)}) %collective-permute-start.12) | collective-permute-done | bytes 98336 | tf_op jit(solution)/shard_map/ppermute | solution.py:394
  20.8 2.4 %collective-permute-start.14 = (bf16[4,2,128,128]{3,2,1,0:T(8,128)(2,1)S(1)}, bf16[4,2,128,128]{3,2,1,0:T(8,128)(2,1)S(1)}, u32[]{:S(2)}, u32[]{:S(2)}) collective-permute-start(bf16[4,2,128,128]{3,2,1,0:T(8,128)(2,1)S(1)} %pad_maximum_fusion.2.kv0), channel_id=1, source_target_pairs={{0,16},{16,32},{32,48},{48,0},{64,80},{80,96},{96,112},{112,64},{1... | collective-permute-start | bytes 786440 | tf_op jit(solution)/shard_map/ppermute | solution.py:394
  23.2 2.1 %collective-permute-start.16 = (bf16[4,2,128,128]{3,2,1,0:T(8,128)(2,1)S(1)}, bf16[4,2,128,128]{3,2,1,0:T(8,128)(2,1)S(1)}, u32[]{:S(2)}, u32[]{:S(2)}) collective-permute-start(bf16[4,2,128,128]{3,2,1,0:T(8,128)(2,1)S(1)} %pad_maximum_fusion.2.kv0), channel_id=1, source_target_pairs={{0,48},{16,0},{32,16},{48,32},{64,112},{80,64},{96,80},{112,96},{1... | collective-permute-start | bytes 786440 | tf_op jit(solution)/shard_map/ppermute | solution.py:394
  26.5 1.3 pad_add_fusion.info
  27.8 2.7 %pack.1 = (bf16[1664,128]{1,0:T(8,128)(2,1)}, bf16[1664,128]{1,0:T(8,128)(2,1)S(1)}, bf16[1664,128]{1,0:T(8,128)(2,1)}, bf16[1664,128]{1,0:T(8,128)(2,1)}) custom-call(s32[3]{0:T(128)} %pad_add_fusion.info, bf16[128,2560]{1,0:T(8,128)(2,1)} %bitcast.42, bf16[128,2560]{1,0:T(8,128)(2,1)} %bitcast.43, bf16[2,48,512]{2,1,0:T(8,128)(2,1)} %copy-done.7, ...), custom_call_target="tpu_custom_call" | custom-call | tf_op jit(solution)/shard_map/pack/pallas_call | solution.py:205
  30.4 20.3 %while.26 = (s32[]{:T(128)}, bf16[1664,128]{1,0:T(8,128)(2,1)S(1)}, bf16[1664,128]{1,0:T(8,128)(2,1)}, bf16[1664,128]{1,0:T(8,128)(2,1)}, s32[]{:T(128)}, /*index=5*/s32[]{:T(128)}) while((s32[]{:T(128)}, bf16[1664,128]{1,0:T(8,128)(2,1)S(1)}, bf16[1664,128]{1,0:T(8,128)(2,1)}, bf16[1664,128]{1,0:T(8,128)(2,1)}, s32[]{:T(128)}, ...), condition=%wide.region_1.2_spmd, body=%wide.region_0.1_spmd.sunk | while | flops 2 | bytes 7667901 | solution.py:465
  30.4 2.1 %collective-permute-start = (bf16[1664,128]{1,0:T(8,128)(2,1)}, bf16[1664,128]{1,0:T(8,128)(2,1)S(1)}, u32[]{:S(2)}, u32[]{:S(2)}) collective-permute-start(bf16[1664,128]{1,0:T(8,128)(2,1)} %get-tuple-element.288), channel_id=1, source_target_pairs={{0,192},{16,208},{32,224},{48,240},{64,0},{80,16},{96,32},{112,48}... | collective-permute-start | bytes 1277960 | tf_op jit(solution)/shard_map/while/body/ppermute | solution.py:389
  32.7 8.5 %collective-permute-done = bf16[1664,128]{1,0:T(8,128)(2,1)S(1)} collective-permute-done((bf16[1664,128]{1,0:T(8,128)(2,1)}, bf16[1664,128]{1,0:T(8,128)(2,1)S(1)}, u32[]{:S(2)}, u32[]{:S(2)}) %collective-permute-start) | collective-permute-done | bytes 426016 | tf_op jit(solution)/shard_map/while/body/ppermute | solution.py:389
  41.4 0.8 copy.29
  42.1 2.1 %collective-permute-done.2 = bf16[1664,128]{1,0:T(8,128)(2,1)S(1)} collective-permute-done((bf16[1664,128]{1,0:T(8,128)(2,1)}, bf16[1664,128]{1,0:T(8,128)(2,1)S(1)}, u32[]{:S(2)}, u32[]{:S(2)}) %collective-permute-start.2) | collective-permute-done | bytes 426016 | tf_op jit(solution)/shard_map/while/body/ppermute | solution.py:389
  44.2 0.8 copy.28
  45.0 5.5 %collective-permute-done.1 = bf16[1664,128]{1,0:T(8,128)(2,1)S(1)} collective-permute-done((bf16[1664,128]{1,0:T(8,128)(2,1)S(1)}, bf16[1664,128]{1,0:T(8,128)(2,1)S(1)}, u32[]{:S(2)}, u32[]{:S(2)}) %collective-permute-start.1) | collective-permute-done | bytes 426016 | tf_op jit(solution)/shard_map/while/body/ppermute | solution.py:389
  50.8 15.7 %forward.1 = (bf16[4,2,48,128]{3,2,1,0:T(8,128)(2,1)S(1)}, bf16[4,2,48,128]{3,2,1,0:T(8,128)(2,1)S(1)}, bf16[4,2,48,128]{3,2,1,0:T(8,128)(2,1)S(1)}, bf16[4,2,48...) custom-call(s32[3]{0:T(128)S(1)} %copy-done.4, ...), custom_call_target="tpu_custom_call" | custom-call | flops 16000000000 | bytes 8388608 | tf_op jit(solution)/shard_map/forward/pallas_call | solution.py:215
  66.5 1.9 %collective-permute-start.20 = (bf16[640,128]{1,0:T(8,128)(2,1)S(1)}, bf16[640,128]{1,0:T(8,128)(2,1)S(1)}, u32[]{:S(2)}, u32[]{:S(2)}) collective-permute-start(bf16[640,128]{1,0:T(8,128)(2,1)S(1)} %get-tuple-element.162), channel_id=1, source_target_pairs={{0,64},{16,80},{32,96},{48,112},{64,128},{80,144},{96,160},{112,17... | collective-permute-start | bytes 491528 | tf_op jit(solution)/shard_map/ppermute | solution.py:389
  68.4 1.1 collective-permute-start.21
  69.5 1.5 collective-permute-start.18
  71.0 1.8 %collective-permute-start.19 = (bf16[4,2,48,128]{3,2,1,0:T(8,128)(2,1)S(1)}, bf16[4,2,48,128]{3,2,1,0:T(8,128)(2,1)S(1)}, u32[]{:S(2)}, u32[]{:S(2)}) collective-permute-start(bf16[4,2,48,128]{3,2,1,0:T(8,128)(2,1)S(1)} %get-tuple-element.161), channel_id=1, source_target_pairs={{0,48},{16,0},{32,16},{48,32},{64,112},{80,64},{96,80},{112,96},{1... | collective-permute-start | bytes 294920 | tf_op jit(solution)/shard_map/ppermute | solution.py:394
  72.8 11.3 %backward.1 = (bf16[1280,128]{1,0:T(8,128)(2,1)S(1)}, bf16[640,128]{1,0:T(8,128)(2,1)S(1)}, bf16[1280,128]{1,0:T(8,128)(2,1)S(1)}, bf16[640,128]{1,0:T(8,128)(2,...) custom-call(s32[3]{0:T(128)S(1)} %copy-done.4, ...), custom_call_target="tpu_custom_call" | custom-call | flops 16000000000 | bytes 8388608 | tf_op jit(solution)/shard_map/backward/pallas_call | solution.py:309
  84.1 0.7 copy-done
  84.8 0.7 copy-done.1
  87.0 1.2 collective-permute-start.22
  88.5 1.2 collective-permute-start.24
  89.6 2.4 %collective-permute-start.25 = (bf16[4,2,128,128]{3,2,1,0:T(8,128)(2,1)S(1)}, bf16[4,2,128,128]{3,2,1,0:T(8,128)(2,1)S(1)}, u32[]{:S(2)}, u32[]{:S(2)}) collective-permute-start(bf16[4,2,128,128]{3,2,1,0:T(8,128)(2,1)S(1)} %get-tuple-element.175), channel_id=1, source_target_pairs={{0,48},{16,0},{32,16},{48,32},{64,112},{80,64},{96,80},{112,96},{1... | collective-permute-start | bytes 786440 | tf_op jit(solution)/shard_map/ppermute | solution.py:394
  92.0 41.0 %while.27 = (s32[]{:T(128)}, f32[2,192,128]{2,1,0:T(8,128)S(1)}, s32[]{:T(128)}, s32[]{:T(128)}, u32[]{:T(128)}, /*index=5*/s32[]{:T(128)}, s32[]{:T(128)}) while((s32[]{:T(128)}, f32[2,192,128]{2,1,0:T(8,128)S(1)}, s32[]{:T(128)}, s32[]{:T(128)}, u32[]{:T(128)}, /*index=5*/s32[]{:T(128)}, s32[]{:T(128)}) %tuple.66), condition=%wide.region_3.4_spmd, body=%wide.region_2.3_spmd.sunk | while | flops 540688 | bytes 2949538 | solution.py:478
  92.1 1.3 collective-permute-done.3
  93.4 9.2 %collective-permute-start.4 = (bf16[192,128]{1,0:T(8,128)(2,1)S(1)}, bf16[192,128]{1,0:T(8,128)(2,1)S(1)}, u32[]{:S(2)}, u32[]{:S(2)}) collective-permute-start(bf16[192,128]{1,0:T(8,128)(2,1)S(1)} %fusion.6), channel_id=1, source_target_pairs={{0,2},{1,3},{2,0},{3,1},{4,6},{5,7},{6,4},{7,5},{8,10},{9,11},{10,... | collective-permute-start | bytes 147464 | tf_op jit(solution)/shard_map/while/body/ppermute | solution.py:402
  102.6 2.0 %collective-permute-done.4 = bf16[192,128]{1,0:T(8,128)(2,1)S(1)} collective-permute-done((bf16[192,128]{1,0:T(8,128)(2,1)S(1)}, bf16[192,128]{1,0:T(8,128)(2,1)S(1)}, u32[]{:S(2)}, u32[]{:S(2)}) %collective-permute-start.4) | collective-permute-done | bytes 49184 | tf_op jit(solution)/shard_map/while/body/ppermute | solution.py:402
  104.7 4.4 %collective-permute-done.5 = bf16[192,128]{1,0:T(8,128)(2,1)S(1)} collective-permute-done((bf16[192,128]{1,0:T(8,128)(2,1)S(1)}, bf16[192,128]{1,0:T(8,128)(2,1)S(1)}, u32[]{:S(2)}, u32[]{:S(2)}) %collective-permute-start.5) | collective-permute-done | bytes 49184 | tf_op jit(solution)/shard_map/while/body/ppermute | solution.py:402
  109.1 18.1 %collective-permute-start.6 = (bf16[192,128]{1,0:T(8,128)(2,1)S(1)}, bf16[192,128]{1,0:T(8,128)(2,1)S(1)}, u32[]{:S(2)}, u32[]{:S(2)}) collective-permute-start(bf16[192,128]{1,0:T(8,128)(2,1)S(1)} %add_convert_fusion.7), channel_id=1, source_target_pairs={{0,8},{1,9},{2,10},{3,11},{4,12},{5,13},{6,14},{7,15},{8,0},{9,1},... | collective-permute-start | bytes 147464 | tf_op jit(solution)/shard_map/while/body/ppermute | solution.py:406
  127.2 1.5 collective-permute-done.6
  128.7 3.3 %collective-permute-start.7 = (bf16[192,128]{1,0:T(8,128)(2,1)S(1)}, bf16[192,128]{1,0:T(8,128)(2,1)S(1)}, u32[]{:S(2)}, u32[]{:S(2)}) collective-permute-start(bf16[192,128]{1,0:T(8,128)(2,1)S(1)} %add_convert_fusion.8), channel_id=1, source_target_pairs={{0,1},{1,0},{2,3},{3,2},{4,5},{5,4},{6,7},{7,6},{8,9},{9,8},{10,11... | collective-permute-start | bytes 147464 | tf_op jit(solution)/shard_map/while/body/ppermute | solution.py:398
  132.1 0.9 collective-permute-done.7
  133.0 0.7 copy.16
  134.7 3.0 %settle.1 = (bf16[128,2560]{1,0:T(8,128)(2,1)}, bf16[352,128]{1,0:T(8,128)(2,1)}, bf16[992,128]{1,0:T(8,128)(2,1)}, bf16[352,128]{1,0:T(8,128)(2,1)}, bf16[992,128]{1,0:T(8,128)(2,1)}) custom-call(s32[3]{0:T(128)} %pad_add_fusion.info, bf16[1280,128]{1,0:T(8,128)(2,1)} %copy-done, bf16[640,128]{1,0:T(8,128)(2,1)} %copy-done.2, bf16[1280,128]{1,0:T(8,128)(2,1)} %copy-done.6, ...), custom_call_target="tpu_custom_call" | custom-call | tf_op jit(solution)/shard_map/settle/pallas_call | solution.py:354
  137.7 1.1 collective-permute-start.26
  138.8 1.5 %collective-permute-start.28 = (bf16[992,128]{1,0:T(8,128)(2,1)}, bf16[992,128]{1,0:T(8,128)(2,1)S(1)}, u32[]{:S(2)}, u32[]{:S(2)}) collective-permute-start(bf16[992,128]{1,0:T(8,128)(2,1)} %get-tuple-element.185), channel_id=1, source_target_pairs={{0,192},{16,208},{32,224},{48,240},{64,0},{80,16},{96,32},{112,48}... | collective-permute-start | bytes 761864 | tf_op jit(solution)/shard_map/ppermute | solution.py:389
  140.4 1.8 %collective-permute-start.27 = (bf16[352,128]{1,0:T(8,128)(2,1)}, bf16[352,128]{1,0:T(8,128)(2,1)S(1)}, u32[]{:S(2)}, u32[]{:S(2)}) collective-permute-start(bf16[352,128]{1,0:T(8,128)(2,1)} %get-tuple-element.184), channel_id=1, source_target_pairs={{0,128},{16,144},{32,160},{48,176},{64,192},{80,208},{96,224},{112... | collective-permute-start | bytes 270344 | tf_op jit(solution)/shard_map/ppermute | solution.py:389
  142.1 6.9 %collective-permute-done.27.p2 = bf16[352,128]{1,0:T(8,128)(2,1)S(1)} collective-permute-done((bf16[352,128]{1,0:T(8,128)(2,1)}, bf16[352,128]{1,0:T(8,128)(2,1)S(1)}, u32[]{:S(2)}, u32[]{:S(2)}) %collective-permute-start.27) | collective-permute-done | bytes 90144 | tf_op jit(solution)/shard_map/ppermute | solution.py:389
  149.9 2.6 %place.1 = (bf16[128,2560]{1,0:T(8,128)(2,1)}, f32[128,512]{1,0:T(8,128)}, f32[128,512]{1,0:T(8,128)}, f32[48,512]{1,0:T(8,128)}, f32[48,512]{1,0:T(8,128)}) custom-call(s32[3]{0:T(128)} %pad_add_fusion.info, bf16[1280,128]{1,0:T(8,128)(2,1)} %copy-done, bf16[1280,128]{1,0:T(8,128)(2,1)} %copy-done.6, bf16[352,128]{1,0:T(8,128)(2,1)} %get-tuple-element.182.p0, ...), custom_call_target="tpu_custom_call" | custom-call | tf_op jit(solution)/shard_map/place/pallas_call | solution.py:378
  (79 shorter events, 5.7 us)
Async XLA Ops:
  1.7 23.6 %copy-start.19 = (s32[16]{0:T(128)S(1)}, s32[16]{0:T(128)}, u32[]{:S(2)}) copy-start(s32[16]{0:T(128)} %param.17) | copy-start | bytes 196
  2.7 10.9 %collective-permute-start.9 = (bf16[2,128,128]{2,1,0:T(8,128)(2,1)S(1)}, bf16[2,128,128]{2,1,0:T(8,128)(2,1)S(1)}, u32[]{:S(2)}, u32[]{:S(2)}) collective-permute-start(bf16[2,128,128]{2,1,0:T(8,128)(2,1)S(1)} %get-tuple-element.215), channel_id=1, source_target_pairs={{0,128},{16,144},{32,160},{48,176},{64,192},{80,208},{96,224},{112... | collective-permute-start | bytes 196616 | tf_op jit(solution)/shard_map/ppermute | solution.py:389
  6.5 7.8 %collective-permute-start.10 = (bf16[2,128,128]{2,1,0:T(8,128)(2,1)S(1)}, bf16[2,128,128]{2,1,0:T(8,128)(2,1)S(1)}, u32[]{:S(2)}, u32[]{:S(2)}) collective-permute-start(bf16[2,128,128]{2,1,0:T(8,128)(2,1)S(1)} %get-tuple-element.214), channel_id=1, source_target_pairs={{0,192},{16,208},{32,224},{48,240},{64,0},{80,16},{96,32},{112,48}... | collective-permute-start | bytes 196616 | tf_op jit(solution)/shard_map/ppermute | solution.py:389
  7.3 7.0 %collective-permute-start.8 = (bf16[2,128,128]{2,1,0:T(8,128)(2,1)S(1)}, bf16[2,128,128]{2,1,0:T(8,128)(2,1)S(1)}, u32[]{:S(2)}, u32[]{:S(2)}) collective-permute-start(bf16[2,128,128]{2,1,0:T(8,128)(2,1)S(1)} %get-tuple-element.216), channel_id=1, source_target_pairs={{0,64},{16,80},{32,96},{48,112},{64,128},{80,144},{96,160},{112,17... | collective-permute-start | bytes 196616 | tf_op jit(solution)/shard_map/ppermute | solution.py:389
  8.8 19.0 %copy-start.7 = (bf16[2,48,512]{2,1,0:T(8,128)(2,1)}, bf16[2,48,512]{2,1,0:T(8,128)(2,1)S(1)}, u32[]{:S(2)}) copy-start(bf16[2,48,512]{2,1,0:T(8,128)(2,1)S(1)} %pad_maximum_fusion.3.k0) | copy-start | bytes 294916
  8.8 6.5 %collective-permute-start.11 = (bf16[2,48,512]{2,1,0:T(8,128)(2,1)S(1)}, bf16[2,48,512]{2,1,0:T(8,128)(2,1)S(1)}, u32[]{:S(2)}, u32[]{:S(2)}) collective-permute-start(bf16[2,48,512]{2,1,0:T(8,128)(2,1)S(1)} %pad_maximum_fusion.3.k0), channel_id=1, source_target_pairs={{0,16},{16,32},{32,48},{48,0},{64,80},{80,96},{96,112},{112,64},{1... | collective-permute-start | bytes 294920 | tf_op jit(solution)/shard_map/ppermute | solution.py:394
  10.5 10.2 %collective-permute-start.12 = (bf16[2,48,512]{2,1,0:T(8,128)(2,1)S(1)}, bf16[2,48,512]{2,1,0:T(8,128)(2,1)S(1)}, u32[]{:S(2)}, u32[]{:S(2)}) collective-permute-start(bf16[2,48,512]{2,1,0:T(8,128)(2,1)S(1)} %pad_maximum_fusion.3.k0), channel_id=1, source_target_pairs={{0,32},{16,48},{32,0},{48,16},{64,96},{80,112},{96,64},{112,80},{1... | collective-permute-start | bytes 294920 | tf_op jit(solution)/shard_map/ppermute | solution.py:394
  13.5 7.2 %collective-permute-start.13 = (bf16[2,48,512]{2,1,0:T(8,128)(2,1)S(1)}, bf16[2,48,512]{2,1,0:T(8,128)(2,1)S(1)}, u32[]{:S(2)}, u32[]{:S(2)}) collective-permute-start(bf16[2,48,512]{2,1,0:T(8,128)(2,1)S(1)} %pad_maximum_fusion.3.k0), channel_id=1, source_target_pairs={{0,48},{16,0},{32,16},{48,32},{64,112},{80,64},{96,80},{112,96},{1... | collective-permute-start | bytes 294920 | tf_op jit(solution)/shard_map/ppermute | solution.py:394
  15.3 12.4 %copy-start.15 = (bf16[2,48,512]{2,1,0:T(8,128)(2,1)}, bf16[2,48,512]{2,1,0:T(8,128)(2,1)S(1)}, u32[]{:S(2)}) copy-start(bf16[2,48,512]{2,1,0:T(8,128)(2,1)S(1)} %collective-permute-done.11.k1) | copy-start | bytes 294916
  20.8 7.0 %copy-start.16 = (bf16[2,48,512]{2,1,0:T(8,128)(2,1)}, bf16[2,48,512]{2,1,0:T(8,128)(2,1)S(1)}, u32[]{:S(2)}) copy-start(bf16[2,48,512]{2,1,0:T(8,128)(2,1)S(1)} %collective-permute-done.12.k2) | copy-start | bytes 294916
  20.8 7.0 %copy-start.17 = (bf16[2,48,512]{2,1,0:T(8,128)(2,1)}, bf16[2,48,512]{2,1,0:T(8,128)(2,1)S(1)}, u32[]{:S(2)}) copy-start(bf16[2,48,512]{2,1,0:T(8,128)(2,1)S(1)} %collective-permute-done.13.k3) | copy-start | bytes 294916
  20.8 30.0 %collective-permute-start.14 = (bf16[4,2,128,128]{3,2,1,0:T(8,128)(2,1)S(1)}, bf16[4,2,128,128]{3,2,1,0:T(8,128)(2,1)S(1)}, u32[]{:S(2)}, u32[]{:S(2)}) collective-permute-start(bf16[4,2,128,128]{3,2,1,0:T(8,128)(2,1)S(1)} %pad_maximum_fusion.2.kv0), channel_id=1, source_target_pairs={{0,16},{16,32},{32,48},{48,0},{64,80},{80,96},{96,112},{112,64},{1... | collective-permute-start | bytes 786440 | tf_op jit(solution)/shard_map/ppermute | solution.py:394
  23.2 27.5 %collective-permute-start.15 = (bf16[4,2,128,128]{3,2,1,0:T(8,128)(2,1)S(1)}, bf16[4,2,128,128]{3,2,1,0:T(8,128)(2,1)S(1)}, u32[]{:S(2)}, u32[]{:S(2)}) collective-permute-start(bf16[4,2,128,128]{3,2,1,0:T(8,128)(2,1)S(1)} %pad_maximum_fusion.2.kv0), channel_id=1, source_target_pairs={{0,32},{16,48},{32,0},{48,16},{64,96},{80,112},{96,64},{112,80},{1... | collective-permute-start | bytes 786440 | tf_op jit(solution)/shard_map/ppermute | solution.py:394
  23.2 27.6 %collective-permute-start.16 = (bf16[4,2,128,128]{3,2,1,0:T(8,128)(2,1)S(1)}, bf16[4,2,128,128]{3,2,1,0:T(8,128)(2,1)S(1)}, u32[]{:S(2)}, u32[]{:S(2)}) collective-permute-start(bf16[4,2,128,128]{3,2,1,0:T(8,128)(2,1)S(1)} %pad_maximum_fusion.2.kv0), channel_id=1, source_target_pairs={{0,48},{16,0},{32,16},{48,32},{64,112},{80,64},{96,80},{112,96},{1... | collective-permute-start | bytes 786440 | tf_op jit(solution)/shard_map/ppermute | solution.py:394
  30.4 20.3 %copy-start.4 = (s32[3]{0:T(128)S(1)}, s32[3]{0:T(128)}, u32[]{:S(2)}) copy-start(s32[3]{0:T(128)} %pad_add_fusion.info) | copy-start | bytes 40
  30.4 20.3 %copy-start.5 = (bf16[1664,128]{1,0:T(8,128)(2,1)S(1)}, bf16[1664,128]{1,0:T(8,128)(2,1)}, u32[]{:S(2)}) copy-start(bf16[1664,128]{1,0:T(8,128)(2,1)} %get-tuple-element.139.x0) | copy-start | bytes 1277956
  30.4 10.7 %collective-permute-start = (bf16[1664,128]{1,0:T(8,128)(2,1)}, bf16[1664,128]{1,0:T(8,128)(2,1)S(1)}, u32[]{:S(2)}, u32[]{:S(2)}) collective-permute-start(bf16[1664,128]{1,0:T(8,128)(2,1)} %get-tuple-element.288), channel_id=1, source_target_pairs={{0,192},{16,208},{32,224},{48,240},{64,0},{80,16},{96,32},{112,48}... | collective-permute-start | bytes 1277960 | tf_op jit(solution)/shard_map/while/body/ppermute | solution.py:389
  32.5 11.7 %collective-permute-start.2 = (bf16[1664,128]{1,0:T(8,128)(2,1)}, bf16[1664,128]{1,0:T(8,128)(2,1)S(1)}, u32[]{:S(2)}, u32[]{:S(2)}) collective-permute-start(bf16[1664,128]{1,0:T(8,128)(2,1)} %get-tuple-element.287), channel_id=1, source_target_pairs={{0,128},{16,144},{32,160},{48,176},{64,192},{80,208},{96,224},{112... | collective-permute-start | bytes 1277960 | tf_op jit(solution)/shard_map/while/body/ppermute | solution.py:389
  41.2 9.3 %collective-permute-start.1 = (bf16[1664,128]{1,0:T(8,128)(2,1)S(1)}, bf16[1664,128]{1,0:T(8,128)(2,1)S(1)}, u32[]{:S(2)}, u32[]{:S(2)}) collective-permute-start(bf16[1664,128]{1,0:T(8,128)(2,1)S(1)} %get-tuple-element.272), channel_id=1, source_target_pairs={{0,64},{16,80},{32,96},{48,112},{64,128},{80,144},{96,160},{112,17... | collective-permute-start | bytes 1277960 | tf_op jit(solution)/shard_map/while/body/ppermute | solution.py:389
  66.5 20.4 %collective-permute-start.20 = (bf16[640,128]{1,0:T(8,128)(2,1)S(1)}, bf16[640,128]{1,0:T(8,128)(2,1)S(1)}, u32[]{:S(2)}, u32[]{:S(2)}) collective-permute-start(bf16[640,128]{1,0:T(8,128)(2,1)S(1)} %get-tuple-element.162), channel_id=1, source_target_pairs={{0,64},{16,80},{32,96},{48,112},{64,128},{80,144},{96,160},{112,17... | collective-permute-start | bytes 491528 | tf_op jit(solution)/shard_map/ppermute | solution.py:389
  68.4 18.5 %collective-permute-start.21 = (bf16[640,128]{1,0:T(8,128)(2,1)S(1)}, bf16[640,128]{1,0:T(8,128)(2,1)S(1)}, u32[]{:S(2)}, u32[]{:S(2)}) collective-permute-start(bf16[640,128]{1,0:T(8,128)(2,1)S(1)} %get-tuple-element.163), channel_id=1, source_target_pairs={{0,192},{16,208},{32,224},{48,240},{64,0},{80,16},{96,32},{112,48}... | collective-permute-start | bytes 491528 | tf_op jit(solution)/shard_map/ppermute | solution.py:389
  69.5 17.4 %collective-permute-start.17 = (bf16[4,2,48,128]{3,2,1,0:T(8,128)(2,1)S(1)}, bf16[4,2,48,128]{3,2,1,0:T(8,128)(2,1)S(1)}, u32[]{:S(2)}, u32[]{:S(2)}) collective-permute-start(bf16[4,2,48,128]{3,2,1,0:T(8,128)(2,1)S(1)} %get-tuple-element.159), channel_id=1, source_target_pairs={{0,16},{16,32},{32,48},{48,0},{64,80},{80,96},{96,112},{112,64},{1... | collective-permute-start | bytes 294920 | tf_op jit(solution)/shard_map/ppermute | solution.py:394
  69.5 17.4 %collective-permute-start.18 = (bf16[4,2,48,128]{3,2,1,0:T(8,128)(2,1)S(1)}, bf16[4,2,48,128]{3,2,1,0:T(8,128)(2,1)S(1)}, u32[]{:S(2)}, u32[]{:S(2)}) collective-permute-start(bf16[4,2,48,128]{3,2,1,0:T(8,128)(2,1)S(1)} %get-tuple-element.160), channel_id=1, source_target_pairs={{0,32},{16,48},{32,0},{48,16},{64,96},{80,112},{96,64},{112,80},{1... | collective-permute-start | bytes 294920 | tf_op jit(solution)/shard_map/ppermute | solution.py:394
  71.0 15.9 %collective-permute-start.19 = (bf16[4,2,48,128]{3,2,1,0:T(8,128)(2,1)S(1)}, bf16[4,2,48,128]{3,2,1,0:T(8,128)(2,1)S(1)}, u32[]{:S(2)}, u32[]{:S(2)}) collective-permute-start(bf16[4,2,48,128]{3,2,1,0:T(8,128)(2,1)S(1)} %get-tuple-element.161), channel_id=1, source_target_pairs={{0,48},{16,0},{32,16},{48,32},{64,112},{80,64},{96,80},{112,96},{1... | collective-permute-start | bytes 294920 | tf_op jit(solution)/shard_map/ppermute | solution.py:394
  84.1 0.7 copy-start
  84.8 0.7 copy-start.1
  85.5 0.7 copy-start.2
  86.2 0.7 copy-start.3
  86.9 5.1 %copy-start.13 = (bf16[640,128]{1,0:T(8,128)(2,1)}, bf16[640,128]{1,0:T(8,128)(2,1)S(1)}, u32[]{:S(2)}) copy-start(bf16[640,128]{1,0:T(8,128)(2,1)S(1)} %collective-permute-done.20.a1) | copy-start | bytes 491524
  86.9 5.1 %copy-start.14 = (bf16[640,128]{1,0:T(8,128)(2,1)}, bf16[640,128]{1,0:T(8,128)(2,1)S(1)}, u32[]{:S(2)}) copy-start(bf16[640,128]{1,0:T(8,128)(2,1)S(1)} %collective-permute-done.21.a3) | copy-start | bytes 491524
  87.0 46.7 %collective-permute-start.22 = (bf16[1280,128]{1,0:T(8,128)(2,1)S(1)}, bf16[1280,128]{1,0:T(8,128)(2,1)S(1)}, u32[]{:S(2)}, u32[]{:S(2)}) collective-permute-start(bf16[1280,128]{1,0:T(8,128)(2,1)S(1)} %get-tuple-element.168), channel_id=1, source_target_pairs={{0,128},{16,144},{32,160},{48,176},{64,192},{80,208},{96,224},{112... | collective-permute-start | bytes 983048 | tf_op jit(solution)/shard_map/ppermute | solution.py:389
  88.2 45.5 %collective-permute-start.23 = (bf16[4,2,128,128]{3,2,1,0:T(8,128)(2,1)S(1)}, bf16[4,2,128,128]{3,2,1,0:T(8,128)(2,1)S(1)}, u32[]{:S(2)}, u32[]{:S(2)}) collective-permute-start(bf16[4,2,128,128]{3,2,1,0:T(8,128)(2,1)S(1)} %get-tuple-element.173), channel_id=1, source_target_pairs={{0,16},{16,32},{32,48},{48,0},{64,80},{80,96},{96,112},{112,64},{1... | collective-permute-start | bytes 786440 | tf_op jit(solution)/shard_map/ppermute | solution.py:394
  88.5 45.2 %collective-permute-start.24 = (bf16[4,2,128,128]{3,2,1,0:T(8,128)(2,1)S(1)}, bf16[4,2,128,128]{3,2,1,0:T(8,128)(2,1)S(1)}, u32[]{:S(2)}, u32[]{:S(2)}) collective-permute-start(bf16[4,2,128,128]{3,2,1,0:T(8,128)(2,1)S(1)} %get-tuple-element.174), channel_id=1, source_target_pairs={{0,32},{16,48},{32,0},{48,16},{64,96},{80,112},{96,64},{112,80},{1... | collective-permute-start | bytes 786440 | tf_op jit(solution)/shard_map/ppermute | solution.py:394
  89.6 44.1 %collective-permute-start.25 = (bf16[4,2,128,128]{3,2,1,0:T(8,128)(2,1)S(1)}, bf16[4,2,128,128]{3,2,1,0:T(8,128)(2,1)S(1)}, u32[]{:S(2)}, u32[]{:S(2)}) collective-permute-start(bf16[4,2,128,128]{3,2,1,0:T(8,128)(2,1)S(1)} %get-tuple-element.175), channel_id=1, source_target_pairs={{0,48},{16,0},{32,16},{48,32},{64,112},{80,64},{96,80},{112,96},{1... | collective-permute-start | bytes 786440 | tf_op jit(solution)/shard_map/ppermute | solution.py:394
  92.0 1.4 collective-permute-start.3
  93.4 11.1 %collective-permute-start.4 = (bf16[192,128]{1,0:T(8,128)(2,1)S(1)}, bf16[192,128]{1,0:T(8,128)(2,1)S(1)}, u32[]{:S(2)}, u32[]{:S(2)}) collective-permute-start(bf16[192,128]{1,0:T(8,128)(2,1)S(1)} %fusion.6), channel_id=1, source_target_pairs={{0,2},{1,3},{2,0},{3,1},{4,6},{5,7},{6,4},{7,5},{8,10},{9,11},{10,... | collective-permute-start | bytes 147464 | tf_op jit(solution)/shard_map/while/body/ppermute | solution.py:402
  104.6 4.5 %collective-permute-start.5 = (bf16[192,128]{1,0:T(8,128)(2,1)S(1)}, bf16[192,128]{1,0:T(8,128)(2,1)S(1)}, u32[]{:S(2)}, u32[]{:S(2)}) collective-permute-start(bf16[192,128]{1,0:T(8,128)(2,1)S(1)} %add_convert_fusion.6), channel_id=1, source_target_pairs={{0,4},{1,5},{2,6},{3,7},{4,0},{5,1},{6,2},{7,3},{8,12},{9,13},{10,... | collective-permute-start | bytes 147464 | tf_op jit(solution)/shard_map/while/body/ppermute | solution.py:402
  109.1 19.6 %collective-permute-start.6 = (bf16[192,128]{1,0:T(8,128)(2,1)S(1)}, bf16[192,128]{1,0:T(8,128)(2,1)S(1)}, u32[]{:S(2)}, u32[]{:S(2)}) collective-permute-start(bf16[192,128]{1,0:T(8,128)(2,1)S(1)} %add_convert_fusion.7), channel_id=1, source_target_pairs={{0,8},{1,9},{2,10},{3,11},{4,12},{5,13},{6,14},{7,15},{8,0},{9,1},... | collective-permute-start | bytes 147464 | tf_op jit(solution)/shard_map/while/body/ppermute | solution.py:406
  128.7 4.2 %collective-permute-start.7 = (bf16[192,128]{1,0:T(8,128)(2,1)S(1)}, bf16[192,128]{1,0:T(8,128)(2,1)S(1)}, u32[]{:S(2)}, u32[]{:S(2)}) collective-permute-start(bf16[192,128]{1,0:T(8,128)(2,1)S(1)} %add_convert_fusion.8), channel_id=1, source_target_pairs={{0,1},{1,0},{2,3},{3,2},{4,5},{5,4},{6,7},{7,6},{8,9},{9,8},{10,11... | collective-permute-start | bytes 147464 | tf_op jit(solution)/shard_map/while/body/ppermute | solution.py:398
  133.7 0.7 copy-start.8
  133.7 0.8 copy-start.9
  133.7 0.8 copy-start.10
  133.7 1.0 copy-start.6
  137.7 11.4 %collective-permute-start.26 = (bf16[992,128]{1,0:T(8,128)(2,1)}, bf16[992,128]{1,0:T(8,128)(2,1)S(1)}, u32[]{:S(2)}, u32[]{:S(2)}) collective-permute-start(bf16[992,128]{1,0:T(8,128)(2,1)} %get-tuple-element.183), channel_id=1, source_target_pairs={{0,64},{16,80},{32,96},{48,112},{64,128},{80,144},{96,160},{112,17... | collective-permute-start | bytes 761864 | tf_op jit(solution)/shard_map/ppermute | solution.py:389
  138.8 10.2 %collective-permute-start.28 = (bf16[992,128]{1,0:T(8,128)(2,1)}, bf16[992,128]{1,0:T(8,128)(2,1)S(1)}, u32[]{:S(2)}, u32[]{:S(2)}) collective-permute-start(bf16[992,128]{1,0:T(8,128)(2,1)} %get-tuple-element.185), channel_id=1, source_target_pairs={{0,192},{16,208},{32,224},{48,240},{64,0},{80,16},{96,32},{112,48}... | collective-permute-start | bytes 761864 | tf_op jit(solution)/shard_map/ppermute | solution.py:389
  140.4 8.7 %collective-permute-start.27 = (bf16[352,128]{1,0:T(8,128)(2,1)}, bf16[352,128]{1,0:T(8,128)(2,1)S(1)}, u32[]{:S(2)}, u32[]{:S(2)}) collective-permute-start(bf16[352,128]{1,0:T(8,128)(2,1)} %get-tuple-element.184), channel_id=1, source_target_pairs={{0,128},{16,144},{32,160},{48,176},{64,192},{80,208},{96,224},{112... | collective-permute-start | bytes 270344 | tf_op jit(solution)/shard_map/ppermute | solution.py:389
  149.0 0.7 copy-start.11
  149.1 0.8 copy-start.12
  (1 other events, 0.6 us)
